TPU v7x, 32 devices: a whole 2x2x4 slice. The times are simulated.
32 devices in a mesh: head: 4 (over y, x), blk: 8 (over z, core).
Axes of the slice: x: 2, y: 2, z: 4, core: 2. Of those that a mesh axis runs over, the one named last changes fastest.
Arguments:
- hidden_in: bfloat16 [4096, 2, 2048], P(('blk', 'head')), may hold values from -6 to 6
- attn_gain: float32 [2048], replicated, may hold values from 0.5 to 1.5
- w_query: bfloat16 [2048, 2048], P('blk', 'head'), may hold values from -0.125 to 0.125
- w_key: bfloat16 [2048, 2048], P('blk', 'head'), may hold values from -0.125 to 0.125
- w_value: bfloat16 [2048, 2048], P('blk', 'head'), may hold values from -0.125 to 0.125
- query_gain: float32 [2048], replicated, may hold values from 0.5 to 1.5
- key_gain: float32 [2048], replicated, may hold values from 0.5 to 1.5
- w_out: bfloat16 [2048, 2048], P('head', 'blk'), may hold values from -2 to 2
- ffn_gain: float32 [2048], replicated, may hold values from 0.5 to 1.5
- w_gate: bfloat16 [32, 2048, 512], P(('blk', 'head')), may hold values from -0.125 to 0.125
- w_up: bfloat16 [32, 2048, 512], P(('blk', 'head')), may hold values from -0.125 to 0.125
- w_down: bfloat16 [32, 512, 2048], P(('blk', 'head')), may hold values from -0.75 to 0.75
- routes: int32 [4096, 2, 8], P(('blk', 'head')), may hold values from 0 to 15, all different within a row; in each aligned block of 256 rows (0 to 255, 256 to 511, ..., all dimensions but the last counted through in order) at most 160 rows name the same one
- gate_weights: float32 [4096, 2, 8], P(('blk', 'head')), may hold values from 0.05 to 0.25
- block_starts: int32 [2, 16], replicated, may hold values from 0 to 15, as said below
- cotangent: bfloat16 [4096, 2, 2048], P(('blk', 'head')), may hold values from -6 to 6
Outputs:
- layer_out: bfloat16 [4096, 2, 2048], P(('blk', 'head'))
- grad_in: bfloat16 [4096, 2, 2048], P(('blk', 'head'))
- grad_attn_gain: float32 [2048], replicated
- grad_query: float32 [2048, 2048], P('blk', 'head')
- grad_key: float32 [2048, 2048], P('blk', 'head')
- grad_value: float32 [2048, 2048], P('blk', 'head')
- grad_query_gain: float32 [2048], replicated
- grad_key_gain: float32 [2048], replicated
- grad_out: float32 [2048, 2048], P('head', 'blk')
- grad_ffn_gain: float32 [2048], replicated
- grad_gate: float32 [32, 2048, 512], P(('blk', 'head'))
- grad_up: float32 [32, 2048, 512], P(('blk', 'head'))
- grad_down: float32 [32, 512, 2048], P(('blk', 'head'))
- stream_stats: float32 [3], replicated
Inputs may be any that keep to these rules, and one draw needn't show every extreme that they name: `routes`: among the rows of one device (position-major, then sequence), no expert is named more than 160 times, a bound that some block reaches. block_starts[s, 0] = 0 and block_starts[s, k] is k or block_starts[s, k - 1]. In every draw, in some sequence the document of block 0 reaches block 14 or further, and in some sequence the last block starts its own document.
All inputs are finite; a program needn't handle non-finite values.
Results may differ from a plain program's by a relative error of at most 0.023.
Values may be sent and summed in bfloat16 or wider, within the bound.
A program may use at most 384 MiB of HBM per device.

v0:
```python
import math

import jax
import jax.numpy as jnp
from jax import lax
from jax.sharding import PartitionSpec as P

HEAD_DIM = 128
BLOCK = 256


EPSILON = 1e-06


def rounded(values):
    return lax.optimization_barrier(values.astype(jnp.bfloat16)).astype(jnp.float32)


def inverse_rms(values):
    return lax.rsqrt(jnp.mean(values * values, axis=-1, keepdims=True) + EPSILON)


def local(
    hidden_in,
    attn_gain,
    w_query,
    w_key,
    w_value,
    query_gain,
    key_gain,
    w_out,
    ffn_gain,
    w_gate,
    w_up,
    w_down,
    routes,
    gate_weights,
    block_starts,
    cotangent,
):
    head_count = lax.axis_size("head")
    blk_count = lax.axis_size("blk")
    head_index = lax.axis_index("head")
    blk_index = lax.axis_index("blk")
    piece, seqs, width = hidden_in.shape
    span = piece * head_count
    per_device = span // BLOCK
    total_blocks = block_starts.shape[1]
    columns = w_query.shape[1]
    heads_here = columns // HEAD_DIM
    top_count = routes.shape[2]
    experts = blk_count * head_count // 2
    tok_rows = piece * seqs
    capacity = max(2, 5 * tok_rows * top_count // (4 * experts))
    scale = 1.0 / math.sqrt(HEAD_DIM)

    def move_rows(buffer):
        return lax.all_to_all(buffer, ("blk", "head"), split_axis=0, concat_axis=0, tiled=True)

    hidden_f = hidden_in.astype(jnp.float32)
    inv_one = inverse_rms(hidden_f)
    normed = (hidden_f * inv_one * attn_gain).astype(jnp.bfloat16)
    group = lax.all_gather(normed, "head", axis=0, tiled=True)
    query_cols, key_cols, value_cols, out_rows = (
        lax.all_gather(w_query, "blk", axis=0, tiled=True),
        lax.all_gather(w_key, "blk", axis=0, tiled=True),
        lax.all_gather(w_value, "blk", axis=0, tiled=True),
        lax.all_gather(w_out, "blk", axis=1, tiled=True),
    )
    query_raw = jnp.einsum("tsd,dc->tsc", group, query_cols, preferred_element_type=jnp.float32)
    key_raw = jnp.einsum("tsd,dc->tsc", group, key_cols, preferred_element_type=jnp.float32)
    value_raw = jnp.einsum("tsd,dc->tsc", group, value_cols, preferred_element_type=jnp.float32)
    square_sums = lax.psum(
        (jnp.sum(query_raw * query_raw, -1), jnp.sum(key_raw * key_raw, -1)), "head"
    )
    inv_query = lax.rsqrt(square_sums[0][..., None] / width + EPSILON)
    inv_key = lax.rsqrt(square_sums[1][..., None] / width + EPSILON)
    gain_query = lax.dynamic_slice_in_dim(query_gain, head_index * columns, columns)
    gain_key = lax.dynamic_slice_in_dim(key_gain, head_index * columns, columns)
    query_n = (query_raw * inv_query * gain_query).astype(jnp.bfloat16)
    key_n = (key_raw * inv_key * gain_key).astype(jnp.bfloat16)
    value_n = value_raw.astype(jnp.bfloat16)
    all_keys, all_values = (
        lax.all_gather(key_n, "blk", axis=0, tiled=True),
        lax.all_gather(value_n, "blk", axis=0, tiled=True),
    )
    query_heads = query_n.reshape(span, seqs, heads_here, HEAD_DIM)
    key_blocks = all_keys.reshape(blk_count, span, seqs, heads_here, HEAD_DIM)
    value_blocks = all_values.reshape(blk_count, span, seqs, heads_here, HEAD_DIM)
    block_ids = jnp.arange(blk_count, dtype=jnp.int32)
    local_block = jnp.arange(span, dtype=jnp.int32) // BLOCK
    query_block = blk_index * per_device + local_block

    def first_of(blocks_now):
        picker = (jnp.arange(total_blocks, dtype=jnp.int32)[None, :] == blocks_now[:, None]).astype(
            jnp.int32
        )
        return jnp.sum(block_starts[:, None, :] * picker[None, :, :], -1)

    def allowed_pair(q_blocks, k_blocks):
        firsts = first_of(q_blocks)
        allowed = (k_blocks[None, None, :] >= firsts[:, :, None]) & (
            k_blocks[None, None, :] <= q_blocks[None, :, None]
        )
        return allowed[:, None]

    def visible(key_index):
        return allowed_pair(query_block, key_index * per_device + local_block)

    def pair_scores(query_blk, key_blk):
        return (
            jnp.einsum("tshe,kshe->shtk", query_blk, key_blk, preferred_element_type=jnp.float32)
            * scale
        )

    def max_sum(carry, item):
        key_blk, key_index = item
        running_max, running_sum = carry
        allowed = visible(key_index)
        scores = jnp.where(allowed, pair_scores(query_heads, key_blk), -1e30)
        new_max = jnp.maximum(running_max, jnp.max(scores, -1))
        weights = jnp.where(allowed, jnp.exp(scores - new_max[..., None]), 0.0)
        running_sum = running_sum * jnp.exp(running_max - new_max) + jnp.sum(weights, -1)
        return ((new_max, running_sum), None)

    start_max = jnp.full((seqs, heads_here, span), -1e30, jnp.float32)
    start_sum = jnp.zeros((seqs, heads_here, span), jnp.float32)
    (final_max, final_sum), _ = lax.scan(max_sum, (start_max, start_sum), (key_blocks, block_ids))
    log_total = final_max + jnp.log(final_sum)

    def pair_probs(query_blk, key_blk, allowed, log_blk):
        scores = jnp.where(allowed, pair_scores(query_blk, key_blk), -1e30)
        return jnp.where(allowed, jnp.exp(scores - log_blk[..., None]), 0.0)

    def probabilities(key_blk, key_index):
        return pair_probs(query_heads, key_blk, visible(key_index), log_total)

    def accumulate(total, item):
        key_blk, value_blk, key_index = item
        probs = probabilities(key_blk, key_index)
        return (
            total
            + jnp.einsum(
                "shtk,kshe->tshe",
                probs.astype(jnp.bfloat16),
                value_blk,
                preferred_element_type=jnp.float32,
            ),
            None,
        )

    start_out = jnp.zeros((span, seqs, heads_here, HEAD_DIM), jnp.float32)
    attended_f, _ = lax.scan(accumulate, start_out, (key_blocks, value_blocks, block_ids))
    attended = attended_f.astype(jnp.bfloat16).reshape(span, seqs, columns)
    branch = lax.psum_scatter(
        jnp.einsum("tsc,cd->tsd", attended, out_rows, preferred_element_type=jnp.float32).astype(
            jnp.bfloat16
        ),
        "head",
        scatter_dimension=0,
        tiled=True,
    ).astype(jnp.float32)
    middle = hidden_f + branch
    inv_two = inverse_rms(middle)
    normed_two = (middle * inv_two * ffn_gain).astype(jnp.bfloat16)
    flat_routes = routes.reshape(tok_rows * top_count)
    one_hot = (flat_routes[:, None] == jnp.arange(experts, dtype=jnp.int32)[None, :]).astype(
        jnp.int32
    )
    slots = jnp.sum((jnp.cumsum(one_hot, 0) - 1) * one_hot, 1)
    owners = jnp.arange(tok_rows * top_count, dtype=jnp.int32) // top_count
    flat_gates = gate_weights.reshape(tok_rows * top_count)

    def place(row_values):
        empty = jnp.zeros((experts, capacity, width), row_values.dtype)
        return jnp.repeat(empty.at[flat_routes, slots].set(row_values), 2, axis=0)

    token_rows = normed_two.reshape(tok_rows, width)
    received = move_rows(place(token_rows[owners]))
    expert_rows = received.reshape(-1, width)
    gate_pre = jnp.dot(expert_rows, w_gate[0], preferred_element_type=jnp.float32)
    up_pre = jnp.dot(expert_rows, w_up[0], preferred_element_type=jnp.float32)
    sigmoid_gate = jax.nn.sigmoid(gate_pre)
    activated = gate_pre * sigmoid_gate
    hidden_units = (activated * up_pre).astype(jnp.bfloat16)
    half_out = jnp.dot(hidden_units, w_down[0], preferred_element_type=jnp.float32).astype(
        jnp.bfloat16
    )
    returned = move_rows(half_out.reshape(received.shape))
    pair_sum = jnp.sum(returned.reshape(experts, 2, capacity, width).astype(jnp.float32), axis=1)
    picked = pair_sum[flat_routes, slots] * flat_gates[:, None]
    expert_sum = jnp.sum(picked.reshape(tok_rows, top_count, width), 1).reshape(piece, seqs, width)
    result = middle + expert_sum
    grad_y = cotangent.astype(jnp.float32)
    grad_rows_out = (flat_gates[:, None] * grad_y.reshape(tok_rows, width)[owners]).astype(
        jnp.bfloat16
    )
    grad_received = move_rows(place(grad_rows_out)).reshape(-1, width)
    grad_down = jnp.einsum(
        "rh,rd->hd", hidden_units, grad_received, preferred_element_type=jnp.float32
    )[None]
    grad_hidden = jnp.einsum(
        "rd,hd->rh", grad_received, w_down[0], preferred_element_type=jnp.float32
    ).astype(jnp.bfloat16)
    grad_gate_pre = (
        grad_hidden * up_pre * sigmoid_gate * (1.0 + gate_pre * (1.0 - sigmoid_gate))
    ).astype(jnp.bfloat16)
    grad_up_pre = (grad_hidden * activated).astype(jnp.bfloat16)
    grad_gate = jnp.einsum(
        "rd,rh->dh", expert_rows, grad_gate_pre, preferred_element_type=jnp.float32
    )[None]
    grad_up = jnp.einsum("rd,rh->dh", expert_rows, grad_up_pre, preferred_element_type=jnp.float32)[
        None
    ]
    grad_expert_rows = jnp.einsum(
        "rh,dh->rd", grad_gate_pre, w_gate[0], preferred_element_type=jnp.float32
    )
    grad_expert_rows = grad_expert_rows + jnp.einsum(
        "rh,dh->rd", grad_up_pre, w_up[0], preferred_element_type=jnp.float32
    )
    grad_returned = lax.all_to_all(
        grad_expert_rows.reshape(received.shape).astype(jnp.bfloat16),
        ("blk", "head"),
        split_axis=0,
        concat_axis=0,
        tiled=True,
    ).astype(jnp.float32)
    grad_pairs = jnp.sum(grad_returned.reshape(experts, 2, capacity, width), axis=1)
    grad_tokens = jnp.sum(grad_pairs[flat_routes, slots].reshape(tok_rows, top_count, width), 1)
    grad_normed_two = rounded(grad_tokens.reshape(piece, seqs, width))
    gained_two = grad_normed_two * ffn_gain
    ffn_gain_part = jnp.sum(grad_normed_two * middle * inv_two, (0, 1))
    grad_middle = (
        grad_y
        + inv_two * gained_two
        - middle * inv_two * inv_two * inv_two * jnp.mean(gained_two * middle, -1, keepdims=True)
    )
    grad_branch = grad_middle.astype(jnp.bfloat16)
    grad_group = lax.all_gather(grad_branch, "head", axis=0, tiled=True)
    grad_attended = jnp.einsum(
        "tsd,cd->tsc", grad_group, out_rows, preferred_element_type=jnp.float32
    ).astype(jnp.bfloat16)
    out_part = jnp.einsum("tsc,tsd->cd", attended, grad_group, preferred_element_type=jnp.float32)
    grad_heads = grad_attended.reshape(span, seqs, heads_here, HEAD_DIM)
    deltas = jnp.einsum("tshe,tshe->sht", grad_heads.astype(jnp.float32), attended_f)
    start_grad = jnp.zeros((span, seqs, heads_here, HEAD_DIM), jnp.float32)

    def grads_step(grad_query_acc, item):
        key_blk, value_blk, key_index = item
        probs = probabilities(key_blk, key_index)
        grad_probs = jnp.einsum(
            "tshe,kshe->shtk", grad_heads, value_blk, preferred_element_type=jnp.float32
        )
        grad_scores = (probs * (grad_probs - deltas[..., None])).astype(jnp.bfloat16)
        grad_query_acc = grad_query_acc + jnp.einsum(
            "shtk,kshe->tshe", grad_scores, key_blk, preferred_element_type=jnp.float32
        )
        grad_key_blk = jnp.einsum(
            "shtk,tshe->kshe", grad_scores, query_heads, preferred_element_type=jnp.float32
        )
        grad_value_blk = jnp.einsum(
            "shtk,tshe->kshe",
            probs.astype(jnp.bfloat16),
            grad_heads,
            preferred_element_type=jnp.float32,
        )
        return (grad_query_acc, (grad_key_blk, grad_value_blk))

    grad_query_heads, (grad_key_all, grad_value_all) = lax.scan(
        grads_step, start_grad, (key_blocks, value_blocks, block_ids)
    )
    grad_key_all = grad_key_all.reshape(blk_count * span, seqs, columns) * scale
    grad_value_all = grad_value_all.reshape(blk_count * span, seqs, columns)
    grad_key_own, grad_value_own = (
        lax.psum_scatter(
            grad_key_all.astype(jnp.bfloat16), "blk", scatter_dimension=0, tiled=True
        ).astype(jnp.float32),
        lax.psum_scatter(
            grad_value_all.astype(jnp.bfloat16), "blk", scatter_dimension=0, tiled=True
        ).astype(jnp.float32),
    )
    grad_query_n = rounded(grad_query_heads.reshape(span, seqs, columns) * scale)
    grad_key_n = rounded(grad_key_own)
    gained_query = grad_query_n * gain_query
    gained_key = grad_key_n * gain_key
    row_sums = lax.psum(
        (jnp.sum(gained_query * query_raw, -1), jnp.sum(gained_key * key_raw, -1)), "head"
    )
    grad_query_raw = (
        inv_query * gained_query
        - query_raw * inv_query * inv_query * inv_query * row_sums[0][..., None] / width
    )
    grad_key_raw = (
        inv_key * gained_key
        - key_raw * inv_key * inv_key * inv_key * row_sums[1][..., None] / width
    )
    query_gain_part = jnp.sum(grad_query_n * query_raw * inv_query, (0, 1))
    key_gain_part = jnp.sum(grad_key_n * key_raw * inv_key, (0, 1))
    grad_query_b = grad_query_raw.astype(jnp.bfloat16)
    grad_key_b = grad_key_raw.astype(jnp.bfloat16)
    grad_value_b = grad_value_own.astype(jnp.bfloat16)
    query_part = jnp.einsum("tsd,tsc->dc", group, grad_query_b, preferred_element_type=jnp.float32)
    key_part = jnp.einsum("tsd,tsc->dc", group, grad_key_b, preferred_element_type=jnp.float32)
    value_part = jnp.einsum("tsd,tsc->dc", group, grad_value_b, preferred_element_type=jnp.float32)
    total = jnp.einsum("tsc,dc->tsd", grad_query_b, query_cols, preferred_element_type=jnp.float32)
    total = total + jnp.einsum(
        "tsc,dc->tsd", grad_key_b, key_cols, preferred_element_type=jnp.float32
    )
    grad_normed = rounded(
        lax.psum_scatter(
            (
                total
                + jnp.einsum(
                    "tsc,dc->tsd", grad_value_b, value_cols, preferred_element_type=jnp.float32
                )
            ).astype(jnp.bfloat16),
            "head",
            scatter_dimension=0,
            tiled=True,
        ).astype(jnp.float32)
    )
    gained_one = grad_normed * attn_gain
    attn_gain_part = jnp.sum(grad_normed * hidden_f * inv_one, (0, 1))
    grad_hidden_in = (
        grad_middle
        + inv_one * gained_one
        - hidden_f
        * inv_one
        * inv_one
        * inv_one
        * jnp.mean(gained_one * hidden_f, -1, keepdims=True)
    )
    grad_query, grad_key, grad_value, grad_out = (
        lax.psum_scatter(
            query_part.astype(jnp.bfloat16), "blk", scatter_dimension=0, tiled=True
        ).astype(jnp.float32),
        lax.psum_scatter(
            key_part.astype(jnp.bfloat16), "blk", scatter_dimension=0, tiled=True
        ).astype(jnp.float32),
        lax.psum_scatter(
            value_part.astype(jnp.bfloat16), "blk", scatter_dimension=0, tiled=True
        ).astype(jnp.float32),
        lax.psum_scatter(
            out_part.astype(jnp.bfloat16), "blk", scatter_dimension=1, tiled=True
        ).astype(jnp.float32),
    )
    zero_width = jnp.zeros((width,), jnp.float32)
    query_gain_full = lax.dynamic_update_slice_in_dim(
        zero_width, query_gain_part, head_index * columns, 0
    )
    key_gain_full = lax.dynamic_update_slice_in_dim(
        zero_width, key_gain_part, head_index * columns, 0
    )
    square_parts = jnp.stack(
        [jnp.sum(result * result), jnp.sum(branch * branch), jnp.sum(expert_sum * expert_sum)]
    )
    totals = lax.psum(
        (square_parts, attn_gain_part, ffn_gain_part, query_gain_full, key_gain_full),
        ("blk", "head"),
    )
    entry_count = piece * seqs * width * blk_count * head_count
    stream_stats = jnp.sqrt(totals[0] / entry_count + EPSILON)
    return (
        result.astype(jnp.bfloat16),
        grad_hidden_in.astype(jnp.bfloat16),
        totals[1],
        grad_query,
        grad_key,
        grad_value,
        totals[3],
        totals[4],
        grad_out,
        totals[2],
        grad_gate,
        grad_up,
        grad_down,
        stream_stats,
    )


def solution(mesh):
    placed = (
        P(("blk", "head"), None, None),
        P(),
        P("blk", "head"),
        P("blk", "head"),
        P("blk", "head"),
        P(),
        P(),
        P("head", "blk"),
        P(),
        P(("blk", "head"), None, None),
        P(("blk", "head"), None, None),
        P(("blk", "head"), None, None),
        P(("blk", "head"), None, None),
        P(("blk", "head"), None, None),
        P(),
        P(("blk", "head"), None, None),
    )
    return jax.shard_map(
        local,
        mesh=mesh,
        in_specs=placed,
        out_specs=(
            P(("blk", "head"), None, None),
            P(("blk", "head"), None, None),
            P(),
            P("blk", "head"),
            P("blk", "head"),
            P("blk", "head"),
            P(),
            P(),
            P("head", "blk"),
            P(),
            P(("blk", "head"), None, None),
            P(("blk", "head"), None, None),
            P(("blk", "head"), None, None),
            P(),
        ),
        check_vma=False,
    )
```

profile of v0, /device:TPU:0, one launch (start us, length us, event | category | flops | bytes accessed | tf_op | source)
XLA Modules:
  0.0 3095.3 jit_solution(18250832605059938386)
XLA Ops:
  16.6 27.2 all-gather.19.cloned.1.call-done
  43.8 54.2 %all-gather.9.cloned.1.call-done = bf16[512,2,2048]{2,0,1:T(8,128)(2,1)} async-done(((bf16[128,2,2048]{2,0,1:T(8,128)(2,1)}), bf16[512,2,2048]{2,0,1:T(8,128)(2,1)}) %all-gather.9.cloned.1.call-update) | async-done | bytes 4194320 | tf_op jit(solution)/shard_map/all_gather | solution.py:63
  98.0 6.5 multiply_reduce_fusion.6
  104.5 26.5 all-gather.15.cloned.1.call-done
  131.0 6.6 multiply_reduce_fusion.7
  137.6 9.7 all-reduce.2
  151.0 9.7 all-gather.11.cloned.1.call-done
  160.7 6.2 fusion.148
  181.3 43.3 %scatter_custom_fusion.1 = bf16[2560,2048]{1,0:T(8,128)(2,1)} fusion(s32[2048]{0:T(1024)S(1)} %get-tuple-element.540, f32[2048]{0:T(1024)S(1)} %mul.455, bf16[]{:T(256)} %constant.142.clone.1, f32[256,2048]{1,0:T(8,128)} %reshape.425, s32[2048]{0:T(1024)S(1)} %get-tuple-element.539), kind=kCustom, calls=%fused_computation.123 | custom fusion | flops 8388608 | bytes 12599298
  224.5 13.1 broadcast_in_dim.103
  248.0 12.3 copy.165
  260.3 14.6 copy.107
  274.9 146.1 %all-gather.13.cloned.1.call-done = bf16[4096,2,512]{2,0,1:T(8,128)(2,1)} async-done(((bf16[512,2,512]{2,0,1:T(8,128)(2,1)}), bf16[4096,2,512]{2,0,1:T(8,128)(2,1)}) %all-gather.13.cloned.1.call-update) | async-done | bytes 8388624 | tf_op jit(solution)/shard_map/all_gather | solution.py:85
  421.0 12.5 reshape.414
  433.5 56.3 %while.39 = (s32[]{:T(128)}, f32[2,4,512]{2,1,0:T(4,128)S(1)}, f32[2,4,512]{2,1,0:T(4,128)S(1)}, s32[8]{0:T(128)S(1)}, s32[2,16]{1,0:T(2,128)S(1)}, /*index=5*/b...) while((s32[]{:T(128)}, f32[2,4,512]{2,1,0:T(4,128)S(1)}, ...), condition=%wide.region_9.10_spmd.clone, body=%wide.region_5.9_spmd.clone.sunk | while | flops 555032576 | bytes 21270820 | solution.py:128
  489.9 116.1 %while.40 = (s32[]{:T(128)}, f32[512,2,4,128]{0,3,2,1:T(8,128)}, bf16[8,512,2,4,128]{4,3,1,0,2:T(4,128)(2,1)}, s32[8]{0:T(128)S(1)}, s32[2,16]{1,0:T(2,128)S(1)}...) while((s32[]{:T(128)}, f32[512,2,4,128]{0,3,2,1:T(8,128)}, ...), condition=%wide.region_12.13_spmd.clone, body=%wide.region_10.12_spmd.clone.sunk | while | flops 1086640128 | bytes 13209903 | solution.py:153
  497.9 6.1 bitcast_add_fusion.4
  511.7 6.8 bitcast_add_fusion.4
  526.3 6.8 bitcast_add_fusion.4
  540.9 6.8 bitcast_add_fusion.4
  555.4 6.8 bitcast_add_fusion.4
  570.0 6.8 bitcast_add_fusion.4
  584.6 6.8 bitcast_add_fusion.4
  599.2 6.8 bitcast_add_fusion.4
  609.1 6.3 convolution_convert_fusion.2
  615.5 102.8 %reduce-scatter.9.cloned.1.call-done = bf16[128,2,2048]{2,0,1:T(8,128)(2,1)} async-done(((bf16[512,2,2048]{2,0,1:T(8,128)(2,1)}), bf16[128,2,2048]{2,0,1:T(8,128)(2,1)}) %reduce-scatter.9.cloned.1.call-update) | async-done | bytes 1048592 | tf_op jit(solution)/shard_map/reduce_scatter | solution.py:155
  724.2 46.8 %scatter_custom_fusion = bf16[2560,2048]{1,0:T(8,128)(2,1)} fusion(s32[2048]{0:T(1024)S(1)} %get-tuple-element.540, bf16[256,2048]{1,0:T(8,128)(2,1)} %reshape.420, s32[2048]{0:T(1024)S(1)} %get-tuple-element.539, bf16[]{:T(256)} %constant.142.clone.1), kind=kCustom, calls=%fused_computation.124 | custom fusion | bytes 10486272
  771.0 40.2 %all-to-all-done.2 = bf16[32,160,2048]{2,1,0:T(8,128)(2,1)} async-done(((bf16[32,160,2048]{2,1,0:T(8,128)(2,1)}), bf16[32,160,2048]{2,1,0:T(8,128)(2,1)}, u32[]{:S(2)}, u32[]{:S(2)}) %all-to-all-start.2) | async-done | bytes 20971552 | tf_op jit(solution)/shard_map/all_to_all | solution.py:58
  811.2 13.3 broadcast_in_dim.102
  828.4 17.4 convolution_convert_fusion.1
  845.8 463.9 %all-to-all-done = bf16[32,160,2048]{2,1,0:T(8,128)(2,1)} async-done(((bf16[32,160,2048]{2,1,0:T(8,128)(2,1)}), bf16[32,160,2048]{2,1,0:T(8,128)(2,1)}, u32[]{:S(2)}, u32[]{:S(2)}) %all-to-all-start) | async-done | bytes 20971552 | tf_op jit(solution)/shard_map/all_to_all | solution.py:58
  1309.8 18.1 fusion.132
  1327.9 22.6 fusion.80
  1350.5 18.0 convolution_convert_fusion
  1372.8 21.7 fusion.130
  1394.6 26.6 add_convert_fusion
  1421.2 433.0 %all-to-all-done.1 = bf16[32,160,2048]{2,1,0:T(8,128)(2,1)} async-done(((bf16[32,160,2048]{2,1,0:T(8,128)(2,1)}), bf16[32,160,2048]{2,1,0:T(8,128)(2,1)}, u32[]{:S(2)}, u32[]{:S(2)}) %all-to-all-start.1) | async-done | bytes 20971552 | tf_op jit(solution)/shard_map/all_to_all | solution.py:58
  1858.2 20.5 convert_reduce_fusion.1
  1878.7 51.0 %gather_fusion = f32[2048,2048]{1,0:T(8,128)} fusion(f32[16,160,2048]{2,1,0:T(8,128)} %convert_reduce_fusion.1, s32[2048]{0:T(1024)S(1)} %bitcast.295), kind=kCustom, calls=%fused_computation.1 | custom fusion | bytes 33570816 | tf_op jit(solution)/shard_map/gather | solution.py:191
  1929.7 10.1 fusion.77
  1943.3 396.1 %all-to-all-done.3 = bf16[32,160,2048]{2,1,0:T(8,128)(2,1)} async-done(((bf16[32,160,2048]{2,1,0:T(8,128)(2,1)}), bf16[32,160,2048]{2,1,0:T(8,128)(2,1)}, u32[]{:S(2)}, u32[]{:S(2)}) %all-to-all-start.3) | async-done | bytes 20971552 | tf_op jit(solution)/shard_map/all_to_all | solution.py:221
  2339.4 20.4 convert_reduce_fusion
  2359.8 51.0 %gather_fusion.1 = f32[2048,2048]{1,0:T(8,128)} fusion(f32[16,160,2048]{2,1,0:T(8,128)} %convert_reduce_fusion, s32[2048]{0:T(1024)S(1)} %bitcast.296), kind=kCustom, calls=%fused_computation.3 | custom fusion | bytes 33570816 | tf_op jit(solution)/shard_map/gather | solution.py:229
  2410.8 9.3 bitcast_reduce_fusion
  2422.1 5.8 fusion.115
  2431.5 48.6 %all-gather.23.cloned.1.call-done = bf16[512,2,2048]{2,0,1:T(8,128)(2,1)} async-done(((bf16[128,2,2048]{2,0,1:T(8,128)(2,1)}), bf16[512,2,2048]{2,0,1:T(8,128)(2,1)}) %all-gather.23.cloned.1.call-update) | async-done | bytes 4194320 | tf_op jit(solution)/shard_map/all_gather | solution.py:239
  2486.9 141.9 %while.41 = (s32[]{:T(128)}, f32[512,2,4,128]{0,3,2,1:T(8,128)}, f32[8,512,2,4,128]{4,1,3,2,0:T(8,128)}, bf16[8,512,2,4,128]{4,1,3,2,0:T(8,128)(2,1)}, bf16[8,51...) while((s32[]{:T(128)}, f32[512,2,4,128]{0,3,2,1:T(8,128)}, ...), condition=%wide.region_27.28_spmd.clone, body=%wide.region_25.27_spmd.clone.sunk | while | flops 2711932928 | bytes 74584464 | solution.py:269
  2628.9 14.7 copy.129
  2643.5 13.5 convert_element_type.225
  2657.1 10.3 multiply_convert_fusion
  2667.4 14.7 copy.126
  2682.1 13.6 convert_element_type.221
  2697.0 5.8 bitcast_convert_fusion
  2702.9 44.0 %reduce-scatter.13.cloned.1.call-done = bf16[512,2,512]{0,2,1:T(8,128)(2,1)} async-done(((bf16[4096,2,512]{0,2,1:T(8,128)(2,1)}), bf16[512,2,512]{0,2,1:T(8,128)(2,1)}) %reduce-scatter.13.cloned.1.call-update) | async-done | bytes 1048592 | tf_op jit(solution)/shard_map/reduce_scatter | solution.py:278
  2746.8 6.2 bitcast_convert_fusion.1
  2755.9 81.4 %reduce-scatter.11.cloned.1.call-done = bf16[512,2,512]{0,2,1:T(8,128)(2,1)} async-done(((bf16[4096,2,512]{0,2,1:T(8,128)(2,1)}), bf16[512,2,512]{0,2,1:T(8,128)(2,1)}) %reduce-scatter.11.cloned.1.call-update) | async-done | bytes 1048592 | tf_op jit(solution)/shard_map/reduce_scatter | solution.py:275
  2839.2 10.0 all-reduce.1
  2875.2 18.5 convolution_bitcast_fusion
  2893.7 16.6 convolution_bitcast_fusion.2
  2910.3 21.8 convolution_bitcast_fusion.1
  2941.4 5.9 reduce-scatter.17.cloned.1.call-done
  2949.0 34.9 %reduce-scatter.19.cloned.1.call-done = bf16[256,512]{1,0:T(8,128)(2,1)} async-done(((bf16[2048,512]{1,0:T(8,128)(2,1)}), bf16[256,512]{1,0:T(8,128)(2,1)}) %reduce-scatter.19.cloned.1.call-update) | async-done | bytes 262160 | tf_op jit(solution)/shard_map/reduce_scatter | solution.py:337
  2985.7 52.6 %reduce-scatter.15.cloned.1.call-done = bf16[128,2,2048]{2,0,1:T(8,128)(2,1)} async-done(((bf16[512,2,2048]{2,0,1:T(8,128)(2,1)}), bf16[128,2,2048]{2,0,1:T(8,128)(2,1)}) %reduce-scatter.15.cloned.1.call-update) | async-done | bytes 1048592 | tf_op jit(solution)/shard_map/reduce_scatter | solution.py:310
  3040.9 40.8 %all-reduce = (f32[2048]{0:T(1024)}, f32[2048]{0:T(1024)}, f32[2048]{0:T(1024)}, f32[2048]{0:T(1024)}, f32[3]{0:T(128)S(1)}) all-reduce(f32[2048]{0:T(1024)S(1)} %get-tuple-element.447, f32[2048]{0:T(1024)S(1)} %dynamic_update_slice.13, f32[2048]{0:T(1024)S(1)} %dynamic_update_slice.14, ...), channel_id=1, replica_groups=mesh['head'=4,'blk'=8] {'blk','head'}, use_global_device_ids=true, to_apply=%region_37.38 | all-reduce | flops 8195 | bytes 65560 | tf_op jit(solution)/shard_map/psum | solution.py:357
  (523 shorter events, 371.7 us)
Async XLA Ops:
  7.2 1320.7 %copy-start = (bf16[1,2048,512]{2,1,0:T(8,128)(2,1)S(1)}, bf16[1,2048,512]{2,1,0:T(8,128)(2,1)}, u32[]{:S(2)}) copy-start(bf16[1,2048,512]{2,1,0:T(8,128)(2,1)} %param.32) | copy-start | bytes 6291460
  7.2 7.1 copy-start.27
  7.2 36.6 %all-gather.19.cloned.1.call-start = ((), (), s32[]{:S(2)}) async-start(), calls=%async_computation.17 | async-start | bytes 2359296 | tf_op jit(solution)/shard_map/all_gather | solution.py:65
  9.2 88.8 %all-gather.9.cloned.1.call-start = ((), (), s32[]{:S(2)}) async-start(), calls=%async_computation.12 | async-start | bytes 5242880 | tf_op jit(solution)/shard_map/all_gather | solution.py:63
  14.3 116.8 %all-gather.15.cloned.1.call-start = ((), (), s32[]{:S(2)}) async-start(), calls=%async_computation.15 | async-start | bytes 2359296 | tf_op jit(solution)/shard_map/all_gather | solution.py:66
  15.2 145.5 %all-gather.11.cloned.1.call-start = ((), (), s32[]{:S(2)}) async-start(), calls=%async_computation.13 | async-start | bytes 2359296 | tf_op jit(solution)/shard_map/all_gather | solution.py:67
  15.8 232.2 %all-gather.17.cloned.1.call-start = ((), (), s32[]{:S(2)}) async-start(), calls=%async_computation.16 | async-start | bytes 9437184 | tf_op jit(solution)/shard_map/all_gather | solution.py:84
  16.6 130.7 %copy-start.40 = (f32[512]{0:T(512)}, f32[512]{0:T(512)S(1)}, u32[]{:S(2)}) copy-start(f32[512]{0:T(512)S(1)} %dynamic_slice.32) | copy-start | bytes 6148
  150.7 16.1 copy-start.53
  150.8 22.1 copy-start.54
  150.8 22.4 copy-start.16
  150.8 270.2 %all-gather.13.cloned.1.call-start = ((), (), s32[]{:S(2)}) async-start(), calls=%async_computation.14 | async-start | bytes 9437184 | tf_op jit(solution)/shard_map/all_gather | solution.py:85
  173.0 7.2 copy-start.21
  173.6 7.4 copy-start.56
  173.6 7.5 copy-start.55
  237.7 573.5 %all-to-all-start.2 = ((bf16[32,160,2048]{2,1,0:T(8,128)(2,1)}), bf16[32,160,2048]{2,1,0:T(8,128)(2,1)}, u32[]{:S(2)}, u32[]{:S(2)}) async-start(bf16[32,160,2048]{2,1,0:T(8,128)(2,1)} %bitcast.297), calls=%async_computation.3 | async-start | bytes 41943040 | tf_op jit(solution)/shard_map/all_to_all | solution.py:58
  241.9 367.1 %all-gather.21.cloned.1.call-start = ((), (), s32[]{:S(2)}) async-start(), calls=%async_computation.18 | async-start | bytes 2359296 | tf_op jit(solution)/shard_map/all_gather | solution.py:68
  242.7 475.6 %reduce-scatter.9.cloned.1.call-start = ((), (), s32[]{:S(2)}) async-start(), calls=%async_computation.19 | async-start | bytes 5242880 | tf_op jit(solution)/shard_map/reduce_scatter | solution.py:155
  243.5 16.7 copy-start.42
  274.9 158.6 %copy-start.28 = (s32[2,16]{1,0:T(2,128)S(1)}, s32[2,16]{1,0:T(2,128)}, u32[]{:S(2)}) copy-start(s32[2,16]{1,0:T(2,128)} %param.36) | copy-start | bytes 388
  606.0 9.4 copy-start.3
  606.0 9.4 copy-start.29
  606.0 9.4 copy-start.47
  615.4 104.6 %copy-start.31 = (f32[2048]{0:T(1024)S(1)}, f32[2048]{0:T(1024)}, u32[]{:S(2)}) copy-start(f32[2048]{0:T(1024)} %param.30) | copy-start | bytes 24580
  615.4 102.8 %copy-start.8 = (bf16[128,2,2048]{2,1,0:T(2,128)(2,1)S(1)}, bf16[128,2,2048]{2,1,0:T(2,128)(2,1)}, u32[]{:S(2)}) copy-start(bf16[128,2,2048]{2,1,0:T(2,128)(2,1)} %param.22) | copy-start | bytes 3145732
  720.0 51.0 %copy-start.44 = (f32[128,2]{0,1:T(2,128)}, f32[128,2]{0,1:T(2,128)S(1)}, u32[]{:S(2)}) copy-start(f32[128,2]{0,1:T(2,128)S(1)} %add_rsqrt_fusion.2) | copy-start | bytes 3076
  824.5 485.3 %all-to-all-start = ((bf16[32,160,2048]{2,1,0:T(8,128)(2,1)}), bf16[32,160,2048]{2,1,0:T(8,128)(2,1)}, u32[]{:S(2)}, u32[]{:S(2)}) async-start(bf16[32,160,2048]{2,1,0:T(8,128)(2,1)} %bitcast.298), calls=%async_computation.1 | async-start | bytes 41943040 | tf_op jit(solution)/shard_map/all_to_all | solution.py:58
  1368.5 485.7 %all-to-all-start.1 = ((bf16[32,160,2048]{2,1,0:T(8,128)(2,1)}), bf16[32,160,2048]{2,1,0:T(8,128)(2,1)}, u32[]{:S(2)}, u32[]{:S(2)}) async-start(bf16[32,160,2048]{2,1,0:T(8,128)(2,1)} %bitcast.303), calls=%async_computation.2 | async-start | bytes 41943040 | tf_op jit(solution)/shard_map/all_to_all | solution.py:58
  1854.1 485.3 %all-to-all-start.3 = ((bf16[32,160,2048]{2,1,0:T(8,128)(2,1)}), bf16[32,160,2048]{2,1,0:T(8,128)(2,1)}, u32[]{:S(2)}, u32[]{:S(2)}) async-start(bf16[32,160,2048]{2,1,0:T(8,128)(2,1)} %bitcast.302), calls=%async_computation.4 | async-start | bytes 41943040 | tf_op jit(solution)/shard_map/all_to_all | solution.py:221
  1858.1 20.6 copy-start.2
  1858.1 622.0 %all-gather.23.cloned.1.call-start = ((), (), s32[]{:S(2)}) async-start(), calls=%async_computation.20 | async-start | bytes 5242880 | tf_op jit(solution)/shard_map/all_gather | solution.py:239
  1878.7 51.0 %copy-start.22 = (f32[128,2,8]{2,1,0:T(2,128)S(1)}, f32[128,2,8]{2,1,0:T(2,128)}, u32[]{:S(2)}) copy-start(f32[128,2,8]{2,1,0:T(2,128)} %copy-done.21) | copy-start | bytes 24580
  2410.8 11.2 copy-start.9
  2410.8 11.2 copy-start.11
  2410.8 11.3 copy-start.32
  2410.8 11.3 copy-start.45
  2422.1 9.3 copy-start.15
  2422.1 6.4 copy-start.17
  2431.4 315.4 %reduce-scatter.13.cloned.1.call-start = ((), (), s32[]{:S(2)}) async-start(), calls=%async_computation.22 | async-start | bytes 9437184 | tf_op jit(solution)/shard_map/reduce_scatter | solution.py:278
  2431.5 55.4 %copy-start.4 = (bf16[512,2,4,128]{3,0,2,1:T(8,128)(2,1)S(1)}, bf16[512,2,4,128]{3,0,2,1:T(8,128)(2,1)}, u32[]{:S(2)}) copy-start(bf16[512,2,4,128]{3,0,2,1:T(8,128)(2,1)} %copy-done.3) | copy-start | bytes 3145732
  2431.5 55.4 %copy-start.30 = (s32[2,16]{1,0:T(2,128)S(1)}, s32[2,16]{1,0:T(2,128)}, u32[]{:S(2)}) copy-start(s32[2,16]{1,0:T(2,128)} %copy-done.29) | copy-start | bytes 388
  2431.5 55.4 %copy-start.48 = (f32[2,4,512]{2,1,0:T(4,128)S(1)}, f32[2,4,512]{2,1,0:T(4,128)}, u32[]{:S(2)}) copy-start(f32[2,4,512]{2,1,0:T(4,128)} %copy-done.47) | copy-start | bytes 49156
  2657.1 180.2 %reduce-scatter.11.cloned.1.call-start = ((), (), s32[]{:S(2)}) async-start(), calls=%async_computation.21 | async-start | bytes 9437184 | tf_op jit(solution)/shard_map/reduce_scatter | solution.py:275
  2695.7 241.9 %reduce-scatter.23.cloned.1.call-start = ((), (), s32[]{:S(2)}) async-start(), calls=%async_computation.27 | async-start | bytes 2359296 | tf_op jit(solution)/shard_map/reduce_scatter | solution.py:343
  2702.8 50.3 %copy-start.7 = (f32[512,2,4,128]{0,3,2,1:T(8,128)S(1)}, f32[512,2,4,128]{0,3,2,1:T(8,128)}, u32[]{:S(2)}) copy-start(f32[512,2,4,128]{0,3,2,1:T(8,128)} %get-tuple-element.191) | copy-start | bytes 6291460
  2702.8 236.7 %reduce-scatter.21.cloned.1.call-start = ((), (), s32[]{:S(2)}) async-start(), calls=%async_computation.26 | async-start | bytes 2359296 | tf_op jit(solution)/shard_map/reduce_scatter | solution.py:340
  2753.0 84.2 %copy-start.36 = (f32[512,2]{0,1:T(2,128)S(1)}, f32[512,2]{0,1:T(2,128)}, u32[]{:S(2)}) copy-start(f32[512,2]{0,1:T(2,128)} %copy-done.35) | copy-start | bytes 12292
  2753.0 84.2 %copy-start.41 = (f32[512]{0:T(512)S(1)}, f32[512]{0:T(512)}, u32[]{:S(2)}) copy-start(f32[512]{0:T(512)} %copy-done.40) | copy-start | bytes 6148
  2753.1 194.1 %reduce-scatter.17.cloned.1.call-start = ((), (), s32[]{:S(2)}) async-start(), calls=%async_computation.24 | async-start | bytes 2359296 | tf_op jit(solution)/shard_map/reduce_scatter | solution.py:334
  2753.4 83.8 %copy-start.13 = (f32[512,2,512]{0,2,1:T(8,128)S(1)}, f32[512,2,512]{0,2,1:T(8,128)}, u32[]{:S(2)}) copy-start(f32[512,2,512]{0,2,1:T(8,128)} %get-tuple-element.534) | copy-start | bytes 6291460
  2856.5 127.4 %reduce-scatter.19.cloned.1.call-start = ((), (), s32[]{:S(2)}) async-start(), calls=%async_computation.25 | async-start | bytes 2359296 | tf_op jit(solution)/shard_map/reduce_scatter | solution.py:337
  2863.2 175.2 %reduce-scatter.15.cloned.1.call-start = ((), (), s32[]{:S(2)}) async-start(), calls=%async_computation.23 | async-start | bytes 5242880 | tf_op jit(solution)/shard_map/reduce_scatter | solution.py:310
  2875.2 18.5 slice-start
  2875.2 18.5 slice-start.1
  2910.3 21.8 copy-start.18
  2910.3 23.9 copy-start.12
  2932.1 106.2 %copy-start.10 = (bf16[128,2,2048]{2,1,0:T(2,128)(2,1)S(1)}, bf16[128,2,2048]{2,1,0:T(2,128)(2,1)}, u32[]{:S(2)}) copy-start(bf16[128,2,2048]{2,1,0:T(2,128)(2,1)} %param.22) | copy-start | bytes 3145732
  2932.1 106.2 %copy-start.34 = (f32[2048]{0:T(1024)S(1)}, f32[2048]{0:T(1024)}, u32[]{:S(2)}) copy-start(f32[2048]{0:T(1024)} %param.23) | copy-start | bytes 24580
  2932.1 106.2 %copy-start.50 = (f32[128,2]{0,1:T(2,128)S(1)}, f32[128,2]{0,1:T(2,128)}, u32[]{:S(2)}) copy-start(f32[128,2]{0,1:T(2,128)} %copy-done.49) | copy-start | bytes 3076
  2934.2 106.7 %copy-start.39 = (f32[2048]{0:T(1024)S(1)}, f32[2048]{0:T(1024)}, u32[]{:S(2)}) copy-start(f32[2048]{0:T(1024)} %get-tuple-element.440) | copy-start | bytes 24580
  2934.2 148.0 %copy-start.33 = (f32[2048]{0:T(1024)S(1)}, f32[2048]{0:T(1024)}, u32[]{:S(2)}) copy-start(f32[2048]{0:T(1024)} %param.30) | copy-start | bytes 24580
  2934.2 148.0 %copy-start.46 = (f32[128,2]{0,1:T(2,128)S(1)}, f32[128,2]{0,1:T(2,128)}, u32[]{:S(2)}) copy-start(f32[128,2]{0,1:T(2,128)} %copy-done.44) | copy-start | bytes 3076
  2934.2 148.0 %copy-start.52 = (f32[128,2]{0,1:T(2,128)S(1)}, f32[128,2]{0,1:T(2,128)}, u32[]{:S(2)}) copy-start(f32[128,2]{0,1:T(2,128)} %copy-done.51) | copy-start | bytes 3076
  3082.1 6.1 copy-start.1
  (33 other events, 83.3 us)
Sparse Core Ops, SparseCore 0:
  10.2 33.5 all-gather.18
  46.2 51.7 all-gather.8
  100.2 30.8 all-gather.14
  132.5 28.1 all-gather.10
  162.7 81.5 all-gather.16
  246.3 174.5 all-gather.12
  422.6 73.6 all-gather.20
  615.6 102.6 reduce-scatter.8
  2431.5 48.5 all-gather.22
  2657.2 89.5 reduce-scatter.12
  2749.2 87.9 reduce-scatter.10
  2839.5 34.1 reduce-scatter.22
  2876.1 34.3 reduce-scatter.20
  2912.8 34.4 reduce-scatter.16
  2949.5 34.4 reduce-scatter.18
  2987.0 51.2 reduce-scatter.14
where the time goes:
time: 3110 us; the launch traced here: 3100 us
  waiting for transfers between devices  1970 us (63%)
  matrix products  433 us (14%)
  local copies, waits for them, and re-layouts  372 us (12%)
  other arithmetic  210 us (7%)
  blocking collectives  60.5 us (2%)
    all_to_all x3, waiting for transfers between devices, move_rows(): lax.all_to_all(buffer, ('blk', 'head'), split_axis=0, concat_axis=0, tile...  937 us
    all_to_all x1, waiting for transfers between devices, local(): lax.all_to_all(grad_expert_rows.reshape(received.shape).astype(jnp.bfloat...  396 us
    all_gather x1, waiting for transfers between devices, local(): lax.all_gather(value_n, 'blk', axis=0, tiled=True)  146 us
    reduce_scatter x1, waiting for transfers between devices, local(): lax.psum_scatter(jnp.einsum('tsc,cd->tsd', attended, out_rows, preferred_...  103 us
    unnamed x133, local copies, waits for them, and re-layouts  90.6 us
    reduce_scatter x1, waiting for transfers between devices, local(): lax.psum_scatter(grad_key_all.astype(jnp.bfloat16), 'blk', scatter_dimens...  81.4 us
    dynamic_slice x48, local copies, waits for them, and re-layouts, local(): lax.scan(max_sum, (start_max, start_sum), (key_blocks, block_ids))  66.4 us
  transfers between devices with their start and end apart: 20, of which 16 were waited for; matrix products, arithmetic and copies ran while one was open for 21% of the time, Pallas kernels for 0%

commit v1 on v0

v1 whole, which is shorter than its diff:
```python
import functools
import math

import jax
import jax.numpy as jnp
from jax import lax
from jax.experimental import pallas as pl
from jax.experimental.pallas import tpu as pltpu
from jax.sharding import PartitionSpec as P

HEAD_DIM = 128
BLOCK = 256
EPSILON = 1e-06
F32 = jnp.float32
BF16 = jnp.bfloat16
VMEM_BYTES = 58 * 1024 * 1024

NN = (((1,), (0,)), ((), ()))
NT = (((1,), (1,)), ((), ()))
TN = (((0,), (0,)), ((), ()))


def mm(left, right, dims=NN):
    return lax.dot_general(left, right, dims, preferred_element_type=F32)


def rounded(values):
    return lax.optimization_barrier(values.astype(BF16)).astype(F32)


def inverse_rms(values):
    return lax.rsqrt(jnp.mean(values * values, axis=-1, keepdims=True) + EPSILON)


def attend_forward(starts, own, qkv, scale, share):
    src, _, per, block, dim = qkv.shape
    blocks = src * per

    def kernel(starts_ref, own_ref, qkv_ref, out_ref, out_t_ref, lse_ref, vt_ref):
        step = pl.program_id(0)

        @pl.when(step == 0)
        def _():
            def flip(j, carry):
                vt_ref[j] = qkv_ref[j // per, 2, j % per].astype(F32).T.astype(BF16)
                return carry

            lax.fori_loop(0, blocks, flip, 0)

        def work():
            query = qkv_ref[step // per, 0, step % per]

            def body(j, carry):
                top, total, acc = carry
                scores = mm(qkv_ref[j // per, 1, j % per], query, NT) * scale
                new_top = jnp.maximum(top, jnp.max(scores, axis=0, keepdims=True))
                weights = jnp.exp(scores - new_top)
                shrink = jnp.exp(top - new_top)
                total = total * shrink + jnp.sum(weights, axis=0, keepdims=True)
                acc = acc * shrink + mm(vt_ref[j], weights.astype(BF16))
                return new_top, total, acc

            top, total, acc = lax.fori_loop(
                starts_ref[step],
                step + 1,
                body,
                (
                    jnp.full((1, block), -1e30, F32),
                    jnp.zeros((1, block), F32),
                    jnp.zeros((dim, block), F32),
                ),
            )
            result = acc / total
            out_t_ref[0] = result
            out_ref[0] = result.T.astype(BF16)
            lse_ref[0] = top + jnp.log(total)

        if share == 1:
            work()
        else:
            mine = step % share == own_ref[0]
            pl.when(mine)(work)

            @pl.when(jnp.logical_not(mine))
            def _():
                out_t_ref[...] = jnp.zeros_like(out_t_ref)
                out_ref[...] = jnp.zeros_like(out_ref)
                lse_ref[...] = jnp.zeros_like(lse_ref)

    return pl.pallas_call(
        kernel,
        grid_spec=pltpu.PrefetchScalarGridSpec(
            num_scalar_prefetch=2,
            grid=(blocks,),
            in_specs=[pl.BlockSpec(qkv.shape, lambda i, *_: (0, 0, 0, 0, 0))],
            out_specs=[
                pl.BlockSpec((1, block, dim), lambda i, *_: (i, 0, 0)),
                pl.BlockSpec((1, dim, block), lambda i, *_: (i, 0, 0)),
                pl.BlockSpec((1, 1, block), lambda i, *_: (i, 0, 0)),
            ],
            scratch_shapes=[pltpu.VMEM((blocks, dim, block), BF16)],
        ),
        out_shape=[
            jax.ShapeDtypeStruct((blocks, block, dim), BF16),
            jax.ShapeDtypeStruct((blocks, dim, block), F32),
            jax.ShapeDtypeStruct((blocks, 1, block), F32),
        ],
        compiler_params=pltpu.CompilerParams(vmem_limit_bytes=VMEM_BYTES),
        name="attend_forward",
    )(starts, own, qkv)


def attend_backward(starts, own, qkv, grad_out, out_t, lse, scale, share):
    src, _, per, block, dim = qkv.shape
    blocks = src * per

    def kernel(
        starts_ref, own_ref, qkv_ref, go_ref, out_t_ref, lse_ref, grad_ref, dk_ref, dv_ref
    ):
        step = pl.program_id(0)

        @pl.when(step == 0)
        def _():
            dk_ref[...] = jnp.zeros_like(dk_ref)
            dv_ref[...] = jnp.zeros_like(dv_ref)

        def work():
            query = qkv_ref[step // per, 0, step % per]
            go = go_ref[0]
            delta = jnp.sum(go.astype(F32).T * out_t_ref[0], axis=0, keepdims=True)
            log_total = lse_ref[0]

            def body(j, dq):
                key = qkv_ref[j // per, 1, j % per]
                value = qkv_ref[j // per, 2, j % per]
                probs = jnp.exp(mm(key, query, NT) * scale - log_total)
                grad_scores = (probs * (mm(value, go, NT) - delta)).astype(BF16)
                dv_ref[j] += mm(probs.astype(BF16), go)
                dk_ref[j] += mm(grad_scores, query)
                return dq + mm(grad_scores, key, TN)

            dq = lax.fori_loop(starts_ref[step], step + 1, body, jnp.zeros((block, dim), F32))
            grad_ref[step // per, 0, step % per] = (dq * scale).astype(BF16)

        if share == 1:
            work()
        else:
            mine = step % share == own_ref[0]
            pl.when(mine)(work)

            @pl.when(jnp.logical_not(mine))
            def _():
                grad_ref[step // per, 0, step % per] = jnp.zeros((block, dim), BF16)

        @pl.when(step == blocks - 1)
        def _():
            def store(j, carry):
                grad_ref[j // per, 1, j % per] = (dk_ref[j] * scale).astype(BF16)
                grad_ref[j // per, 2, j % per] = dv_ref[j].astype(BF16)
                return carry

            lax.fori_loop(0, blocks, store, 0)

    return pl.pallas_call(
        kernel,
        grid_spec=pltpu.PrefetchScalarGridSpec(
            num_scalar_prefetch=2,
            grid=(blocks,),
            in_specs=[
                pl.BlockSpec(qkv.shape, lambda i, *_: (0, 0, 0, 0, 0)),
                pl.BlockSpec((1, block, dim), lambda i, *_: (i, 0, 0)),
                pl.BlockSpec((1, dim, block), lambda i, *_: (i, 0, 0)),
                pl.BlockSpec((1, 1, block), lambda i, *_: (i, 0, 0)),
            ],
            out_specs=pl.BlockSpec(qkv.shape, lambda i, *_: (0, 0, 0, 0, 0)),
            scratch_shapes=[
                pltpu.VMEM((blocks, block, dim), F32),
                pltpu.VMEM((blocks, block, dim), F32),
            ],
        ),
        out_shape=jax.ShapeDtypeStruct(qkv.shape, BF16),
        compiler_params=pltpu.CompilerParams(vmem_limit_bytes=VMEM_BYTES),
        name="attend_backward",
    )(starts, own, qkv, grad_out, out_t, lse)


def expert_rows(tokens, cots, slots, gates, w_gate, w_up, w_down, rows, step_blocks):
    blocks, tok, width = tokens.shape
    half = w_gate.shape[1]
    count = step_blocks * rows
    steps = blocks // step_blocks
    chunk = min(512, width)

    def kernel(
        tok_ref, cot_ref, slot_ref, gate_ref, wg_ref, wu_ref, wd_ref,
        moe_ref, dx_ref, xr_ref, er_ref, hid_ref, dgp_ref, dup_ref,
    ):
        lanes = lax.broadcasted_iota(jnp.int32, (rows, tok), 0)
        picks = []
        weights = []
        for b in range(step_blocks):
            hit = lanes == slot_ref[b]
            pick = jnp.where(hit, 1.0, 0.0).astype(BF16)
            weight = jnp.sum(jnp.where(hit, gate_ref[b], 0.0), axis=1, keepdims=True)
            here = slice(b * rows, (b + 1) * rows)
            picks.append(pick)
            weights.append(weight)
            for c in range(0, width, chunk):
                cols = slice(c, c + chunk)
                xr_ref[0, here, cols] = mm(pick, tok_ref[b, :, cols]).astype(BF16)
                er_ref[0, here, cols] = (weight * mm(pick, cot_ref[b, :, cols])).astype(BF16)
        x = xr_ref[0]
        gate_pre = mm(x, wg_ref[...])
        up_pre = mm(x, wu_ref[...])
        sig = jax.nn.sigmoid(gate_pre)
        act = gate_pre * sig
        hid = (act * up_pre).astype(BF16)
        hid_ref[0] = hid
        dhid = mm(er_ref[0], wd_ref[...], NT).astype(BF16).astype(F32)
        dgp = (dhid * up_pre * sig * (1.0 + gate_pre * (1.0 - sig))).astype(BF16)
        dup = (dhid * act).astype(BF16)
        dgp_ref[0] = dgp
        dup_ref[0] = dup
        for c in range(0, width, chunk):
            cols = slice(c, c + chunk)
            part = mm(hid, wd_ref[:, cols]).astype(BF16).astype(F32)
            drow = (mm(dgp, wg_ref[cols, :], NT) + mm(dup, wu_ref[cols, :], NT)).astype(BF16)
            for b in range(step_blocks):
                here = slice(b * rows, (b + 1) * rows)
                weighted = (part[here] * weights[b]).astype(BF16)
                moe_ref[b, :, cols] = mm(picks[b], weighted, TN).astype(BF16)
                dx_ref[b, :, cols] = mm(picks[b], drow[here], TN).astype(BF16)

    whole = lambda shape: pl.BlockSpec(shape, lambda i: (0,) * len(shape), pipeline_mode=pl.Buffered(1))
    per_step = lambda *shape: pl.BlockSpec(shape, lambda i: (i,) + (0,) * (len(shape) - 1))
    return pl.pallas_call(
        kernel,
        grid=(steps,),
        in_specs=[
            per_step(step_blocks, tok, width),
            per_step(step_blocks, tok, width),
            per_step(step_blocks, 1, tok),
            per_step(step_blocks, 1, tok),
            whole(w_gate.shape),
            whole(w_up.shape),
            whole(w_down.shape),
        ],
        out_specs=[
            per_step(step_blocks, tok, width),
            per_step(step_blocks, tok, width),
            per_step(1, count, width),
            per_step(1, count, width),
            per_step(1, count, half),
            per_step(1, count, half),
            per_step(1, count, half),
        ],
        out_shape=[
            jax.ShapeDtypeStruct((blocks, tok, width), BF16),
            jax.ShapeDtypeStruct((blocks, tok, width), BF16),
            jax.ShapeDtypeStruct((steps, count, width), BF16),
            jax.ShapeDtypeStruct((steps, count, width), BF16),
            jax.ShapeDtypeStruct((steps, count, half), BF16),
            jax.ShapeDtypeStruct((steps, count, half), BF16),
            jax.ShapeDtypeStruct((steps, count, half), BF16),
        ],
        compiler_params=pltpu.CompilerParams(vmem_limit_bytes=VMEM_BYTES),
        name="expert_rows",
    )(tokens, cots, slots, gates, w_gate, w_up, w_down)


def local(
    hidden_in,
    attn_gain,
    w_query,
    w_key,
    w_value,
    query_gain,
    key_gain,
    w_out,
    ffn_gain,
    w_gate,
    w_up,
    w_down,
    routes,
    gate_weights,
    block_starts,
    cotangent,
):
    head_count = lax.axis_size("head")
    blk_count = lax.axis_size("blk")
    head_index = lax.axis_index("head")
    blk_index = lax.axis_index("blk")
    piece, seqs, width = hidden_in.shape
    span = piece * head_count
    per = span // BLOCK
    columns = w_query.shape[1]
    heads_here = columns // HEAD_DIM
    top_count = routes.shape[2]
    experts = blk_count * head_count // 2
    devices = blk_count * head_count
    tok = piece * seqs
    capacity = max(2, 5 * tok * top_count // (4 * experts))
    rows = -(-capacity // 32) * 32
    items = seqs * heads_here
    share = blk_count // items
    scale = 1.0 / math.sqrt(HEAD_DIM)
    everyone = ("blk", "head")

    def own_rows(values):
        return values.transpose(1, 0, 2).reshape(tok, values.shape[2])

    def out_rows(values):
        return values.reshape(seqs, piece, width).transpose(1, 0, 2)

    expert = (blk_index * head_count + head_index) // 2
    all_routes = lax.all_gather(own_rows(routes), everyone, axis=0, tiled=False)
    all_gates = lax.all_gather(own_rows(gate_weights), everyone, axis=0, tiled=False)
    named = all_routes == expert
    hit = jnp.any(named, axis=-1)
    gates = jnp.sum(jnp.where(named, all_gates, 0.0), axis=-1)[:, None, :]
    before = jnp.triu(jnp.ones((tok, tok), BF16), 1)
    places = jnp.dot(hit.astype(BF16), before, preferred_element_type=F32).astype(jnp.int32)
    slots = jnp.where(hit, places, -1)[:, None, :]

    hidden_f = own_rows(hidden_in).astype(F32)
    grad_y_b = own_rows(cotangent)
    grad_y = grad_y_b.astype(F32)

    inv_one = inverse_rms(hidden_f)
    normed = (hidden_f * inv_one * attn_gain).astype(BF16)
    group = lax.all_gather(normed, "head", axis=0, tiled=True)
    query_cols = lax.all_gather(w_query, "blk", axis=0, tiled=True)
    key_cols = lax.all_gather(w_key, "blk", axis=0, tiled=True)
    value_cols = lax.all_gather(w_value, "blk", axis=0, tiled=True)
    out_w = lax.all_gather(w_out, "blk", axis=1, tiled=True)
    all_cots = lax.all_gather(grad_y_b, everyone, axis=0, tiled=False)

    query_raw = mm(group, query_cols)
    key_raw = mm(group, key_cols)
    value_raw = mm(group, value_cols)
    square_sums = lax.psum(
        jnp.stack([jnp.sum(query_raw * query_raw, -1), jnp.sum(key_raw * key_raw, -1)]), "head"
    )
    inv_query = lax.rsqrt(square_sums[0][:, None] / width + EPSILON)
    inv_key = lax.rsqrt(square_sums[1][:, None] / width + EPSILON)
    gain_query = lax.dynamic_slice_in_dim(query_gain, head_index * columns, columns)
    gain_key = lax.dynamic_slice_in_dim(key_gain, head_index * columns, columns)
    query_n = (query_raw * inv_query * gain_query).astype(BF16)
    key_n = (key_raw * inv_key * gain_key).astype(BF16)
    value_n = value_raw.astype(BF16)

    def to_items(values):
        parts = values.reshape(head_count, seqs, piece, heads_here, HEAD_DIM)
        parts = parts.transpose(1, 3, 0, 2, 4).reshape(items, span, HEAD_DIM)
        return jnp.repeat(parts, share, axis=0) if share > 1 else parts

    def from_items(values):
        if share > 1:
            values = values.reshape(items, share, span, HEAD_DIM).astype(F32).sum(1)
        parts = values.reshape(seqs, heads_here, head_count, piece, HEAD_DIM)
        return parts.transpose(2, 0, 3, 1, 4).reshape(head_count * tok, columns)

    def swap(values):
        return lax.all_to_all(values, "blk", split_axis=0, concat_axis=0, tiled=True)

    item = blk_index // share
    own = (blk_index % share).reshape(1).astype(jnp.int32)
    starts = lax.dynamic_index_in_dim(block_starts, item // heads_here, 0, keepdims=False)
    qkv = swap(jnp.stack([to_items(query_n), to_items(key_n), to_items(value_n)], axis=1))
    qkv = qkv.reshape(blk_count, 3, per, BLOCK, HEAD_DIM)
    heads_out, heads_out_t, log_total = attend_forward(starts, own, qkv, scale, share)
    attended = from_items(swap(heads_out.reshape(blk_count, span, HEAD_DIM))).astype(BF16)
    branch = lax.psum_scatter(
        mm(attended, out_w).astype(BF16), "head", scatter_dimension=0, tiled=True
    ).astype(F32)
    middle = hidden_f + branch
    inv_two = inverse_rms(middle)
    normed_two = (middle * inv_two * ffn_gain).astype(BF16)

    all_tokens = lax.all_gather(normed_two, everyone, axis=0, tiled=False)
    step_blocks = 2
    moe_parts, dx_parts, xr, er, hid, dgp, dup = expert_rows(
        all_tokens, all_cots, slots, gates, w_gate[0], w_up[0], w_down[0], rows, step_blocks
    )

    def give_back(parts):
        parts = parts.reshape(devices * tok, width)
        parts = lax.psum_scatter(parts, "blk", scatter_dimension=0, tiled=True)
        return lax.psum_scatter(parts, "head", scatter_dimension=0, tiled=True)

    grad_normed_two = give_back(dx_parts).astype(F32)
    expert_sum = give_back(moe_parts).astype(F32)

    xr, er = xr.reshape(-1, width), er.reshape(-1, width)
    hid, dgp, dup = [v.reshape(-1, v.shape[-1]) for v in (hid, dgp, dup)]
    grad_down = mm(hid, er, TN)[None]
    grad_gate = mm(xr, dgp, TN)[None]
    grad_up = mm(xr, dup, TN)[None]

    result = middle + expert_sum
    gained_two = grad_normed_two * ffn_gain
    ffn_gain_part = jnp.sum(grad_normed_two * middle * inv_two, 0)
    grad_middle = (
        grad_y
        + inv_two * gained_two
        - middle * inv_two * inv_two * inv_two * jnp.mean(gained_two * middle, -1, keepdims=True)
    )
    grad_branch = grad_middle.astype(BF16)
    grad_group = lax.all_gather(grad_branch, "head", axis=0, tiled=True)
    grad_attended = mm(grad_group, out_w, NT).astype(BF16)
    out_part = mm(attended, grad_group, TN)
    grad_heads = swap(to_items(grad_attended)).reshape(blk_count * per, BLOCK, HEAD_DIM)
    grad_qkv = attend_backward(
        starts, own, qkv, grad_heads, heads_out_t, log_total, scale, share
    ).reshape(blk_count, 3, span, HEAD_DIM)
    grad_qkv = swap(grad_qkv)
    grad_query_n = rounded(from_items(grad_qkv[:, 0]))
    grad_key_n = rounded(from_items(grad_qkv[:, 1]))
    grad_value_b = from_items(grad_qkv[:, 2]).astype(BF16)
    gained_query = grad_query_n * gain_query
    gained_key = grad_key_n * gain_key
    row_sums = lax.psum(
        jnp.stack([jnp.sum(gained_query * query_raw, -1), jnp.sum(gained_key * key_raw, -1)]),
        "head",
    )
    grad_query_b = (
        inv_query * gained_query
        - query_raw * inv_query * inv_query * inv_query * row_sums[0][:, None] / width
    ).astype(BF16)
    grad_key_b = (
        inv_key * gained_key
        - key_raw * inv_key * inv_key * inv_key * row_sums[1][:, None] / width
    ).astype(BF16)
    query_gain_part = jnp.sum(grad_query_n * query_raw * inv_query, 0)
    key_gain_part = jnp.sum(grad_key_n * key_raw * inv_key, 0)
    total = (
        mm(grad_query_b, query_cols, NT)
        + mm(grad_key_b, key_cols, NT)
        + mm(grad_value_b, value_cols, NT)
    )
    grad_normed = rounded(
        lax.psum_scatter(total.astype(BF16), "head", scatter_dimension=0, tiled=True).astype(F32)
    )
    query_part = mm(group, grad_query_b, TN)
    key_part = mm(group, grad_key_b, TN)
    value_part = mm(group, grad_value_b, TN)
    gained_one = grad_normed * attn_gain
    attn_gain_part = jnp.sum(grad_normed * hidden_f * inv_one, 0)
    grad_hidden_in = (
        grad_middle
        + inv_one * gained_one
        - hidden_f
        * inv_one
        * inv_one
        * inv_one
        * jnp.mean(gained_one * hidden_f, -1, keepdims=True)
    )

    def over_blk(values, dim):
        return lax.psum_scatter(
            values.astype(BF16), "blk", scatter_dimension=dim, tiled=True
        ).astype(F32)

    grad_query = over_blk(query_part, 0)
    grad_key = over_blk(key_part, 0)
    grad_value = over_blk(value_part, 0)
    grad_out = over_blk(out_part, 1)
    zero_width = jnp.zeros((width,), F32)
    query_gain_full = lax.dynamic_update_slice_in_dim(
        zero_width, query_gain_part, head_index * columns, 0
    )
    key_gain_full = lax.dynamic_update_slice_in_dim(
        zero_width, key_gain_part, head_index * columns, 0
    )
    square_parts = jnp.stack(
        [jnp.sum(result * result), jnp.sum(branch * branch), jnp.sum(expert_sum * expert_sum)]
    )
    totals = lax.psum(
        (square_parts, attn_gain_part, ffn_gain_part, query_gain_full, key_gain_full),
        everyone,
    )
    entry_count = tok * width * devices
    stream_stats = jnp.sqrt(totals[0] / entry_count + EPSILON)
    return (
        out_rows(result.astype(BF16)),
        out_rows(grad_hidden_in.astype(BF16)),
        totals[1],
        grad_query,
        grad_key,
        grad_value,
        totals[3],
        totals[4],
        grad_out,
        totals[2],
        grad_gate,
        grad_up,
        grad_down,
        stream_stats,
    )


def solution(mesh):
    rows3 = P(("blk", "head"), None, None)
    placed = (
        rows3, P(), P("blk", "head"), P("blk", "head"), P("blk", "head"), P(), P(),
        P("head", "blk"), P(), rows3, rows3, rows3, rows3, rows3, P(), rows3,
    )
    return jax.shard_map(
        local,
        mesh=mesh,
        in_specs=placed,
        out_specs=(
            rows3, rows3, P(), P("blk", "head"), P("blk", "head"), P("blk", "head"), P(), P(),
            P("head", "blk"), P(), rows3, rows3, rows3, P(),
        ),
        check_vma=False,
    )
```

time: 3110 us -> 2170 us (0.70)
  waiting for transfers between devices: 1970 us -> 1420 us
  local copies, waits for them, and re-layouts: 372 us -> 49.1 us
  matrix products: 433 us -> 125 us
  blocking collectives: 60.5 us -> 278 us
  Pallas kernels: 0 us -> 195 us
  other arithmetic: 210 us -> 48.1 us
    all_to_all x4 -> x2, waiting for transfers between devices: 1330 us -> 172 us  [swap(): lax.all_to_all(values, 'blk', split_axis=0, concat_axis=0, tiled=True)]
    reduce_scatter x8 -> x10, waiting for transfers between devices: 322 us -> 876 us  [the longest x2 649 us: give_back(): parts = lax.psum_scatter(parts, 'blk', scatter_dimension=0, tiled=True)]
    dot_general x77 -> x16, matrix products: 433 us -> 125 us  [the longest x15 125 us: mm(): return lax.dot_general(left, right, dims, preferred_element_type=F32)]
    pallas_call x0 -> x3, Pallas kernels: none -> 195 us  [the longest x1 108 us: expert_rows(): pl.pallas_call(kernel, grid=(steps,), in_specs=[per_step(step_blocks, tok...]
    all_gather x0 -> x2, blocking collectives: none -> 138 us  [the longest x1 70.7 us: local(): all_routes = lax.all_gather(own_rows(routes), everyone, axis=0, tiled=False)]
    gather x2 -> x0, local copies, waits for them, and re-layouts: 102 us -> none  [the longest x1 51 us: local(): grad_pairs[flat_routes, slots].reshape(tok_rows, top_count, width)]
    unnamed x133 -> x62, local copies, waits for them, and re-layouts: 90.6 us -> 8.2 us
    reduce_sum x42 -> x5, other arithmetic: 91.5 us -> 10.5 us  [the longest x1 5.11 us: local(): ffn_gain_part = jnp.sum(grad_normed_two * middle * inv_two, 0)]
  transfers between devices with their start and end apart: 20 -> 20, of which waited for: 16 -> 16; matrix products, arithmetic and copies ran while one was open for 21% -> 8% of each run, Pallas kernels for 0% -> 2%
where the time goes in v1:
time: 2170 us; the launch traced here: 2160 us
  waiting for transfers between devices  1420 us (65%)
  blocking collectives  278 us (13%)
  Pallas kernels  195 us (9%)
  matrix products  125 us (6%)
  local copies, waits for them, and re-layouts  49.1 us (2%)
  other arithmetic  48.1 us (2%)
  starting transfers between devices  30.8 us (1%)
    reduce_scatter x2, waiting for transfers between devices, give_back(): parts = lax.psum_scatter(parts, 'blk', scatter_dimension=0, tiled=True)  649 us
    all_gather x1, waiting for transfers between devices, local(): all_tokens = lax.all_gather(normed_two, everyone, axis=0, tiled=False)  197 us
    all_to_all x2, waiting for transfers between devices, swap(): lax.all_to_all(values, 'blk', split_axis=0, concat_axis=0, tiled=True)  172 us
    dot_general x15, matrix products, mm(): return lax.dot_general(left, right, dims, preferred_element_type=F32)  125 us
    reduce_scatter x2, waiting for transfers between devices, give_back(): return lax.psum_scatter(parts, 'head', scatter_dimension=0, tiled=True)  110 us
    pallas_call x1, Pallas kernels, expert_rows(): pl.pallas_call(kernel, grid=(steps,), in_specs=[per_step(step_blocks, tok...  108 us
    all_to_all x2, blocking collectives, swap(): lax.all_to_all(values, 'blk', split_axis=0, concat_axis=0, tiled=True)  80.1 us
    all_gather x1, blocking collectives, local(): all_routes = lax.all_gather(own_rows(routes), everyone, axis=0, tiled=False)  70.7 us
  transfers between devices with their start and end apart: 20, of which 16 were waited for; matrix products, arithmetic and copies ran while one was open for 8% of the time, Pallas kernels for 2%

profile of v1, /device:TPU:0, one launch (start us, length us, event | category | flops | bytes accessed | tf_op | source)
XLA Modules:
  0.0 2159.0 jit_solution(3425851643482398527)
XLA Ops:
  8.8 2.4 convert_bitcast_fusion
  17.9 24.4 %all-gather.12.cloned.1.call-done = bf16[2048,512]{1,0:T(8,128)(2,1)} async-done(((bf16[256,512]{1,0:T(8,128)(2,1)}), bf16[2048,512]{1,0:T(8,128)(2,1)}) %all-gather.12.cloned.1.call-update) | async-done | bytes 2097168 | tf_op jit(solution)/shard_map/all_gather | solution.py:332
  42.3 54.6 %all-gather.10.cloned.1.call-done = bf16[1024,2048]{1,0:T(8,128)(2,1)} async-done(((bf16[256,2048]{1,0:T(8,128)(2,1)}), bf16[1024,2048]{1,0:T(8,128)(2,1)}) %all-gather.10.cloned.1.call-update) | async-done | bytes 4194320 | tf_op jit(solution)/shard_map/all_gather | solution.py:331
  96.9 6.6 multiply_reduce_fusion.3
  103.5 24.2 %all-gather.14.cloned.1.call-done = bf16[2048,512]{1,0:T(8,128)(2,1)} async-done(((bf16[256,512]{1,0:T(8,128)(2,1)}), bf16[2048,512]{1,0:T(8,128)(2,1)}) %all-gather.14.cloned.1.call-update) | async-done | bytes 2097168 | tf_op jit(solution)/shard_map/all_gather | solution.py:333
  127.7 6.6 multiply_reduce_fusion.2
  134.3 10.2 psum.49
  144.5 2.8 multiply_convert_fusion.2
  149.1 2.0 copy.83
  151.1 2.8 multiply_convert_fusion.1
  155.7 2.0 copy.84
  157.8 6.2 convolution_convert_fusion.6
  166.8 2.0 pad_maximum_fusion
  168.8 4.5 all-to-all-start
  174.5 87.2 %all-to-all-done = bf16[8,3,512,128]{3,2,1,0:T(8,128)(2,1)} async-done(((bf16[8,3,512,128]{3,2,1,0:T(8,128)(2,1)}), bf16[8,3,512,128]{3,2,1,0:T(8,128)(2,1)}, u32[]{:S(2)}, u32[]{:S(2)}) %all-to-all-start) | async-done | bytes 3145760 | tf_op jit(solution)/shard_map/all_to_all | solution.py:364
  261.7 41.0 %attend_forward.1 = (bf16[16,256,128]{2,1,0:T(8,128)(2,1)}, f32[16,128,256]{2,1,0:T(8,128)}, f32[16,1,256]{2,1,0:T(1,128)}) custom-call(s32[16]{0:T(128)} %dynamic-slice_bitcast_fusion.starts_ref, s32[1]{0:T(128)} %constant.81.clone.1.own_ref, bf16[8,3,2,256,128]{4,3,2,1,0:T(8,128)(2,1)} %bitcast.15.qkv_ref), custom_call_target="tpu_custom_call" | custom-call | tf_op jit(solution)/shard_map/attend_forward/pallas_call | solution.py:90
  302.7 49.0 %all_to_all.20 = bf16[8,512,128]{2,1,0:T(8,128)(2,1)S(1)} all-to-all(bf16[8,512,128]{2,1,0:T(8,128)(2,1)} %bitcast.172), channel_id=1, replica_groups=mesh['head'=4,'blk'=8] {'blk'}, dimensions={0} | all-to-all | bytes 2097152 | tf_op jit(solution)/shard_map/all_to_all | solution.py:364
  352.5 6.3 convolution_convert_fusion
  361.5 56.8 %reduce-scatter.11.cloned.1.call-done = bf16[256,2048]{1,0:T(8,128)(2,1)} async-done(((bf16[1024,2048]{1,0:T(8,128)(2,1)}), bf16[256,2048]{1,0:T(8,128)(2,1)}) %reduce-scatter.11.cloned.1.call-update) | async-done | bytes 1048592 | tf_op jit(solution)/shard_map/reduce_scatter | solution.py:373
  418.3 2.7 multiply_reduce_fusion.1
  423.6 70.7 %all_gather.41 = s32[32,256,8]{1,2,0:T(8,128)S(1)} all-gather(s32[1,256,8]{1,2,0:T(8,128)S(1)} %bitcast.186), channel_id=1, replica_groups=mesh['head'=4,'blk'=8] {'blk','head'}, dimensions={0}, use_global_device_ids=true | all-gather | bytes 270336 | tf_op jit(solution)/shard_map/all_gather | solution.py:316
  494.3 67.7 %all_gather.42 = f32[32,256,8]{1,2,0:T(8,128)S(1)} all-gather(f32[1,256,8]{1,2,0:T(8,128)S(1)} %bitcast.187), channel_id=1, replica_groups=mesh['head'=4,'blk'=8] {'blk','head'}, dimensions={0}, use_global_device_ids=true | all-gather | bytes 270336 | tf_op jit(solution)/shard_map/all_gather | solution.py:317
  563.6 12.6 all-gather.20.cloned.1.call-done.cot_ref
  576.2 197.0 %all-gather.24.cloned.1.call-done = bf16[8192,2048]{1,0:T(8,128)(2,1)} async-done(((bf16[256,2048]{1,0:T(8,128)(2,1)}), bf16[8192,2048]{1,0:T(8,128)(2,1)}) %all-gather.24.cloned.1.call-update) | async-done | bytes 33554448 | tf_op jit(solution)/shard_map/all_gather | solution.py:380
  773.2 107.9 %expert_rows.1 = (bf16[32,256,2048]{2,1,0:T(8,128)(2,1)}, bf16[32,256,2048]{2,1,0:T(8,128)(2,1)}, bf16[16,320,2048]{2,1,0:T(8,128)(2,1)}, bf16[16,320,2048]{2,1,...) custom-call(bf16[32,256,2048]{2,1,0:T(8,128)(2,1)} %bitcast.143, ...), custom_call_target="tpu_custom_call" | custom-call | tf_op jit(solution)/shard_map/expert_rows/pallas_call | solution.py:236
  881.9 323.1 %reduce-scatter.13.cloned.1.call-done = bf16[1024,2048]{1,0:T(8,128)(2,1)} async-done(((bf16[8192,2048]{1,0:T(8,128)(2,1)}), bf16[1024,2048]{1,0:T(8,128)(2,1)}) %reduce-scatter.13.cloned.1.call-update) | async-done | bytes 4194320 | tf_op jit(solution)/shard_map/reduce_scatter | solution.py:388
  1205.0 326.2 %reduce-scatter.17.cloned.1.call-done = bf16[1024,2048]{1,0:T(8,128)(2,1)} async-done(((bf16[8192,2048]{1,0:T(8,128)(2,1)}), bf16[1024,2048]{1,0:T(8,128)(2,1)}) %reduce-scatter.17.cloned.1.call-update) | async-done | bytes 4194320 | tf_op jit(solution)/shard_map/reduce_scatter | solution.py:388
  1531.3 54.3 %reduce-scatter.15.cloned.1.call-done = bf16[256,2048]{1,0:T(8,128)(2,1)} async-done(((bf16[1024,2048]{1,0:T(8,128)(2,1)}), bf16[256,2048]{1,0:T(8,128)(2,1)}) %reduce-scatter.15.cloned.1.call-update) | async-done | bytes 1048592 | tf_op jit(solution)/shard_map/reduce_scatter | solution.py:389
  1585.6 55.5 %reduce-scatter.19.cloned.1.call-done = bf16[256,2048]{1,0:T(8,128)(2,1)} async-done(((bf16[1024,2048]{1,0:T(8,128)(2,1)}), bf16[256,2048]{1,0:T(8,128)(2,1)}) %reduce-scatter.19.cloned.1.call-update) | async-done | bytes 1048592 | tf_op jit(solution)/shard_map/reduce_scatter | solution.py:389
  1641.1 5.1 fusion.24
  1648.1 52.8 %all-gather.22.cloned.1.call-done = bf16[1024,2048]{1,0:T(8,128)(2,1)} async-done(((bf16[256,2048]{1,0:T(8,128)(2,1)}), bf16[1024,2048]{1,0:T(8,128)(2,1)}) %all-gather.22.cloned.1.call-update) | async-done | bytes 4194320 | tf_op jit(solution)/shard_map/all_gather | solution.py:409
  1701.0 6.2 convolution_convert_fusion.5
  1707.2 2.1 reshape.175
  1710.8 31.1 %all_to_all.21 = bf16[8,512,128]{2,1,0:T(8,128)(2,1)} all-to-all(bf16[8,512,128]{2,1,0:T(8,128)(2,1)S(1)} %bitcast.154), channel_id=1, replica_groups=mesh['head'=4,'blk'=8] {'blk'}, dimensions={0} | all-to-all | bytes 2097152 | tf_op jit(solution)/shard_map/all_to_all | solution.py:364
  1741.9 46.0 %attend_backward.1 = bf16[8,3,2,256,128]{4,3,2,1,0:T(8,128)(2,1)} custom-call(s32[16]{0:T(128)} %dynamic-slice_bitcast_fusion.starts_ref, s32[1]{0:T(128)} %constant.81.clone.1.own_ref, bf16[8,3,2,256,128]{4,3,2,1,0:T(8,128)(2,1)} %bitcast.15.qkv_ref, bf16[16,256,128]{2,1,0:T(8,128)(2,1)} %bitcast.148, f32[16,128,256]{2,1,0:T(8,128)} %get-tuple-element.27.out_t_ref, ...), custom_call_target="tpu_custom_call" | custom-call | tf_op jit(solution)/shard_map/attend_backward/pallas_call | solution.py:164
  1787.9 25.0 %all-to-all-start.3 = ((bf16[8,3,512,128]{3,2,1,0:T(8,128)(2,1)}), bf16[8,3,512,128]{3,2,1,0:T(8,128)(2,1)}, u32[]{:S(2)}, u32[]{:S(2)}) async-start(bf16[8,3,512,128]{3,2,1,0:T(8,128)(2,1)} %bitcast.145), calls=%async_computation.8 | async-start | bytes 6291456 | tf_op jit(solution)/shard_map/all_to_all | solution.py:364
  1813.4 6.3 convolution_convert_fusion.1
  1819.7 84.5 %all-to-all-done.3 = bf16[8,3,512,128]{3,2,1,0:T(8,128)(2,1)} async-done(((bf16[8,3,512,128]{3,2,1,0:T(8,128)(2,1)}), bf16[8,3,512,128]{3,2,1,0:T(8,128)(2,1)}, u32[]{:S(2)}, u32[]{:S(2)}) %all-to-all-start.3) | async-done | bytes 3145760 | tf_op jit(solution)/shard_map/all_to_all | solution.py:364
  1904.3 3.6 fusion.53
  1907.9 3.7 copy.90
  1911.6 2.6 reshape.179
  1914.2 3.7 copy.91
  1917.8 2.6 reshape.180
  1920.4 2.7 fusion.26
  1924.0 9.1 psum.50
  1933.1 2.7 fusion.14
  1936.8 3.8 convolution_convert_fusion.3
  1940.7 2.7 fusion.16
  1944.4 3.8 convolution_convert_fusion.4
  1948.4 2.0 copy.93
  1951.4 6.0 convolution_convert_fusion.2
  1957.5 4.5 fusion.56
  1962.0 5.6 fusion.55
  1967.7 8.2 add_convert_fusion
  1975.9 18.3 convolution_bitcast_fusion
  1994.2 18.2 convolution_bitcast_fusion.1
  2012.3 18.3 convolution_bitcast_fusion.2
  2030.7 2.0 copy.118
  2032.7 2.0 pad_maximum_fusion.3
  2040.6 7.4 reduce-scatter.27.cloned.1.call-done
  2049.8 52.7 %reduce-scatter.21.cloned.1.call-done = bf16[256,2048]{1,0:T(8,128)(2,1)} async-done(((bf16[1024,2048]{1,0:T(8,128)(2,1)}), bf16[256,2048]{1,0:T(8,128)(2,1)}) %reduce-scatter.21.cloned.1.call-update) | async-done | bytes 1048592 | tf_op jit(solution)/shard_map/reduce_scatter | solution.py:442
  2104.4 40.5 %all-reduce = (f32[2048]{0:T(1024)}, f32[2048]{0:T(1024)}, f32[2048]{0:T(1024)}, f32[2048]{0:T(1024)}, f32[3]{0:T(128)S(1)}) all-reduce(f32[2048]{0:T(1024)S(1)} %get-tuple-element.40, f32[2048]{0:T(1024)S(1)} %dynamic_update_slice.6, f32[2048]{0:T(1024)S(1)} %dynamic_update_slice.7, ...), channel_id=1, replica_groups=mesh['head'=4,'blk'=8] {'blk','head'}, use_global_device_ids=true, to_apply=%region_19.20 | all-reduce | flops 8195 | bytes 65560 | tf_op jit(solution)/shard_map/psum | solution.py:478
  2145.4 4.0 fusion.10
  2149.3 2.0 copy.117
  (141 shorter events, 41.5 us)
Async XLA Ops:
  8.0 165.9 %copy-start = (s32[2,16]{1,0:T(2,128)S(1)}, s32[2,16]{1,0:T(2,128)}, u32[]{:S(2)}) copy-start(s32[2,16]{1,0:T(2,128)} %param.30) | copy-start | bytes 388
  8.0 34.3 %all-gather.12.cloned.1.call-start = ((), (), s32[]{:S(2)}) async-start(), calls=%async_computation.15 | async-start | bytes 2359296 | tf_op jit(solution)/shard_map/all_gather | solution.py:332
  8.8 88.2 %all-gather.10.cloned.1.call-start = ((), (), s32[]{:S(2)}) async-start(), calls=%async_computation.14 | async-start | bytes 5242880 | tf_op jit(solution)/shard_map/all_gather | solution.py:331
  11.3 1.2 copy-start.8
  11.3 2.5 copy-start.21
  13.7 1.3 copy-start.23
  15.0 112.7 %all-gather.14.cloned.1.call-start = ((), (), s32[]{:S(2)}) async-start(), calls=%async_computation.16 | async-start | bytes 2359296 | tf_op jit(solution)/shard_map/all_gather | solution.py:333
  15.8 142.0 %all-gather.16.cloned.1.call-start = ((), (), s32[]{:S(2)}) async-start(), calls=%async_computation.17 | async-start | bytes 2359296 | tf_op jit(solution)/shard_map/all_gather | solution.py:334
  165.3 1.2 copy-start.12
  165.3 1.5 copy-start.13
  168.8 92.9 %all-to-all-start = ((bf16[8,3,512,128]{3,2,1,0:T(8,128)(2,1)}), bf16[8,3,512,128]{3,2,1,0:T(8,128)(2,1)}, u32[]{:S(2)}, u32[]{:S(2)}) async-start(bf16[8,3,512,128]{3,2,1,0:T(8,128)(2,1)} %pad_maximum_fusion), calls=%async_computation | async-start | bytes 6291456 | tf_op jit(solution)/shard_map/all_to_all | solution.py:364
  173.3 179.2 %all-gather.18.cloned.1.call-start = ((), (), s32[]{:S(2)}) async-start(), calls=%async_computation.18 | async-start | bytes 2359296 | tf_op jit(solution)/shard_map/all_gather | solution.py:335
  173.9 244.4 %reduce-scatter.11.cloned.1.call-start = ((), (), s32[]{:S(2)}) async-start(), calls=%async_computation.19 | async-start | bytes 5242880 | tf_op jit(solution)/shard_map/reduce_scatter | solution.py:373
  352.5 6.3 copy-start.16
  358.9 1.2 copy-start.15
  358.9 217.3 %all-gather.20.cloned.1.call-start = ((), (), s32[]{:S(2)}) async-start(), calls=%async_computation.20 | async-start | bytes 34603008 | tf_op jit(solution)/shard_map/all_gather | solution.py:336
  361.4 60.9 %copy-start.20 = (f32[2048]{0:T(1024)S(1)}, f32[2048]{0:T(1024)}, u32[]{:S(2)}) copy-start(f32[2048]{0:T(1024)} %param.24) | copy-start | bytes 24580
  361.4 411.7 %all-gather.24.cloned.1.call-start = ((), (), s32[]{:S(2)}) async-start(), calls=%async_computation.31 | async-start | bytes 34603008 | tf_op jit(solution)/shard_map/all_gather | solution.py:380
  421.0 1.3 copy-start.2
  422.3 1.3 copy-start.25
  422.3 72.0 %copy-start.26 = (f32[128,2,8]{0,2,1:T(8,128)S(1)}, f32[128,2,8]{0,2,1:T(8,128)}, u32[]{:S(2)}) copy-start(f32[128,2,8]{0,2,1:T(8,128)} %param.29) | copy-start | bytes 24580
  423.5 781.4 %reduce-scatter.13.cloned.1.call-start = ((), (), s32[]{:S(2)}) async-start(), calls=%async_computation.21 | async-start | bytes 37748736 | tf_op jit(solution)/shard_map/reduce_scatter | solution.py:388
  881.1 650.2 %reduce-scatter.17.cloned.1.call-start = ((), (), s32[]{:S(2)}) async-start(), calls=%async_computation.23 | async-start | bytes 37748736 | tf_op jit(solution)/shard_map/reduce_scatter | solution.py:388
  881.8 703.8 %reduce-scatter.15.cloned.1.call-start = ((), (), s32[]{:S(2)}) async-start(), calls=%async_computation.22 | async-start | bytes 5242880 | tf_op jit(solution)/shard_map/reduce_scatter | solution.py:389
  1205.0 436.2 %reduce-scatter.19.cloned.1.call-start = ((), (), s32[]{:S(2)}) async-start(), calls=%async_computation.24 | async-start | bytes 5242880 | tf_op jit(solution)/shard_map/reduce_scatter | solution.py:389
  1531.3 115.0 %copy-start.5 = (bf16[128,2,2048]{2,0,1:T(8,128)(2,1)S(1)}, bf16[128,2,2048]{2,0,1:T(8,128)(2,1)}, u32[]{:S(2)}) copy-start(bf16[128,2,2048]{2,0,1:T(8,128)(2,1)} %copy.87) | copy-start | bytes 3145732
  1531.3 169.7 %all-gather.22.cloned.1.call-start = ((), (), s32[]{:S(2)}) async-start(), calls=%async_computation.25 | async-start | bytes 5242880 | tf_op jit(solution)/shard_map/all_gather | solution.py:409
  1641.1 5.1 copy-start.3
  1641.1 5.1 copy-start.7
  1787.9 116.3 %all-to-all-start.3 = ((bf16[8,3,512,128]{3,2,1,0:T(8,128)(2,1)}), bf16[8,3,512,128]{3,2,1,0:T(8,128)(2,1)}, u32[]{:S(2)}, u32[]{:S(2)}) async-start(bf16[8,3,512,128]{3,2,1,0:T(8,128)(2,1)} %bitcast.145), calls=%async_computation.8 | async-start | bytes 6291456 | tf_op jit(solution)/shard_map/all_to_all | solution.py:364
  1813.0 221.8 %reduce-scatter.29.cloned.1.call-start = ((), (), s32[]{:S(2)}) async-start(), calls=%async_computation.30 | async-start | bytes 2359296 | tf_op jit(solution)/shard_map/reduce_scatter | solution.py:460
  1819.7 217.3 %reduce-scatter.25.cloned.1.call-start = ((), (), s32[]{:S(2)}) async-start(), calls=%async_computation.28 | async-start | bytes 2359296 | tf_op jit(solution)/shard_map/reduce_scatter | solution.py:460
  1920.4 2.7 copy-start.4
  1920.4 2.8 copy-start.6
  1933.1 3.7 copy-start.27
  1935.8 1.0 copy-start.17
  1940.6 98.2 %reduce-scatter.23.cloned.1.call-start = ((), (), s32[]{:S(2)}) async-start(), calls=%async_computation.27 | async-start | bytes 2359296 | tf_op jit(solution)/shard_map/reduce_scatter | solution.py:460
  1940.7 3.7 copy-start.28
  1943.4 1.0 copy-start.18
  1948.2 99.8 %reduce-scatter.27.cloned.1.call-start = ((), (), s32[]{:S(2)}) async-start(), calls=%async_computation.29 | async-start | bytes 2359296 | tf_op jit(solution)/shard_map/reduce_scatter | solution.py:460
  1950.5 1.0 copy-start.9
  1957.4 145.0 %reduce-scatter.21.cloned.1.call-start = ((), (), s32[]{:S(2)}) async-start(), calls=%async_computation.26 | async-start | bytes 5242880 | tf_op jit(solution)/shard_map/reduce_scatter | solution.py:442
  1957.5 4.5 copy-start.19
  1957.5 4.5 copy-start.29
  1962.0 5.6 copy-start.10
  1962.0 5.6 copy-start.14
  2012.3 18.3 copy-start.11
  2032.7 69.8 %copy-start.22 = (f32[2048]{0:T(1024)S(1)}, f32[2048]{0:T(1024)}, u32[]{:S(2)}) copy-start(f32[2048]{0:T(1024)} %param.17) | copy-start | bytes 24580
  2032.7 69.8 %copy-start.24 = (f32[128,2]{0,1:T(2,128)S(1)}, f32[128,2]{0,1:T(2,128)}, u32[]{:S(2)}) copy-start(f32[128,2]{0,1:T(2,128)} %copy-done.23) | copy-start | bytes 3076
  2145.4 6.0 copy-start.1
Sparse Core Ops, SparseCore 0:
  10.5 31.7 all-gather.11
  44.7 52.1 all-gather.9
  98.5 29.0 all-gather.13
  129.1 28.5 all-gather.15
  175.4 74.1 all-gather.17
  359.0 59.2 reduce-scatter.10
  881.2 323.6 reduce-scatter.12
  1207.3 323.8 reduce-scatter.16
  1534.5 51.0 reduce-scatter.14
  1588.4 52.6 reduce-scatter.18
  1648.3 52.6 all-gather.21
  1819.8 59.8 reduce-scatter.28
  1940.7 33.6 reduce-scatter.24
  1976.7 34.4 reduce-scatter.22
  2013.4 34.5 reduce-scatter.26
  2051.1 51.3 reduce-scatter.20
Sparse Core Ops, SparseCore 1:
  363.2 212.9 all-gather.19
  579.9 193.2 all-gather.23

commit v2 on v1

v2 whole, which is shorter than its diff:
```python
import functools
import math

import jax
import jax.numpy as jnp
from jax import lax
from jax.experimental import pallas as pl
from jax.experimental.pallas import tpu as pltpu
from jax.sharding import PartitionSpec as P

HEAD_DIM = 128
BLOCK = 256
EPSILON = 1e-06
F32 = jnp.float32
BF16 = jnp.bfloat16
VMEM_BYTES = 58 * 1024 * 1024

NN = (((1,), (0,)), ((), ()))
NT = (((1,), (1,)), ((), ()))
TN = (((0,), (0,)), ((), ()))


def mm(left, right, dims=NN):
    return lax.dot_general(left, right, dims, preferred_element_type=F32)


def rounded(values):
    return lax.optimization_barrier(values.astype(BF16)).astype(F32)


def inverse_rms(values):
    return lax.rsqrt(jnp.mean(values * values, axis=-1, keepdims=True) + EPSILON)


def nearest(here, rank, count):
    below = here
    above = count - 1 - here
    swing = jnp.where(rank % 2 == 1, here - (rank + 1) // 2, here + rank // 2)
    far = jnp.where(below < above, rank, count - 1 - rank)
    return jnp.where(rank <= 2 * jnp.minimum(below, above), swing, far)


def greet(peers):
    barrier = pltpu.get_barrier_semaphore()
    count = 0
    for device, condition in peers:

        def signal(device=device):
            pl.semaphore_signal(
                barrier, inc=1, device_id=device, device_id_type=pl.DeviceIdType.MESH
            )

        if condition is None:
            signal()
            count = count + 1
        else:
            pl.when(condition)(signal)
            count = count + jnp.where(condition, 1, 0)
    pl.semaphore_wait(barrier, count)


class Relay:
    def __init__(self, arrays, nz, ny, send_sem, recv_sem):
        self.arrays, self.nz, self.ny = arrays, nz, ny
        self.send_sem, self.recv_sem = send_sem, recv_sem
        head, blk = lax.axis_index("head"), lax.axis_index("blk")
        self.x, self.y = x, y = head % 2, head // 2
        self.core, self.z = core, z = blk % 2, blk // 2

        def device(z_at, y_at, core_at):
            return {"blk": z_at * 2 + core_at, "head": y_at * 2 + x}

        self.sibling = device(z, y, 1 - core)
        self.targets = [
            self.sibling, device(z, y + 1, core), device(z, y - 1, core),
            device(z + 1, y, core), device(z - 1, y, core),
        ]
        self.present = [None, y < ny - 1, y > 0, z < nz - 1, z > 0]
        self.pieces = []
        for n, (own, everything, parts) in enumerate(arrays):
            rows = own.shape[0] // parts
            for part in range(parts):
                self.pieces.append((n, pl.ds(part * rows, rows)))

    @staticmethod
    def when(condition, work):
        if condition is None:
            work()
        else:
            pl.when(condition)(work)

    def peers(self):
        return list(zip(self.targets, self.present))

    def conditions(self, z_at, y_at):
        column = y_at == self.y
        there = self.present
        return [
            None, (y_at <= self.y) & there[1], (y_at >= self.y) & there[2],
            column & (z_at <= self.z) & there[3], column & (z_at >= self.z) & there[4],
        ]

    def copy(self, z_at, y_at, core_at, piece, way, own=False):
        n, here = self.pieces[piece]
        everything = self.arrays[n][1]
        place = everything.at[z_at, core_at, y_at, here]
        return pltpu.make_async_remote_copy(
            src_ref=self.arrays[n][0].at[here] if own else place,
            dst_ref=place,
            send_sem=self.send_sem.at[way, z_at * self.ny + y_at, piece],
            recv_sem=self.recv_sem.at[core_at, z_at * self.ny + y_at, piece],
            device_id=self.targets[way],
            device_id_type=pl.DeviceIdType.MESH,
        )

    def start(self):
        for piece in range(len(self.pieces)):
            for way in (3, 4, 1, 2, 0):
                self.when(self.present[way], lambda way=way, piece=piece: self.copy(
                    self.z, self.y, self.core, piece, way, own=True).start())

    def keep(self, stages, sems):
        loads = [
            pltpu.make_async_copy(own, stage, sems.at[n])
            for n, ((own, _, _), stage) in enumerate(zip(self.arrays, stages))
        ]
        for copy in loads:
            copy.start()
        for copy in loads:
            copy.wait()
        stores = [
            pltpu.make_async_copy(stage, everything.at[self.z, self.core, self.y], sems.at[n])
            for n, ((_, everything, _), stage) in enumerate(zip(self.arrays, stages))
        ]
        for copy in stores:
            copy.start()
        return stores

    def arrived(self, z_at, y_at, core_at):
        for piece in range(len(self.pieces)):
            self.copy(z_at, y_at, core_at, piece, 0).wait_recv()

    def pass_on(self, z_at, y_at):
        for piece in range(len(self.pieces)):
            self.copy(z_at, y_at, self.core, piece, 0).wait_recv()
            for way, condition in enumerate(self.conditions(z_at, y_at)):
                self.when(condition, lambda way=way, piece=piece: self.copy(
                    z_at, y_at, self.core, piece, way).start())

    def pass_on_z(self, away):
        pl.when(self.z - away >= 0)(lambda: self.pass_on(self.z - away, self.y))
        pl.when(self.z + away < self.nz)(lambda: self.pass_on(self.z + away, self.y))

    def drain(self):
        def one(index, carry):
            z_at, y_at = index // self.ny, index % self.ny
            for way, condition in enumerate(self.conditions(z_at, y_at)):
                for piece in range(len(self.pieces)):
                    self.when(condition, lambda way=way, piece=piece: self.copy(
                        z_at, y_at, self.core, piece, way).wait_send())
            return carry

        lax.fori_loop(0, self.nz * self.ny, one, 0)


class Swap:
    def __init__(self, pairs, send_sem, recv_sem):
        head, blk = lax.axis_index("head"), lax.axis_index("blk")
        self.neighbour = {"blk": blk, "head": head + 1 - 2 * (head % 2)}
        self.copies = [
            pltpu.make_async_remote_copy(
                src_ref=source,
                dst_ref=target,
                send_sem=send_sem.at[n],
                recv_sem=recv_sem.at[n],
                device_id=self.neighbour,
                device_id_type=pl.DeviceIdType.MESH,
            )
            for n, (source, target) in enumerate(pairs)
        ]

    def peers(self):
        return [(self.neighbour, None)]

    def start(self):
        for copy in self.copies:
            copy.start()

    def wait(self):
        for copy in self.copies:
            copy.wait()


class Return:
    parts = 2

    @classmethod
    def scratch(cls, nz, tok, width):
        return [
            pltpu.VMEM((nz, tok, width), BF16),
            pltpu.VMEM((nz, tok, width), BF16),
            pltpu.VMEM((2, nz, tok, width), BF16),
            pltpu.SemaphoreType.DMA((nz, cls.parts)),
            pltpu.SemaphoreType.DMA((nz, cls.parts)),
            pltpu.SemaphoreType.DMA((nz, cls.parts)),
            pltpu.SemaphoreType.DMA((nz, cls.parts)),
            pltpu.SemaphoreType.DMA((2, nz, cls.parts)),
        ]

    def __init__(self, share_ref, out_ref, scratch):
        self.share_ref, self.out_ref = share_ref, out_ref
        (
            self.mine, self.from_y, self.from_z,
            self.mine_sem, self.y_send, self.y_recv, self.z_send, self.z_recv,
        ) = scratch
        self.nz, _, tok, _ = share_ref.shape
        self.piece = tok // self.parts
        self.step_rows = min(64, self.piece)
        head, blk = lax.axis_index("head"), lax.axis_index("blk")
        x, self.y, self.z = head % 2, head // 2, blk // 2
        self.beside = {"blk": blk, "head": (1 - self.y) * 2 + x}
        self.onward = [{"blk": blk + 2, "head": head}, {"blk": blk - 2, "head": head}]
        self.has = [self.z > 0, self.z < self.nz - 1]
        self.targets = [nearest(self.z, rank, self.nz) for rank in reversed(range(self.nz))]

    def peers(self):
        return [(self.beside, None), (self.onward[1], self.has[0]), (self.onward[0], self.has[1])]

    def cut(self, part):
        return pl.ds(part * self.piece, self.piece)

    def own_copy(self, target, part):
        return pltpu.make_async_copy(
            self.share_ref.at[target, self.y, self.cut(part)],
            self.mine.at[target, self.cut(part)],
            self.mine_sem.at[target, part],
        )

    def y_copy(self, target, part):
        return pltpu.make_async_remote_copy(
            src_ref=self.share_ref.at[target, 1 - self.y, self.cut(part)],
            dst_ref=self.from_y.at[target, self.cut(part)],
            send_sem=self.y_send.at[target, part],
            recv_sem=self.y_recv.at[target, part],
            device_id=self.beside,
            device_id_type=pl.DeviceIdType.MESH,
        )

    def z_copy(self, way, target, part):
        return pltpu.make_async_remote_copy(
            src_ref=self.mine.at[target, self.cut(part)],
            dst_ref=self.from_z.at[way, target, self.cut(part)],
            send_sem=self.z_send.at[target, part],
            recv_sem=self.z_recv.at[way, target, part],
            device_id=self.onward[way],
            device_id_type=pl.DeviceIdType.MESH,
        )

    def start(self):
        for target in self.targets:
            for part in range(self.parts):
                self.y_copy(target, part).start()
                self.own_copy(target, part).start()

    def add(self, target, part, ways, out=None):
        for r in range(part * self.piece, (part + 1) * self.piece, self.step_rows):
            here = pl.ds(r, self.step_rows)
            total = self.mine[target, here, :].astype(F32) + self.from_y[target, here, :].astype(F32)
            for way in ways:
                total = total + self.from_z[way, target, here, :].astype(F32)
            if out is None:
                self.mine[target, here, :] = total.astype(BF16)
            else:
                out[here, :] = total.astype(BF16)

    def send(self, turn):
        target = self.targets[turn]
        for part in range(self.parts):
            self.own_copy(target, part).wait()
            self.y_copy(target, part).wait_recv()
            for way in range(2):
                going = target > self.z if way == 0 else target < self.z

                @pl.when(going & self.has[way])
                def _(way=way, part=part):
                    self.z_copy(way, target, part).wait_recv()
                    self.add(target, part, (way,))

                @pl.when(going & jnp.logical_not(self.has[way]))
                def _(part=part):
                    self.add(target, part, ())

                @pl.when(going)
                def _(way=way, part=part):
                    self.z_copy(way, target, part).start()

    def finish(self):
        z, has = self.z, self.has
        for part in range(self.parts):
            self.own_copy(z, part).wait()
            self.y_copy(z, part).wait_recv()
            for way in range(2):
                pl.when(has[way])(lambda way=way, part=part: self.z_copy(way, z, part).wait_recv())
            for condition, ways in (
                (has[0] & has[1], (0, 1)),
                (has[0] & jnp.logical_not(has[1]), (0,)),
                (jnp.logical_not(has[0]) & has[1], (1,)),
            ):
                pl.when(condition)(
                    lambda ways=ways, part=part: self.add(z, part, ways, self.out_ref)
                )
        for target in self.targets:
            for part in range(self.parts):
                self.y_copy(target, part).wait_send()
        for target in self.targets[:-1]:
            for part in range(self.parts):
                self.z_copy(0, target, part).wait_send()


def attend_forward(bias, qkv, cots, table, swaps, nz, ny, scale, share, collective_id):
    src, _, per, block, dim = qkv.shape
    blocks = src * per
    parts = 2
    events = [blocks * 5 // 8, blocks * 7 // 8]

    count = len(swaps)

    def kernel(bias_ref, qkv_ref, cot_ref, table_ref, *refs):
        swap_in, refs = refs[:count], refs[count:]
        out_ref, out_t_ref, lse_ref, cots_ref, tables_ref, *refs = refs
        swap_out, refs = refs[:count], refs[count:]
        (
            vt_ref, cot_stage, table_stage, send_sem, recv_sem, own_sem, swap_send, swap_recv,
        ) = refs
        swap = Swap(list(zip(swap_in, swap_out)), swap_send, swap_recv)
        relay = Relay(
            [(cot_ref, cots_ref, parts), (table_ref, tables_ref, 1)], nz, ny, send_sem, recv_sem
        )
        greet(relay.peers() + swap.peers())
        relay.start()
        swap.start()
        kept = relay.keep((cot_stage, table_stage), own_sem)

        def flip(j, carry):
            vt_ref[j] = qkv_ref[j // per, 2, j % per].astype(F32).T.astype(BF16)
            return carry

        lax.fori_loop(0, blocks, flip, 0)
        own = lax.axis_index("blk") % share

        def query_block(step, carry):
            for n, event in enumerate(events):
                if n + 1 < nz:
                    pl.when(step == event)(lambda n=n: relay.pass_on_z(n + 1))

            def work():
                query = qkv_ref[step // per, 0, step % per]

                def body(j, carry):
                    top, total, acc = carry
                    scores = mm(qkv_ref[j // per, 1, j % per], query, NT) * scale
                    scores = scores + bias_ref[step * blocks + j]
                    new_top = jnp.maximum(top, jnp.max(scores, axis=0, keepdims=True))
                    weights = jnp.exp(scores - new_top)
                    shrink = jnp.exp(top - new_top)
                    total = total * shrink + jnp.sum(weights, axis=0, keepdims=True)
                    acc = acc * shrink + mm(vt_ref[j], weights.astype(BF16))
                    return new_top, total, acc

                top, total, acc = lax.fori_loop(
                    0,
                    step + 1,
                    body,
                    (
                        jnp.full((1, block), -1e30, F32),
                        jnp.zeros((1, block), F32),
                        jnp.zeros((dim, block), F32),
                    ),
                )
                result = acc / total
                out_t_ref[step] = result
                out_ref[step] = result.T.astype(BF16)
                lse_ref[step] = top + jnp.log(total)

            if share == 1:
                work()
            else:
                mine = step % share == own
                pl.when(mine)(work)

                @pl.when(jnp.logical_not(mine))
                def _():
                    out_t_ref[step] = jnp.zeros((dim, block), F32)
                    out_ref[step] = jnp.zeros((block, dim), BF16)
                    lse_ref[step] = jnp.zeros((1, block), F32)

            return carry

        lax.fori_loop(0, blocks, query_block, 0)
        for away in range(len(events) + 1, nz):
            relay.pass_on_z(away)
        for turn in range(1, ny):
            for rank in range(nz):
                relay.pass_on(nearest(relay.z, rank, nz), nearest(relay.y, turn, ny))

        def from_sibling(index, carry):
            relay.arrived(index // ny, index % ny, 1 - relay.core)
            return carry

        lax.fori_loop(0, nz * ny, from_sibling, 0)
        relay.drain()
        swap.wait()
        for copy in kept:
            copy.wait()

    anywhere = pl.BlockSpec(memory_space=pl.ANY)
    inside = pl.BlockSpec(memory_space=pltpu.VMEM)
    return pl.pallas_call(
        kernel,
        in_specs=[pl.BlockSpec(memory_space=pltpu.SMEM), inside, anywhere, anywhere]
        + [anywhere] * count,
        out_specs=[inside] * 3 + [anywhere] * (2 + count),
        out_shape=[
            jax.ShapeDtypeStruct((blocks, block, dim), BF16),
            jax.ShapeDtypeStruct((blocks, dim, block), F32),
            jax.ShapeDtypeStruct((blocks, 1, block), F32),
            jax.ShapeDtypeStruct((nz, 2, ny) + cots.shape, cots.dtype),
            jax.ShapeDtypeStruct((nz, 2, ny) + table.shape, table.dtype),
        ]
        + [jax.ShapeDtypeStruct(v.shape, v.dtype) for v in swaps],
        scratch_shapes=[
            pltpu.VMEM((blocks, dim, block), BF16),
            pltpu.VMEM(cots.shape, cots.dtype),
            pltpu.VMEM(table.shape, table.dtype),
            pltpu.SemaphoreType.DMA((5, nz * ny, parts + 1)),
            pltpu.SemaphoreType.DMA((2, nz * ny, parts + 1)),
            pltpu.SemaphoreType.DMA((2,)),
            pltpu.SemaphoreType.DMA((count,)),
            pltpu.SemaphoreType.DMA((count,)),
        ],
        compiler_params=pltpu.CompilerParams(
            collective_id=collective_id, has_side_effects=True, vmem_limit_bytes=VMEM_BYTES
        ),
        name="attend_forward",
    )(bias, qkv, cots, table, *swaps)


def attend_backward(bias, qkv, grad_out, out_t, lse, swaps, shares, scale, share, collective_id):
    src, _, per, block, dim = qkv.shape
    blocks = src * per
    count = len(swaps)
    events = [blocks * 9 // 16, blocks * 13 // 16]

    def kernel(bias_ref, qkv_ref, go_ref, out_t_ref, lse_ref, *refs):
        swap_in, refs = refs[:count], refs[count:]
        share_ref, refs = refs[: len(shares)], refs[len(shares) :]
        grad_ref, *refs = refs
        swap_out, refs = refs[:count], refs[count:]
        sum_ref, refs = refs[: len(shares)], refs[len(shares) :]
        dk_ref, dv_ref, swap_send, swap_recv, *refs = refs
        swap = Swap(list(zip(swap_in, swap_out)), swap_send, swap_recv)
        back = Return(share_ref[0], sum_ref[0], refs) if shares else None
        greet(swap.peers() + (back.peers() if back else []))
        if back:
            back.start()
        swap.start()
        dk_ref[...] = jnp.zeros_like(dk_ref)
        dv_ref[...] = jnp.zeros_like(dv_ref)
        own = lax.axis_index("blk") % share

        def query_block(step, carry):
            for n, event in enumerate(events):
                if back and n < back.nz - 1:
                    pl.when(step == event)(lambda n=n: back.send(n))

            def work():
                query = qkv_ref[step // per, 0, step % per]
                go = go_ref[step]
                delta = jnp.sum(go.astype(F32).T * out_t_ref[step], axis=0, keepdims=True)
                log_total = lse_ref[step]

                def body(j, dq):
                    key = qkv_ref[j // per, 1, j % per]
                    value = qkv_ref[j // per, 2, j % per]
                    scores = mm(key, query, NT) * scale + bias_ref[step * blocks + j]
                    probs = jnp.exp(scores - log_total)
                    grad_scores = (probs * (mm(value, go, NT) - delta)).astype(BF16)
                    dv_ref[j] += mm(probs.astype(BF16), go)
                    dk_ref[j] += mm(grad_scores, query)
                    return dq + mm(grad_scores, key, TN)

                dq = lax.fori_loop(0, step + 1, body, jnp.zeros((block, dim), F32))
                grad_ref[step // per, 0, step % per] = (dq * scale).astype(BF16)

            if share == 1:
                work()
            else:
                mine = step % share == own
                pl.when(mine)(work)

                @pl.when(jnp.logical_not(mine))
                def _():
                    grad_ref[step // per, 0, step % per] = jnp.zeros((block, dim), BF16)

            return carry

        lax.fori_loop(0, blocks, query_block, 0)
        if back:
            for turn in range(len(events), back.nz - 1):
                back.send(turn)

        def store(j, carry):
            grad_ref[j // per, 1, j % per] = (dk_ref[j] * scale).astype(BF16)
            grad_ref[j // per, 2, j % per] = dv_ref[j].astype(BF16)
            return carry

        lax.fori_loop(0, blocks, store, 0)
        if back:
            back.finish()
        swap.wait()

    anywhere = pl.BlockSpec(memory_space=pl.ANY)
    inside = pl.BlockSpec(memory_space=pltpu.VMEM)
    nz, _, tok, width = shares[0].shape if shares else (0, 0, 0, 0)
    out = pl.pallas_call(
        kernel,
        in_specs=[pl.BlockSpec(memory_space=pltpu.SMEM)] + [inside] * 4
        + [anywhere] * (count + len(shares)),
        out_specs=[inside] + [anywhere] * count + [inside] * len(shares),
        out_shape=[jax.ShapeDtypeStruct(qkv.shape, BF16)]
        + [jax.ShapeDtypeStruct(v.shape, v.dtype) for v in swaps]
        + [jax.ShapeDtypeStruct((tok, width), BF16)] * len(shares),
        scratch_shapes=[
            pltpu.VMEM((blocks, block, dim), F32),
            pltpu.VMEM((blocks, block, dim), F32),
            pltpu.SemaphoreType.DMA((count,)),
            pltpu.SemaphoreType.DMA((count,)),
        ]
        + (Return.scratch(nz, tok, width) if shares else []),
        compiler_params=pltpu.CompilerParams(
            collective_id=collective_id, has_side_effects=True, vmem_limit_bytes=VMEM_BYTES
        ),
        name="attend_backward",
    )(bias, qkv, grad_out, out_t, lse, *swaps, *shares)
    return out[0], out[1 : 1 + count], out[1 + count :]


def expert_exchange(tokens, cots, slots, gates, weights, nh, nb, rows, collective_id):
    tok, width = tokens.shape
    half = weights[0].shape[1]
    nz, ny = nb // 2, nh // 2
    steps = nz * ny
    count = 2 * rows
    parts = 2
    chunk = min(512, width)
    full = 2 * half

    def kernel(own_ref, slot_ref, gate_ref, cot_ref, *refs):
        weight_refs = refs[0:6]
        *sum_refs, xr_out, er_out, hid_out, dpre_out, all_ref = refs[6:13]
        (
            in_w, down_w, tok_buf, cot_buf, xr, er, hid, dpre, keep, give, got,
            send_sem, recv_sem, weight_sem, tok_sem, cot_sem, row_sem, sum_sem, give_sem, got_sem, free_sem,
        ) = refs[13:]
        relay = Relay([(own_ref, all_ref, parts)], nz, ny, send_sem, recv_sem)
        y, core, z, sibling = relay.y, relay.core, relay.z, relay.sibling
        weight_copies = [
            pltpu.make_async_copy(ref, place, weight_sem.at[n])
            for n, (ref, place) in enumerate(zip(
                weight_refs,
                [in_w.at[:, pl.ds(n * half, half)] for n in range(4)]
                + [down_w.at[pl.ds(n * half, half)] for n in range(2)],
            ))
        ]
        for copy in weight_copies:
            copy.start()
        greet(relay.peers())
        relay.start()

        lanes = lax.broadcasted_iota(jnp.int32, (rows, tok), 0)

        def places(step):
            return nearest(z, step // ny, nz), nearest(y, step % ny, ny)

        def row_copies(step, slot):
            return [
                pltpu.make_async_copy(buf.at[slot], out.at[step], row_sem.at[slot, n])
                for n, (buf, out) in enumerate(
                    ((xr, xr_out), (er, er_out), (hid, hid_out), (dpre, dpre_out))
                )
            ]

        def sum_copies(step, slot):
            z_at, y_at = places(step)
            return [
                pltpu.make_async_copy(keep.at[slot, n], sum_refs[n].at[z_at, y_at], sum_sem.at[slot, n])
                for n in range(2)
            ]

        def give_copies(slot):
            return [
                pltpu.make_async_remote_copy(
                    src_ref=give.at[slot, n],
                    dst_ref=got.at[slot, n],
                    send_sem=give_sem.at[slot, n],
                    recv_sem=got_sem.at[slot, n],
                    device_id=sibling,
                    device_id_type=pl.DeviceIdType.MESH,
                )
                for n in range(2)
            ]

        def finish(step, slot):
            for n, copy in enumerate(give_copies(slot)):
                copy.wait_recv()
                for r in range(0, tok, 64):
                    here = pl.ds(r, 64)
                    keep[slot, n, here, :] = (
                        keep[slot, n, here, :].astype(F32) + got[slot, n, here, :].astype(F32)
                    ).astype(BF16)
            for copy in sum_copies(step, slot):
                copy.start()
            pl.semaphore_signal(free_sem, inc=1, device_id=sibling, device_id_type=pl.DeviceIdType.MESH)

        def block_copies(step, source, buffer, sems):
            z_at, y_at = places(step)
            return [
                pltpu.make_async_copy(source.at[z_at, c, y_at], buffer.at[n], sems.at[n])
                for n, c in enumerate((core, 1 - core))
            ]

        def cot_copies(step):
            return block_copies(step, cot_ref, cot_buf, cot_sem)

        def tok_copies(step):
            return block_copies(step, all_ref, tok_buf, tok_sem)

        def load_cots(step):
            for copy in cot_copies(step):
                copy.start()

        def load_tokens(step):
            z_at, y_at = places(step)
            z_rank, y_rank = step // ny, step % ny

            @pl.when(y_rank > 0)
            def _():
                relay.pass_on(z_at, y_at)

            for away in range(1, nz):

                @pl.when((y_rank == ny - 1) & (z_rank + 1 == away))
                def _(away=away):
                    relay.pass_on_z(away)

            relay.arrived(z_at, y_at, 1 - core)
            if isinstance(step, int):
                pltpu.make_async_copy(own_ref, tok_buf.at[0], tok_sem.at[0]).start()
                pltpu.make_async_copy(all_ref.at[z, 1 - core, y], tok_buf.at[1], tok_sem.at[1]).start()
                return
            for copy in tok_copies(step):
                copy.start()

        load_cots(0)
        load_tokens(0)
        for copy in weight_copies:
            copy.wait()

        def body(step, carry):
            z_at, y_at = places(step)
            slot = step % 2
            cores = (core, 1 - core)

            @pl.when(step >= 2)
            def _():
                for copy in row_copies(step - 2, slot):
                    copy.wait()
                for copy in sum_copies(step - 2, slot):
                    copy.wait()
                for copy in give_copies(slot):
                    copy.wait_send()

            for copy in tok_copies(step):
                copy.wait()
            picks = []
            scale_by = []
            for n, c in enumerate(cores):
                hit = lanes == slot_ref[z_at, c, y_at]
                picks.append(jnp.where(hit, 1.0, 0.0).astype(BF16))
                scale_by.append(
                    jnp.sum(jnp.where(hit, gate_ref[z_at, c, y_at], 0.0), axis=1, keepdims=True)
                )
                here = slice(n * rows, (n + 1) * rows)
                for col in range(0, width, chunk):
                    cols = slice(col, col + chunk)
                    xr[slot, here, cols] = mm(picks[n], tok_buf[n, :, cols]).astype(BF16)
            for copy in cot_copies(step):
                copy.wait()
            for n in range(2):
                here = slice(n * rows, (n + 1) * rows)
                for col in range(0, width, chunk):
                    cols = slice(col, col + chunk)
                    er[slot, here, cols] = (
                        scale_by[n] * mm(picks[n], cot_buf[n, :, cols])
                    ).astype(BF16)

            @pl.when(step + 1 < steps)
            def _():
                load_cots(step + 1)

            for m in range(0, full, half):
                gate_cols, up_cols = slice(m, m + half), slice(full + m, full + m + half)
                gate_pre = mm(xr[slot], in_w[:, gate_cols])
                up_pre = mm(xr[slot], in_w[:, up_cols])
                sig = jax.nn.sigmoid(gate_pre)
                act = gate_pre * sig
                hid[slot, :, gate_cols] = (act * up_pre).astype(BF16)
                dhid = mm(er[slot], down_w[gate_cols, :], NT).astype(BF16).astype(F32)
                dpre[slot, :, gate_cols] = (
                    dhid * up_pre * sig * (1.0 + gate_pre * (1.0 - sig))
                ).astype(BF16)
                dpre[slot, :, up_cols] = (dhid * act).astype(BF16)
            for copy in row_copies(step, slot):
                copy.start()
            for col in range(0, width, chunk):
                if col == width - chunk:

                    @pl.when(step + 1 < steps)
                    def _():
                        load_tokens(step + 1)

                cols = slice(col, col + chunk)
                part_sum = mm(hid[slot], down_w[:, cols])
                drow = mm(dpre[slot], in_w[cols, :], NT).astype(BF16)
                for n, dest in enumerate((keep, give)):
                    here = slice(n * rows, (n + 1) * rows)
                    dest[slot, 0, :, cols] = mm(picks[n], drow[here], TN).astype(BF16)
                    scaled = (part_sum[here] * scale_by[n]).astype(BF16)
                    dest[slot, 1, :, cols] = mm(picks[n], scaled, TN).astype(BF16)

            @pl.when(step >= 2)
            def _():
                pl.semaphore_wait(free_sem, 1)

            for copy in give_copies(slot):
                copy.start()

            @pl.when(step >= 1)
            def _():
                finish(step - 1, 1 - slot)

            return carry

        lax.fori_loop(0, steps, body, 0)
        last = (steps - 1) % 2
        finish(steps - 1, last)
        for step in (steps - 2, steps - 1):
            slot = step % 2
            for copy in row_copies(step, slot):
                copy.wait()
            for copy in sum_copies(step, slot):
                copy.wait()
            for copy in give_copies(slot):
                copy.wait_send()
        pl.semaphore_wait(free_sem, 2)

        relay.drain()

    anywhere = pl.BlockSpec(memory_space=pl.ANY)
    inside = pl.BlockSpec(memory_space=pltpu.VMEM)
    out = pl.pallas_call(
        kernel,
        in_specs=[anywhere, inside, inside] + [anywhere] * 7,
        out_specs=[anywhere] * 7,
        out_shape=[
            jax.ShapeDtypeStruct((nz, ny, tok, width), BF16),
            jax.ShapeDtypeStruct((nz, ny, tok, width), BF16),
            jax.ShapeDtypeStruct((steps, count, width), BF16),
            jax.ShapeDtypeStruct((steps, count, width), BF16),
            jax.ShapeDtypeStruct((steps, count, full), BF16),
            jax.ShapeDtypeStruct((steps, count, 2 * full), BF16),
            jax.ShapeDtypeStruct((nz, 2, ny, tok, width), BF16),
        ],
        scratch_shapes=[
            pltpu.VMEM((width, 2 * full), BF16),
            pltpu.VMEM((full, width), BF16),
            pltpu.VMEM((2, tok, width), BF16),
            pltpu.VMEM((2, tok, width), BF16),
            pltpu.VMEM((2, count, width), BF16),
            pltpu.VMEM((2, count, width), BF16),
            pltpu.VMEM((2, count, full), BF16),
            pltpu.VMEM((2, count, 2 * full), BF16),
            pltpu.VMEM((2, 2, tok, width), BF16),
            pltpu.VMEM((2, 2, tok, width), BF16),
            pltpu.VMEM((2, 2, tok, width), BF16),
            pltpu.SemaphoreType.DMA((5, steps, parts)),
            pltpu.SemaphoreType.DMA((2, steps, parts)),
            pltpu.SemaphoreType.DMA((6,)),
            pltpu.SemaphoreType.DMA((2,)),
            pltpu.SemaphoreType.DMA((2,)),
            pltpu.SemaphoreType.DMA((2, 4)),
            pltpu.SemaphoreType.DMA((2, 2)),
            pltpu.SemaphoreType.DMA((2, 2)),
            pltpu.SemaphoreType.DMA((2, 2)),
            pltpu.SemaphoreType.REGULAR,
        ],
        compiler_params=pltpu.CompilerParams(
            collective_id=collective_id, has_side_effects=True, vmem_limit_bytes=VMEM_BYTES
        ),
        name="expert_exchange",
    )(tokens, slots, gates, cots, *weights)
    return out[:6]


def return_sum(shares, collective_id):
    nz, ny, tok, width = shares.shape
    assert ny == 2

    def kernel(share_ref, out_ref, *scratch):
        back = Return(share_ref, out_ref, scratch)
        greet(back.peers())
        back.start()
        for turn in range(nz - 1):
            back.send(turn)
        back.finish()

    return pl.pallas_call(
        kernel,
        in_specs=[pl.BlockSpec(memory_space=pl.ANY)],
        out_specs=pl.BlockSpec(memory_space=pltpu.VMEM),
        out_shape=jax.ShapeDtypeStruct((tok, width), BF16),
        scratch_shapes=Return.scratch(nz, tok, width),
        compiler_params=pltpu.CompilerParams(
            collective_id=collective_id, has_side_effects=True, vmem_limit_bytes=VMEM_BYTES
        ),
        name="return_sum",
    )(shares)


def local(
    hidden_in,
    attn_gain,
    w_query,
    w_key,
    w_value,
    query_gain,
    key_gain,
    w_out,
    ffn_gain,
    w_gate,
    w_up,
    w_down,
    routes,
    gate_weights,
    block_starts,
    cotangent,
):
    head_count = lax.axis_size("head")
    blk_count = lax.axis_size("blk")
    head_index = lax.axis_index("head")
    blk_index = lax.axis_index("blk")
    piece, seqs, width = hidden_in.shape
    span = piece * head_count
    per = span // BLOCK
    columns = w_query.shape[1]
    heads_here = columns // HEAD_DIM
    top_count = routes.shape[2]
    experts = blk_count * head_count // 2
    devices = blk_count * head_count
    tok = piece * seqs
    capacity = max(2, 5 * tok * top_count // (4 * experts))
    rows = -(-capacity // 32) * 32
    items = seqs * heads_here
    share = blk_count // items
    scale = 1.0 / math.sqrt(HEAD_DIM)
    everyone = ("blk", "head")

    def own_rows(values):
        return values.transpose(1, 0, 2).reshape(tok, values.shape[2])

    def out_rows(values):
        return values.reshape(seqs, piece, width).transpose(1, 0, 2)

    nz, ny = blk_count // 2, head_count // 2

    def flip_head(values, bit):
        return lax.ppermute(values, "head", [(h, h ^ bit) for h in range(head_count)])

    def flip_blk(values, bit):
        return lax.ppermute(values, "blk", [(b, b ^ bit) for b in range(blk_count)])

    gate_other = flip_head(w_gate[0], 1)

    table = jnp.concatenate([own_rows(routes).astype(F32).T, own_rows(gate_weights).T], axis=0)

    hidden_f = own_rows(hidden_in).astype(F32)
    grad_y_b = own_rows(cotangent)
    grad_y = grad_y_b.astype(F32)

    inv_one = inverse_rms(hidden_f)
    normed = (hidden_f * inv_one * attn_gain).astype(BF16)
    group = lax.all_gather(normed, "head", axis=0, tiled=True)
    query_cols = lax.all_gather(w_query, "blk", axis=0, tiled=True)
    key_cols = lax.all_gather(w_key, "blk", axis=0, tiled=True)
    value_cols = lax.all_gather(w_value, "blk", axis=0, tiled=True)
    out_w = lax.all_gather(w_out, "blk", axis=1, tiled=True)

    query_raw = mm(group, query_cols)
    key_raw = mm(group, key_cols)
    value_raw = mm(group, value_cols)
    square_sums = lax.psum(
        jnp.stack([jnp.sum(query_raw * query_raw, -1), jnp.sum(key_raw * key_raw, -1)]), "head"
    )
    inv_query = lax.rsqrt(square_sums[0][:, None] / width + EPSILON)
    inv_key = lax.rsqrt(square_sums[1][:, None] / width + EPSILON)
    gain_query = lax.dynamic_slice_in_dim(query_gain, head_index * columns, columns)
    gain_key = lax.dynamic_slice_in_dim(key_gain, head_index * columns, columns)
    query_n = (query_raw * inv_query * gain_query).astype(BF16)
    key_n = (key_raw * inv_key * gain_key).astype(BF16)
    value_n = value_raw.astype(BF16)

    def to_items(values):
        parts = values.reshape(head_count, seqs, piece, heads_here, HEAD_DIM)
        parts = parts.transpose(1, 3, 0, 2, 4).reshape(items, span, HEAD_DIM)
        return jnp.repeat(parts, share, axis=0) if share > 1 else parts

    def from_items(values):
        if share > 1:
            values = values.reshape(items, share, span, HEAD_DIM).astype(F32).sum(1)
        parts = values.reshape(seqs, heads_here, head_count, piece, HEAD_DIM)
        return parts.transpose(2, 0, 3, 1, 4).reshape(head_count * tok, columns)

    def swap(values):
        return lax.all_to_all(values, "blk", split_axis=0, concat_axis=0, tiled=True)

    item = blk_index // share
    starts = lax.dynamic_index_in_dim(block_starts, item // heads_here, 0, keepdims=False)
    qkv = jnp.stack([to_items(query_n), to_items(key_n), to_items(value_n)], axis=1)
    qkv, gate_other = lax.optimization_barrier((qkv, gate_other))
    qkv = swap(qkv)
    qkv = qkv.reshape(blk_count, 3, per, BLOCK, HEAD_DIM)
    total_blocks = blk_count * per
    key_block = jnp.arange(total_blocks, dtype=jnp.int32)
    bias = jnp.where(key_block[None, :] >= starts[:, None], 0.0, -1e30).astype(F32).reshape(-1)
    heads_out, heads_out_t, log_total, all_cots, tables, up_other, down_other = attend_forward(
        bias, qkv, grad_y_b, table, (w_up[0], w_down[0]), nz, ny, scale, share, 2
    )
    expert_weights = (w_gate[0], gate_other, w_up[0], up_other, w_down[0], down_other)

    expert = (blk_index * head_count + head_index) // 2
    named = tables[..., :top_count, :] == expert.astype(F32)
    hit = jnp.any(named, axis=-2)
    gates = jnp.sum(jnp.where(named, tables[..., top_count:, :], 0.0), axis=-2)[..., None, :]
    before = jnp.triu(jnp.ones((tok, tok), BF16), 1)
    ranks = jnp.dot(
        hit.reshape(-1, tok).astype(BF16), before, preferred_element_type=F32
    ).astype(jnp.int32)
    slots = jnp.where(hit, ranks.reshape(hit.shape), -1)[..., None, :]

    attended = from_items(swap(heads_out.reshape(blk_count, span, HEAD_DIM))).astype(BF16)
    branch = lax.psum_scatter(
        mm(attended, out_w).astype(BF16), "head", scatter_dimension=0, tiled=True
    ).astype(F32)
    middle = hidden_f + branch
    inv_two = inverse_rms(middle)
    normed_two = (middle * inv_two * ffn_gain).astype(BF16)

    dx_share, moe_share, xr, er, hid, dpre = expert_exchange(
        normed_two, all_cots, slots, gates, expert_weights, head_count, blk_count, rows, 0
    )

    def halvings(count):
        return [1 << i for i in reversed(range(count.bit_length() - 1))]

    def halve(values, flip, bit, mine):
        pair = values.reshape((2, values.shape[0] // 2) + values.shape[1:])
        kept = lax.dynamic_index_in_dim(pair, mine, 0, keepdims=False)
        sent = lax.dynamic_index_in_dim(pair, 1 - mine, 0, keepdims=False)
        return kept, flip(sent.astype(BF16), bit)

    y_bits = [(flip_head, 2 * b, (head_index // (2 * b)) % 2) for b in halvings(ny)]
    z_bits = [(flip_blk, 2 * b, (blk_index // (2 * b)) % 2) for b in halvings(nz)]

    def give_back(values, bits):
        for flip, bit, mine in bits:
            kept, came = halve(values, flip, bit, mine)
            values = kept.astype(F32) + came.astype(F32)
        return values[0]

    if ny == 2:
        grad_normed_two = return_sum(dx_share, 1)
    else:
        grad_normed_two = give_back(dx_share.swapaxes(0, 1), y_bits)
        grad_normed_two = give_back(grad_normed_two, z_bits).astype(BF16)
    grad_normed_two, moe_share = lax.optimization_barrier((grad_normed_two, moe_share))
    grad_normed_two = grad_normed_two.astype(F32)
    xr, er = xr.reshape(-1, width), er.reshape(-1, width)
    hid, dpre = [v.reshape(-1, v.shape[-1]) for v in (hid, dpre)]
    half = w_gate.shape[2]
    dgate, dgate_other, dup, dup_other = [dpre[:, n * half : (n + 1) * half] for n in range(4)]

    halves = [
        mm(hid[:, :half], er, TN), mm(xr, dgate, TN), mm(xr, dup, TN),
        mm(hid[:, half:], er, TN), mm(xr, dgate_other, TN), mm(xr, dup_other, TN),
    ]
    gained_two = grad_normed_two * ffn_gain
    ffn_gain_part = jnp.sum(grad_normed_two * middle * inv_two, 0)
    grad_middle = (
        grad_y
        + inv_two * gained_two
        - middle * inv_two * inv_two * inv_two * jnp.mean(gained_two * middle, -1, keepdims=True)
    )
    grad_branch = grad_middle.astype(BF16)
    grad_group = lax.all_gather(grad_branch, "head", axis=0, tiled=True)
    grad_group, *halves = lax.optimization_barrier((grad_group, *halves))
    others = [v.astype(BF16) for v in halves[3:]]
    grad_attended = mm(grad_group, out_w, NT).astype(BF16)
    out_part = mm(attended, grad_group, TN)
    grad_heads = swap(to_items(grad_attended)).reshape(blk_count * per, BLOCK, HEAD_DIM)
    own_sum = ny == 2
    grad_qkv, others[1:], sums = attend_backward(
        bias, qkv, grad_heads, heads_out_t, log_total, others[1:], [moe_share] * own_sum,
        scale, share, 3,
    )
    others[0] = flip_head(others[0], 1)
    grad_qkv = swap(grad_qkv.reshape(blk_count, 3, span, HEAD_DIM))
    grad_qkv, others[0] = lax.optimization_barrier((grad_qkv, others[0]))
    grad_down, grad_gate, grad_up = [
        (mine + other.astype(F32))[None] for mine, other in zip(halves[:3], others)
    ]
    if own_sum:
        expert_sum = sums[0].astype(F32)
    else:
        expert_sum = give_back(give_back(moe_share.swapaxes(0, 1), y_bits), z_bits)
    result = middle + expert_sum
    grad_query_n = rounded(from_items(grad_qkv[:, 0]))
    grad_key_n = rounded(from_items(grad_qkv[:, 1]))
    grad_value_b = from_items(grad_qkv[:, 2]).astype(BF16)
    gained_query = grad_query_n * gain_query
    gained_key = grad_key_n * gain_key
    row_sums = lax.psum(
        jnp.stack([jnp.sum(gained_query * query_raw, -1), jnp.sum(gained_key * key_raw, -1)]),
        "head",
    )
    grad_query_b = (
        inv_query * gained_query
        - query_raw * inv_query * inv_query * inv_query * row_sums[0][:, None] / width
    ).astype(BF16)
    grad_key_b = (
        inv_key * gained_key
        - key_raw * inv_key * inv_key * inv_key * row_sums[1][:, None] / width
    ).astype(BF16)
    query_gain_part = jnp.sum(grad_query_n * query_raw * inv_query, 0)
    key_gain_part = jnp.sum(grad_key_n * key_raw * inv_key, 0)
    total = (
        mm(grad_query_b, query_cols, NT)
        + mm(grad_key_b, key_cols, NT)
        + mm(grad_value_b, value_cols, NT)
    )
    grad_normed = rounded(
        lax.psum_scatter(total.astype(BF16), "head", scatter_dimension=0, tiled=True).astype(F32)
    )
    query_part = mm(group, grad_query_b, TN)
    key_part = mm(group, grad_key_b, TN)
    value_part = mm(group, grad_value_b, TN)
    gained_one = grad_normed * attn_gain
    attn_gain_part = jnp.sum(grad_normed * hidden_f * inv_one, 0)
    grad_hidden_in = (
        grad_middle
        + inv_one * gained_one
        - hidden_f
        * inv_one
        * inv_one
        * inv_one
        * jnp.mean(gained_one * hidden_f, -1, keepdims=True)
    )

    def over_blk(values, dim):
        return lax.psum_scatter(
            values.astype(BF16), "blk", scatter_dimension=dim, tiled=True
        ).astype(F32)

    grad_query = over_blk(query_part, 0)
    grad_key = over_blk(key_part, 0)
    grad_value = over_blk(value_part, 0)
    grad_out = over_blk(out_part, 1)
    zero_width = jnp.zeros((width,), F32)
    query_gain_full = lax.dynamic_update_slice_in_dim(
        zero_width, query_gain_part, head_index * columns, 0
    )
    key_gain_full = lax.dynamic_update_slice_in_dim(
        zero_width, key_gain_part, head_index * columns, 0
    )
    square_parts = jnp.stack(
        [jnp.sum(result * result), jnp.sum(branch * branch), jnp.sum(expert_sum * expert_sum)]
    )
    totals = lax.psum(
        (square_parts, attn_gain_part, ffn_gain_part, query_gain_full, key_gain_full),
        everyone,
    )
    entry_count = tok * width * devices
    stream_stats = jnp.sqrt(totals[0] / entry_count + EPSILON)
    return (
        out_rows(result.astype(BF16)),
        out_rows(grad_hidden_in.astype(BF16)),
        totals[1],
        grad_query,
        grad_key,
        grad_value,
        totals[3],
        totals[4],
        grad_out,
        totals[2],
        grad_gate,
        grad_up,
        grad_down,
        stream_stats,
    )


def solution(mesh):
    rows3 = P(("blk", "head"), None, None)
    placed = (
        rows3, P(), P("blk", "head"), P("blk", "head"), P("blk", "head"), P(), P(),
        P("head", "blk"), P(), rows3, rows3, rows3, rows3, rows3, P(), rows3,
    )
    return jax.shard_map(
        local,
        mesh=mesh,
        in_specs=placed,
        out_specs=(
            rows3, rows3, P(), P("blk", "head"), P("blk", "head"), P("blk", "head"), P(), P(),
            P("head", "blk"), P(), rows3, rows3, rows3, P(),
        ),
        check_vma=False,
    )
```

time: 2170 us -> 1290 us (0.59)
  waiting for transfers between devices: 1420 us -> 434 us
  Pallas kernels: 195 us -> 462 us
  blocking collectives: 278 us -> 121 us
    reduce_scatter x4 -> x0, waiting for transfers between devices: 759 us -> none  [the longest x2 649 us: give_back(): parts = lax.psum_scatter(parts, 'blk', scatter_dimension=0, tiled=True)]
    pallas_call x3 -> x4, Pallas kernels: 195 us -> 462 us  [the longest x1 134 us: expert_exchange(): pl.pallas_call(kernel, in_specs=[anywhere, inside, inside] + [anywhere] *...]
    all_gather x2 -> x0, waiting for transfers between devices: 210 us -> none  [the longest x1 197 us: local(): all_tokens = lax.all_gather(normed_two, everyone, axis=0, tiled=False)]
    all_gather x2 -> x0, blocking collectives: 138 us -> none  [the longest x1 70.7 us: local(): all_routes = lax.all_gather(own_rows(routes), everyone, axis=0, tiled=False)]
    all_gather x1, waiting for transfers between devices: 52.8 us -> 0.01 us  [local(): grad_group = lax.all_gather(grad_branch, 'head', axis=0, tiled=True)]
    all_to_all x2, waiting for transfers between devices: 172 us -> 128 us  [swap(): lax.all_to_all(values, 'blk', split_axis=0, concat_axis=0, tiled=True)]
    reduce_scatter x4, waiting for transfers between devices: 7.39 us -> 51 us  [over_blk(): lax.psum_scatter(values.astype(BF16), 'blk', scatter_dimension=dim, tiled...]
    ppermute x0 -> x2, waiting for transfers between devices: none -> 40.6 us  [flip_head(): lax.ppermute(values, 'head', [(h, h ^ bit) for h in range(head_count)])]
  transfers between devices with their start and end apart: 20 -> 16, of which waited for: 16 -> 10; matrix products, arithmetic and copies ran while one was open for 8% -> 15% of each run, Pallas kernels for 2% -> 8%
where the time goes in v2:
time: 1290 us; the launch traced here: 1280 us
  Pallas kernels  462 us (36%)
  waiting for transfers between devices  434 us (34%)
  matrix products  123 us (10%)
  blocking collectives  121 us (9%)
  other arithmetic  63.1 us (5%)
  local copies, waits for them, and re-layouts  50.9 us (4%)
  between operations  15.3 us (1%)
  starting transfers between devices  14.1 us (1%)
    pallas_call x1, Pallas kernels, expert_exchange(): pl.pallas_call(kernel, in_specs=[anywhere, inside, inside] + [anywhere] *...  134 us
    all_to_all x2, waiting for transfers between devices, swap(): lax.all_to_all(values, 'blk', split_axis=0, concat_axis=0, tiled=True)  128 us
    pallas_call x1, Pallas kernels, attend_backward(): pl.pallas_call(kernel, in_specs=[pl.BlockSpec(memory_space=pltpu.SMEM)] +...  125 us
    dot_general x18, matrix products, mm(): return lax.dot_general(left, right, dims, preferred_element_type=F32)  123 us
    pallas_call x1, Pallas kernels, attend_forward(): pl.pallas_call(kernel, in_specs=[pl.BlockSpec(memory_space=pltpu.SMEM), i...  108 us
    pallas_call x1, Pallas kernels, return_sum(): pl.pallas_call(kernel, in_specs=[pl.BlockSpec(memory_space=pl.ANY)], out_...  95.2 us
    all_gather x1, waiting for transfers between devices, local(): group = lax.all_gather(normed, 'head', axis=0, tiled=True)  65.2 us
    all_to_all x2, blocking collectives, swap(): lax.all_to_all(values, 'blk', split_axis=0, concat_axis=0, tiled=True)  60.7 us
  transfers between devices with their start and end apart: 16, of which 10 were waited for; matrix products, arithmetic and copies ran while one was open for 15% of the time, Pallas kernels for 8%

profile of v2, /device:TPU:0, one launch (start us, length us, event | category | flops | bytes accessed | tf_op | source)
XLA Modules:
  0.0 1283.9 jit_solution(9316406267349550251)
XLA Ops:
  8.0 2.4 convert_bitcast_fusion
  15.5 3.0 collective-permute-start
  20.0 21.4 %all-gather.9.cloned.1.call-done = bf16[2048,512]{1,0:T(8,128)(2,1)} async-done(((bf16[256,512]{1,0:T(8,128)(2,1)}), bf16[2048,512]{1,0:T(8,128)(2,1)}) %all-gather.9.cloned.1.call-update) | async-done | bytes 2097168 | tf_op jit(solution)/shard_map/all_gather | solution.py:903
  41.5 65.2 %all-gather.7.cloned.1.call-done = bf16[1024,2048]{1,0:T(8,128)(2,1)} async-done(((bf16[256,2048]{1,0:T(8,128)(2,1)}), bf16[1024,2048]{1,0:T(8,128)(2,1)}) %all-gather.7.cloned.1.call-update) | async-done | bytes 4194320 | tf_op jit(solution)/shard_map/all_gather | solution.py:902
  106.7 6.6 multiply_reduce_fusion.3
  113.3 24.2 %all-gather.11.cloned.1.call-done = bf16[2048,512]{1,0:T(8,128)(2,1)} async-done(((bf16[256,512]{1,0:T(8,128)(2,1)}), bf16[2048,512]{1,0:T(8,128)(2,1)}) %all-gather.11.cloned.1.call-update) | async-done | bytes 2097168 | tf_op jit(solution)/shard_map/all_gather | solution.py:904
  137.4 6.6 multiply_reduce_fusion.2
  144.0 10.2 psum.49
  154.2 2.8 multiply_convert_fusion.2
  158.9 2.0 copy.85
  160.9 2.8 multiply_convert_fusion.1
  165.5 2.0 copy.86
  167.5 6.2 convolution_convert_fusion.6
  176.6 2.0 pad_maximum_fusion
  178.6 4.6 all-to-all-start
  186.5 85.0 %all-to-all-done = bf16[8,3,512,128]{3,2,1,0:T(8,128)(2,1)} async-done(((bf16[8,3,512,128]{3,2,1,0:T(8,128)(2,1)}), bf16[8,3,512,128]{3,2,1,0:T(8,128)(2,1)}, u32[]{:S(2)}, u32[]{:S(2)}) %all-to-all-start) | async-done | bytes 3145760 | tf_op jit(solution)/shard_map/all_to_all | solution.py:934
  271.6 107.6 %attend_forward.1 = (bf16[16,256,128]{2,1,0:T(8,128)(2,1)}, f32[16,128,256]{2,1,0:T(8,128)}, f32[16,1,256]{2,1,0:T(1,128)}, bf16[4,2,2,256,2048]{4,3,2,1,0:T(8,1...) custom-call(f32[256]{0:T(256)} %select_n.49.bias_ref, ...), custom_call_target="tpu_custom_call" | custom-call | tf_op jit(solution)/shard_map/attend_forward/pallas_call | solution.py:418
  379.2 30.1 %all_to_all.20 = bf16[8,512,128]{2,1,0:T(8,128)(2,1)S(1)} all-to-all(bf16[8,512,128]{2,1,0:T(8,128)(2,1)} %bitcast.167), channel_id=1, replica_groups=mesh['head'=4,'blk'=8] {'blk'}, dimensions={0} | all-to-all | bytes 2097152 | tf_op jit(solution)/shard_map/all_to_all | solution.py:934
  411.0 6.3 convolution_convert_fusion
  419.8 48.3 %reduce-scatter.7.cloned.1.call-done = bf16[256,2048]{1,0:T(8,128)(2,1)} async-done(((bf16[1024,2048]{1,0:T(8,128)(2,1)}), bf16[256,2048]{1,0:T(8,128)(2,1)}) %reduce-scatter.7.cloned.1.call-update) | async-done | bytes 1048592 | tf_op jit(solution)/shard_map/reduce_scatter | solution.py:961
  468.2 2.7 multiply_reduce_fusion.1
  472.3 134.2 %expert_exchange.1 = (bf16[4,2,256,2048]{3,2,1,0:T(8,128)(2,1)}, bf16[4,2,256,2048]{3,2,1,0:T(8,128)(2,1)}, bf16[8,320,2048]{2,1,0:T(8,128)(2,1)}, bf16[8,320,20...) custom-call(bf16[256,2048]{1,0:T(8,128)(2,1)} %multiply_convert_fusi, ...), custom_call_target="tpu_custom_call" | custom-call | tf_op jit(solution)/shard_map/expert_exchange/pallas_call | solution.py:771
  606.6 95.2 %return_sum.1 = bf16[256,2048]{1,0:T(8,128)(2,1)} custom-call(bf16[4,2,256,2048]{3,2,1,0:T(8,128)(2,1)} %get-tuple-element.51.share_ref), custom_call_target="tpu_custom_call" | custom-call | tf_op jit(solution)/shard_map/return_sum/pallas_call | solution.py:827
  701.9 2.0 fusion.35
  705.8 11.7 fusion.refs_1_
  717.5 10.3 fusion.4
  727.8 10.5 fusion.10
  738.4 7.3 fusion.2.refs_0_
  745.7 7.9 fusion.6
  753.7 7.6 fusion.8
  761.2 6.3 convolution_convert_fusion.5
  767.5 2.2 reshape.214
  771.1 30.6 %all_to_all.21 = bf16[8,512,128]{2,1,0:T(8,128)(2,1)} all-to-all(bf16[8,512,128]{2,1,0:T(8,128)(2,1)S(1)} %bitcast.152), channel_id=1, replica_groups=mesh['head'=4,'blk'=8] {'blk'}, dimensions={0} | all-to-all | bytes 2097152 | tf_op jit(solution)/shard_map/all_to_all | solution.py:934
  801.8 125.2 %attend_backward.1 = (bf16[8,3,2,256,128]{4,3,2,1,0:T(8,128)(2,1)}, bf16[2048,512]{1,0:T(8,128)(2,1)}, bf16[2048,512]{1,0:T(8,128)(2,1)}, bf16[256,2048]{1,0:T(8,128)(2,1)}) custom-call(f32[256]{0:T(256)} %select_n.49.bias_ref, bf16[8,3,2,256,128]{4,3,2,1,0:T(8,128)(2,1)} %bitcast.16.qkv_ref, bf16[16,256,128]{2,1,0:T(8,128)(2,1)} %bitcast.144, ...), custom_call_target="tpu_custom_call" | custom-call | tf_op jit(solution)/shard_map/attend_backward/pallas_call | solution.py:525
  927.0 4.4 all-to-all-start.3
  932.8 6.2 convolution_convert_fusion.1
  939.1 40.5 %collective-permute-done.1 = bf16[512,2048]{1,0:T(8,128)(2,1)} collective-permute-done((bf16[512,2048]{1,0:T(8,128)(2,1)}, bf16[512,2048]{1,0:T(8,128)(2,1)}, u32[]{:S(2)}, u32[]{:S(2)}) %collective-permute-start.1) | collective-permute-done | bytes 2097184 | tf_op jit(solution)/shard_map/ppermute | solution.py:887
  979.7 43.0 %all-to-all-done.3 = bf16[8,3,512,128]{3,2,1,0:T(8,128)(2,1)} async-done(((bf16[8,3,512,128]{3,2,1,0:T(8,128)(2,1)}), bf16[8,3,512,128]{3,2,1,0:T(8,128)(2,1)}, u32[]{:S(2)}, u32[]{:S(2)}) %all-to-all-start.3) | async-done | bytes 3145760 | tf_op jit(solution)/shard_map/all_to_all | solution.py:934
  1022.6 3.1 fusion.65
  1025.7 3.7 copy.94
  1029.4 2.6 reshape.219
  1031.9 3.7 copy.95
  1035.6 2.6 reshape.220
  1038.2 2.7 fusion.38
  1041.7 9.3 psum.50
  1051.0 2.7 fusion.26
  1054.7 3.9 convolution_convert_fusion.3
  1058.7 2.7 fusion.28
  1062.4 3.9 convolution_convert_fusion.4
  1066.4 2.2 copy.96
  1071.2 3.8 convolution_convert_fusion.2
  1075.3 4.5 fusion.68
  1079.8 5.7 fusion.67
  1085.5 8.2 add_convert_fusion
  1093.7 9.5 add_bitcast_fusion.1
  1105.5 5.8 add_bitcast_fusion
  1113.1 15.9 %reduce-scatter.11.cloned.1.call-done = bf16[256,512]{1,0:T(8,128)(2,1)} async-done(((bf16[2048,512]{1,0:T(8,128)(2,1)}), bf16[256,512]{1,0:T(8,128)(2,1)}) %reduce-scatter.11.cloned.1.call-update) | async-done | bytes 262160 | tf_op jit(solution)/shard_map/reduce_scatter | solution.py:1079
  1130.9 35.1 %reduce-scatter.15.cloned.1.call-done = bf16[256,512]{1,0:T(8,128)(2,1)} async-done(((bf16[2048,512]{1,0:T(8,128)(2,1)}), bf16[256,512]{1,0:T(8,128)(2,1)}) %reduce-scatter.15.cloned.1.call-update) | async-done | bytes 262160 | tf_op jit(solution)/shard_map/reduce_scatter | solution.py:1079
  1167.8 52.7 %reduce-scatter.9.cloned.1.call-done = bf16[256,2048]{1,0:T(8,128)(2,1)} async-done(((bf16[1024,2048]{1,0:T(8,128)(2,1)}), bf16[256,2048]{1,0:T(8,128)(2,1)}) %reduce-scatter.9.cloned.1.call-update) | async-done | bytes 1048592 | tf_op jit(solution)/shard_map/reduce_scatter | solution.py:1061
  1220.4 2.0 fusion.42
  1222.6 5.0 multiply_reduce_fusion
  1227.6 2.0 pad_maximum_fusion.4
  1229.6 40.7 %all-reduce = (f32[2048]{0:T(1024)}, f32[2048]{0:T(1024)}, f32[2048]{0:T(1024)}, f32[2048]{0:T(1024)}, f32[3]{0:T(128)S(1)}) all-reduce(f32[2048]{0:T(1024)S(1)} %get-tuple-element.80, f32[2048]{0:T(1024)S(1)} %dynamic_update_slice.6, f32[2048]{0:T(1024)S(1)} %dynamic_update_slice.7, ...), channel_id=1, replica_groups=mesh['head'=4,'blk'=8] {'blk','head'}, use_global_device_ids=true, to_apply=%region_15.16 | all-reduce | flops 8195 | bytes 65560 | tf_op jit(solution)/shard_map/psum | solution.py:1097
  1270.9 5.7 copy_bitcast_fusion
  (154 shorter events, 41.8 us)
Async XLA Ops:
  7.2 176.7 %copy-start = (s32[2,16]{1,0:T(2,128)S(1)}, s32[2,16]{1,0:T(2,128)}, u32[]{:S(2)}) copy-start(s32[2,16]{1,0:T(2,128)} %param.30) | copy-start | bytes 388
  7.2 34.3 %all-gather.9.cloned.1.call-start = ((), (), s32[]{:S(2)}) async-start(), calls=%async_computation.11 | async-start | bytes 2359296 | tf_op jit(solution)/shard_map/all_gather | solution.py:903
  7.9 98.8 %all-gather.7.cloned.1.call-start = ((), (), s32[]{:S(2)}) async-start(), calls=%async_computation.10 | async-start | bytes 5242880 | tf_op jit(solution)/shard_map/all_gather | solution.py:902
  10.4 1.2 copy-start.9
  10.4 2.5 copy-start.21
  12.9 1.3 copy-start.23
  14.2 123.2 %all-gather.11.cloned.1.call-start = ((), (), s32[]{:S(2)}) async-start(), calls=%async_computation.12 | async-start | bytes 2359296 | tf_op jit(solution)/shard_map/all_gather | solution.py:904
  14.9 152.6 %all-gather.13.cloned.1.call-start = ((), (), s32[]{:S(2)}) async-start(), calls=%async_computation.13 | async-start | bytes 2359296 | tf_op jit(solution)/shard_map/all_gather | solution.py:905
  15.5 163.1 %collective-permute-start = (bf16[2048,512]{1,0:T(8,128)(2,1)}, bf16[2048,512]{1,0:T(8,128)(2,1)}, u32[]{:S(2)}, u32[]{:S(2)}) collective-permute-start(bf16[2048,512]{1,0:T(8,128)(2,1)} %bitcast.162), channel_id=1, source_target_pairs={{0,8},{8,0},{16,24},{24,16},{1,9},{9,1},{17,25},{25,17},{2,10},{10... | collective-permute-start | bytes 6291464 | tf_op jit(solution)/shard_map/ppermute | solution.py:887
  175.0 1.2 copy-start.12
  175.0 1.5 copy-start.13
  178.6 6.0 copy-start.15
  178.6 93.0 %all-to-all-start = ((bf16[8,3,512,128]{3,2,1,0:T(8,128)(2,1)}), bf16[8,3,512,128]{3,2,1,0:T(8,128)(2,1)}, u32[]{:S(2)}, u32[]{:S(2)}) async-start(bf16[8,3,512,128]{3,2,1,0:T(8,128)(2,1)} %pad_maximum_fusion), calls=%async_computation | async-start | bytes 6291456 | tf_op jit(solution)/shard_map/all_to_all | solution.py:934
  183.2 2.8 copy-start.25
  183.2 2.8 copy-start.26
  183.2 227.9 %all-gather.15.cloned.1.call-start = ((), (), s32[]{:S(2)}) async-start(), calls=%async_computation.14 | async-start | bytes 2359296 | tf_op jit(solution)/shard_map/all_gather | solution.py:906
  183.8 284.4 %reduce-scatter.7.cloned.1.call-start = ((), (), s32[]{:S(2)}) async-start(), calls=%async_computation.15 | async-start | bytes 5242880 | tf_op jit(solution)/shard_map/reduce_scatter | solution.py:961
  417.3 0.9 copy-start.19
  417.3 343.9 %all-gather.17.cloned.1.call-start = ((), (), s32[]{:S(2)}) async-start(), calls=%async_computation.16 | async-start | bytes 5242880 | tf_op jit(solution)/shard_map/all_gather | solution.py:1014
  419.8 51.0 %copy-start.20 = (f32[2048]{0:T(1024)S(1)}, f32[2048]{0:T(1024)}, u32[]{:S(2)}) copy-start(f32[2048]{0:T(1024)} %param.24) | copy-start | bytes 24580
  470.9 233.1 %copy-start.2 = (f32[256,2048]{1,0:T(8,128)}, f32[256,2048]{1,0:T(8,128)S(1)}, u32[]{:S(2)}) copy-start(f32[256,2048]{1,0:T(8,128)S(1)} %get-tuple-element.92) | copy-start | bytes 6291460
  701.8 2.1 copy-start.5
  701.8 2.1 copy-start.6
  717.5 20.8 %slice-start = ((s8[10485760]{0:T(1024)(128)(4,1)}), s8[4194304]{0:T(1024)(128)(4,1)S(1)}, s32[]{:S(2)}) async-start(s8[10485760]{0:T(1024)(128)(4,1)} %bitcast.186), calls=%async_computation.22 | async-start | bytes 8388608
  717.5 20.8 %slice-start.1 = ((s8[10485760]{0:T(1024)(128)(4,1)}), s8[4194304]{0:T(1024)(128)(4,1)S(1)}, s32[]{:S(2)}) async-start(s8[10485760]{0:T(1024)(128)(4,1)} %bitcast.186), calls=%async_computation.23 | async-start | bytes 8388608
  717.5 20.8 %slice-start.3 = ((s8[10485760]{0:T(1024)(128)(4,1)}), s8[4194304]{0:T(1024)(128)(4,1)S(1)}, s32[]{:S(2)}) async-start(s8[10485760]{0:T(1024)(128)(4,1)} %bitcast.192), calls=%async_computation.25 | async-start | bytes 8388608
  717.5 20.8 %slice-start.4 = ((s8[10485760]{0:T(1024)(128)(4,1)}), s8[4194304]{0:T(1024)(128)(4,1)S(1)}, s32[]{:S(2)}) async-start(s8[10485760]{0:T(1024)(128)(4,1)} %bitcast.192), calls=%async_computation.26 | async-start | bytes 8388608
  727.8 10.6 slice-start.2
  727.8 10.6 slice-start.5
  927.0 95.7 %all-to-all-start.3 = ((bf16[8,3,512,128]{3,2,1,0:T(8,128)(2,1)}), bf16[8,3,512,128]{3,2,1,0:T(8,128)(2,1)}, u32[]{:S(2)}, u32[]{:S(2)}) async-start(bf16[8,3,512,128]{3,2,1,0:T(8,128)(2,1)} %bitcast.161), calls=%async_computation.4 | async-start | bytes 6291456 | tf_op jit(solution)/shard_map/all_to_all | solution.py:934
  931.4 171.8 %reduce-scatter.17.cloned.1.call-start = ((), (), s32[]{:S(2)}) async-start(), calls=%async_computation.21 | async-start | bytes 2359296 | tf_op jit(solution)/shard_map/reduce_scatter | solution.py:1079
  931.5 48.2 %collective-permute-start.1 = (bf16[512,2048]{1,0:T(8,128)(2,1)}, bf16[512,2048]{1,0:T(8,128)(2,1)}, u32[]{:S(2)}, u32[]{:S(2)}) collective-permute-start(bf16[512,2048]{1,0:T(8,128)(2,1)} %fusion.4), channel_id=1, source_target_pairs={{0,8},{8,0},{16,24},{24,16},{1,9},{9,1},{17,25},{25,17},{2,10},{10... | collective-permute-start | bytes 6291464 | tf_op jit(solution)/shard_map/ppermute | solution.py:887
  939.1 172.2 %reduce-scatter.13.cloned.1.call-start = ((), (), s32[]{:S(2)}) async-start(), calls=%async_computation.19 | async-start | bytes 2359296 | tf_op jit(solution)/shard_map/reduce_scatter | solution.py:1079
  1038.2 2.7 copy-start.4
  1038.2 2.8 copy-start.8
  1051.0 3.7 copy-start.27
  1053.8 1.0 copy-start.16
  1058.6 70.4 %reduce-scatter.11.cloned.1.call-start = ((), (), s32[]{:S(2)}) async-start(), calls=%async_computation.18 | async-start | bytes 2359296 | tf_op jit(solution)/shard_map/reduce_scatter | solution.py:1079
  1058.7 3.7 copy-start.28
  1061.4 1.0 copy-start.17
  1066.3 99.6 %reduce-scatter.15.cloned.1.call-start = ((), (), s32[]{:S(2)}) async-start(), calls=%async_computation.20 | async-start | bytes 2359296 | tf_op jit(solution)/shard_map/reduce_scatter | solution.py:1079
  1068.6 2.6 copy-start.29
  1069.5 1.0 copy-start.10
  1075.0 145.4 %reduce-scatter.9.cloned.1.call-start = ((), (), s32[]{:S(2)}) async-start(), calls=%async_computation.17 | async-start | bytes 5242880 | tf_op jit(solution)/shard_map/reduce_scatter | solution.py:1061
  1075.3 4.5 copy-start.18
  1075.3 4.5 copy-start.30
  1079.8 5.7 copy-start.11
  1079.8 5.7 copy-start.14
  1111.3 109.1 %copy-start.22 = (f32[2048]{0:T(1024)S(1)}, f32[2048]{0:T(1024)}, u32[]{:S(2)}) copy-start(f32[2048]{0:T(1024)} %param.17) | copy-start | bytes 24580
  1111.3 109.1 %copy-start.24 = (f32[128,2]{0,1:T(2,128)S(1)}, f32[128,2]{0,1:T(2,128)}, u32[]{:S(2)}) copy-start(f32[128,2]{0,1:T(2,128)} %copy-done.23) | copy-start | bytes 3076
  1220.4 2.0 copy-start.3
  1220.4 2.2 copy-start.7
  1270.9 5.7 copy-start.1
Sparse Core Ops, SparseCore 0:
  9.6 31.7 all-gather.8
  43.9 62.7 all-gather.6
  108.3 29.0 all-gather.10
  138.9 28.5 all-gather.12
  185.3 74.1 all-gather.14
  417.5 50.6 reduce-scatter.6
  706.0 52.1 all-gather.16
  939.2 59.1 reduce-scatter.16
  1058.7 33.4 reduce-scatter.12
  1094.5 34.5 reduce-scatter.10
  1131.5 34.4 reduce-scatter.14
  1169.0 51.3 reduce-scatter.8

commit v3 on v2

--- a/solution.py
+++ b/solution.py
@@ -60,15 +60,16 @@
 
 
 class Relay:
-    def __init__(self, arrays, nz, ny, send_sem, recv_sem):
+    def __init__(self, arrays, nz, ny, send_sem, recv_sem, spread_y=True):
         self.arrays, self.nz, self.ny = arrays, nz, ny
         self.send_sem, self.recv_sem = send_sem, recv_sem
         head, blk = lax.axis_index("head"), lax.axis_index("blk")
-        self.x, self.y = x, y = head % 2, head // 2
+        x, y = head % 2, head // 2 if spread_y else 0
+        self.y = y
         self.core, self.z = core, z = blk % 2, blk // 2
 
         def device(z_at, y_at, core_at):
-            return {"blk": z_at * 2 + core_at, "head": y_at * 2 + x}
+            return {"blk": z_at * 2 + core_at, "head": y_at * 2 + x if spread_y else head}
 
         self.sibling = device(z, y, 1 - core)
         self.targets = [
@@ -76,6 +77,7 @@
             device(z + 1, y, core), device(z - 1, y, core),
         ]
         self.present = [None, y < ny - 1, y > 0, z < nz - 1, z > 0]
+        self.ways = range(5) if spread_y else (0, 3, 4)
         self.pieces = []
         for n, (own, everything, parts) in enumerate(arrays):
             rows = own.shape[0] // parts
@@ -115,7 +117,7 @@
 
     def start(self):
         for piece in range(len(self.pieces)):
-            for way in (3, 4, 1, 2, 0):
+            for way in reversed(self.ways):
                 self.when(self.present[way], lambda way=way, piece=piece: self.copy(
                     self.z, self.y, self.core, piece, way, own=True).start())
 
@@ -143,8 +145,9 @@
     def pass_on(self, z_at, y_at):
         for piece in range(len(self.pieces)):
             self.copy(z_at, y_at, self.core, piece, 0).wait_recv()
-            for way, condition in enumerate(self.conditions(z_at, y_at)):
-                self.when(condition, lambda way=way, piece=piece: self.copy(
+            conditions = self.conditions(z_at, y_at)
+            for way in self.ways:
+                self.when(conditions[way], lambda way=way, piece=piece: self.copy(
                     z_at, y_at, self.core, piece, way).start())
 
     def pass_on_z(self, away):
@@ -154,9 +157,10 @@
     def drain(self):
         def one(index, carry):
             z_at, y_at = index // self.ny, index % self.ny
-            for way, condition in enumerate(self.conditions(z_at, y_at)):
+            conditions = self.conditions(z_at, y_at)
+            for way in self.ways:
                 for piece in range(len(self.pieces)):
-                    self.when(condition, lambda way=way, piece=piece: self.copy(
+                    self.when(conditions[way], lambda way=way, piece=piece: self.copy(
                         z_at, y_at, self.core, piece, way).wait_send())
             return carry
 
@@ -213,7 +217,7 @@
             self.mine, self.from_y, self.from_z,
             self.mine_sem, self.y_send, self.y_recv, self.z_send, self.z_recv,
         ) = scratch
-        self.nz, _, tok, _ = share_ref.shape
+        self.nz, tok = self.mine.shape[:2]
         self.piece = tok // self.parts
         self.step_rows = min(64, self.piece)
         head, blk = lax.axis_index("head"), lax.axis_index("blk")
@@ -235,6 +239,9 @@
             self.mine.at[target, self.cut(part)],
             self.mine_sem.at[target, part],
         )
+
+    def own_wait(self, target, part):
+        self.own_copy(target, part).wait()
 
     def y_copy(self, target, part):
         return pltpu.make_async_remote_copy(
@@ -271,12 +278,15 @@
             if out is None:
                 self.mine[target, here, :] = total.astype(BF16)
             else:
-                out[here, :] = total.astype(BF16)
+                self.store(out, here, total)
+
+    def store(self, out, here, total):
+        out[here, :] = total.astype(out.dtype)
 
     def send(self, turn):
         target = self.targets[turn]
         for part in range(self.parts):
-            self.own_copy(target, part).wait()
+            self.own_wait(target, part)
             self.y_copy(target, part).wait_recv()
             for way in range(2):
                 going = target > self.z if way == 0 else target < self.z
@@ -297,7 +307,7 @@
     def finish(self):
         z, has = self.z, self.has
         for part in range(self.parts):
-            self.own_copy(z, part).wait()
+            self.own_wait(z, part)
             self.y_copy(z, part).wait_recv()
             for way in range(2):
                 pl.when(has[way])(lambda way=way, part=part: self.z_copy(way, z, part).wait_recv())
@@ -315,6 +325,39 @@
         for target in self.targets[:-1]:
             for part in range(self.parts):
                 self.z_copy(0, target, part).wait_send()
+
+
+class TileReturn(Return):
+    def __init__(self, give_ref, out_refs, scratch):
+        super().__init__(give_ref, out_refs, scratch)
+        blk = lax.axis_index("blk")
+        self.core = blk % 2
+        self.beside = {"blk": blk + 1 - 2 * self.core, "head": lax.axis_index("head")}
+
+    @classmethod
+    def scratch(cls, nz, tok, width):
+        return [pltpu.VMEM((nz, tok, width), BF16)] + super().scratch(nz, tok, width)
+
+    def own_copy(self, target, part):
+        return None
+
+    def own_wait(self, target, part):
+        pass
+
+    def y_copy(self, target, part):
+        return pltpu.make_async_remote_copy(
+            src_ref=self.share_ref.at[target, self.cut(part)],
+            dst_ref=self.from_y.at[target, self.cut(part)],
+            send_sem=self.y_send.at[target, part],
+            recv_sem=self.y_recv.at[target, part],
+            device_id=self.beside,
+            device_id_type=pl.DeviceIdType.MESH,
+        )
+
+    def store(self, out, here, total):
+        size = total.shape[1] // len(out)
+        for n, ref in enumerate(out):
+            ref[here, :] = total[:, n * size : (n + 1) * size]
 
 
 def attend_forward(bias, qkv, cots, table, swaps, nz, ny, scale, share, collective_id):
@@ -837,6 +880,370 @@
     )(shares)
 
 
+def project_forward(normed, weights, gains, swaps, nh, nb, seqs, share, collective_id):
+    tok, width = normed.shape
+    tile, columns = weights[0].shape
+    heads = columns // HEAD_DIM
+    items = seqs * heads
+    piece = tok // seqs
+    span = nh * piece
+    rows = nh * tok
+    nz = nb // 2
+    lots = nh * seqs
+    count = len(swaps)
+
+    def kernel(normed_ref, wq_ref, wk_ref, wv_ref, gain_ref, *refs):
+        swap_in, refs = refs[:count], refs[count:]
+        out_ref, qraw_ref, kraw_ref, inv_ref, group_ref, *refs = refs
+        all_refs, refs = refs[:3], refs[3:]
+        swap_out, refs = refs[:count], refs[count:]
+        (
+            vraw_ref, give_ref, sum_ref, norm_send, norm_recv, relay_send, relay_recv,
+            sum_send, sum_recv, give_send, give_recv, swap_send, swap_recv,
+        ) = refs
+        head, blk = lax.axis_index("head"), lax.axis_index("blk")
+        own_refs = (wq_ref, wk_ref, wv_ref)
+        relay = Relay(
+            [(own, everything, 1) for own, everything in zip(own_refs, all_refs)],
+            nz, 1, relay_send, relay_recv, spread_y=False,
+        )
+        z, core = relay.z, relay.core
+        swap = Swap(list(zip(swap_in, swap_out)), swap_send, swap_recv)
+        others = [lax.rem(head + k, nh) for k in range(1, nh)]
+        devices = [{"blk": blk, "head": other} for other in others]
+        blks = [lax.rem(blk + k, nb) for k in range(1, nb)]
+        greet(
+            [(device, None) for device in devices]
+            + [({"blk": other, "head": head}, None) for other in blks]
+        )
+        relay.start()
+
+        def lines(slot):
+            return pl.ds(pl.multiple_of(slot * tok, tok), tok)
+
+        def norm_copy(k, slot):
+            return pltpu.make_async_remote_copy(
+                src_ref=normed_ref,
+                dst_ref=group_ref.at[lines(slot)],
+                send_sem=norm_send.at[k],
+                recv_sem=norm_recv.at[slot],
+                device_id=devices[k],
+                device_id_type=pl.DeviceIdType.MESH,
+            )
+
+        def sum_copy(k, slot):
+            return pltpu.make_async_remote_copy(
+                src_ref=sum_ref.at[slot],
+                dst_ref=sum_ref.at[slot],
+                send_sem=sum_send.at[k],
+                recv_sem=sum_recv.at[slot],
+                device_id=devices[k],
+                device_id_type=pl.DeviceIdType.MESH,
+            )
+
+        def give_copy(k, n, slot):
+            return pltpu.make_async_remote_copy(
+                src_ref=give_ref.at[blks[k] // share, n],
+                dst_ref=out_ref.at[slot, n],
+                send_sem=give_send.at[k, n],
+                recv_sem=give_recv.at[slot, n],
+                device_id={"blk": blks[k], "head": head},
+                device_id_type=pl.DeviceIdType.MESH,
+            )
+
+        for k in range(nh - 1):
+            norm_copy(k, head).start()
+        swap.start()
+        group_ref[lines(head), :] = normed_ref[...]
+        for own, everything in zip(own_refs, all_refs):
+            everything[z, core, 0] = own[...]
+
+        raws = (qraw_ref, kraw_ref, vraw_ref)
+
+        def multiply(rank):
+            at = nearest(z, rank, nz)
+            relay.arrived(at, 0, 1 - core)
+            cols = pl.ds(pl.multiple_of(at * 2 * tile, 2 * tile), 2 * tile)
+            for n in (2, 0, 1):
+                product = mm(group_ref[:, cols], all_refs[n][at].reshape(2 * tile, columns))
+                if rank == 0:
+                    raws[n][...] = product
+                else:
+                    raws[n][...] += product
+
+        for away in range(1, nz - 1):
+            relay.pass_on_z(away)
+        for k in range(nh - 1):
+            norm_copy(k, others[k]).wait_recv()
+        for rank in range(nz - 1):
+            multiply(rank)
+        relay.pass_on_z(nz - 1)
+        multiply(nz - 1)
+
+        def place(n, lot, hl):
+            at, s = lot // seqs, lot % seqs
+            return give_ref.at[s * heads + hl, n, pl.ds(at * piece, piece)]
+
+        for lot in range(lots):
+            here = slice(lot * piece, (lot + 1) * piece)
+            for hl in range(heads):
+                cols = slice(hl * HEAD_DIM, (hl + 1) * HEAD_DIM)
+                place(2, lot, hl)[...] = vraw_ref[here, cols].astype(BF16)
+            for n in range(2):
+                total = jnp.zeros((piece, HEAD_DIM), F32)
+                for hl in range(heads):
+                    raw = raws[n][here, hl * HEAD_DIM : (hl + 1) * HEAD_DIM]
+                    total = total + raw * raw
+                sum_ref[head, n * lots + lot : n * lots + lot + 1, :] = jnp.sum(
+                    total.T, axis=0, keepdims=True
+                )
+        for k in range(nh - 1):
+            sum_copy(k, head).start()
+        for k in range(nb - 1):
+            give_copy(k, 2, blk).start()
+        for k in range(nh - 1):
+            sum_copy(k, others[k]).wait_recv()
+        total_sums = sum_ref[0]
+        for slot in range(1, nh):
+            total_sums = total_sums + sum_ref[slot]
+        inv_ref[...] = lax.rsqrt(total_sums / width + EPSILON)
+        for n in range(2):
+            for lot in range(lots):
+                here = slice(lot * piece, (lot + 1) * piece)
+                row = inv_ref[n * lots + lot : n * lots + lot + 1, :]
+                inv = jnp.broadcast_to(row, (HEAD_DIM, piece)).T
+                for hl in range(heads):
+                    cols = slice(hl * HEAD_DIM, (hl + 1) * HEAD_DIM)
+                    place(n, lot, hl)[...] = (
+                        raws[n][here, cols] * inv * gain_ref[n : n + 1, cols]
+                    ).astype(BF16)
+            for k in range(nb - 1):
+                give_copy(k, n, blk).start()
+        for n in range(3):
+            out_ref[blk, n] = give_ref[blk // share, n]
+        for n in (2, 0, 1):
+            for k in range(nb - 1):
+                give_copy(k, n, blks[k]).wait_recv()
+                give_copy(k, n, blk).wait_send()
+        for k in range(nh - 1):
+            norm_copy(k, head).wait_send()
+            sum_copy(k, head).wait_send()
+        swap.wait()
+        relay.drain()
+
+    anywhere = pl.BlockSpec(memory_space=pl.ANY)
+    inside = pl.BlockSpec(memory_space=pltpu.VMEM)
+    out = pl.pallas_call(
+        kernel,
+        in_specs=[inside] * 5 + [anywhere] * count,
+        out_specs=[inside] * 8 + [anywhere] * count,
+        out_shape=[
+            jax.ShapeDtypeStruct((nb, 3, span, HEAD_DIM), BF16),
+            jax.ShapeDtypeStruct((rows, columns), F32),
+            jax.ShapeDtypeStruct((rows, columns), F32),
+            jax.ShapeDtypeStruct((2 * lots, piece), F32),
+            jax.ShapeDtypeStruct((rows, width), BF16),
+        ]
+        + [jax.ShapeDtypeStruct((nz, 2, 1, tile, columns), BF16)] * 3
+        + [jax.ShapeDtypeStruct(v.shape, v.dtype) for v in swaps],
+        scratch_shapes=[
+            pltpu.VMEM((rows, columns), F32),
+            pltpu.VMEM((items, 3, span, HEAD_DIM), BF16),
+            pltpu.VMEM((nh, 2 * lots, piece), F32),
+            pltpu.SemaphoreType.DMA((nh - 1,)),
+            pltpu.SemaphoreType.DMA((nh,)),
+            pltpu.SemaphoreType.DMA((5, nz, 3)),
+            pltpu.SemaphoreType.DMA((2, nz, 3)),
+            pltpu.SemaphoreType.DMA((nh - 1,)),
+            pltpu.SemaphoreType.DMA((nh,)),
+            pltpu.SemaphoreType.DMA((nb - 1, 3)),
+            pltpu.SemaphoreType.DMA((nb, 3)),
+            pltpu.SemaphoreType.DMA((count,)),
+            pltpu.SemaphoreType.DMA((count,)),
+        ],
+        compiler_params=pltpu.CompilerParams(
+            collective_id=collective_id, has_side_effects=True, vmem_limit_bytes=VMEM_BYTES
+        ),
+        name="project_forward",
+    )(normed, *weights, gains, *swaps)
+    gathered = [v.reshape(width, columns) for v in out[5:8]]
+    return out[0], out[1:3], out[3], out[4], gathered, out[8:]
+
+
+def project_backward(grads, raws, invs, gains, group, weights, nh, nb, collective_id):
+    rows, width = group.shape
+    columns = raws[0].shape[1]
+    items = grads.shape[0]
+    heads = columns // HEAD_DIM
+    seqs = items // heads
+    tok = rows // nh
+    piece = tok // seqs
+    nz = nb // 2
+    tile = width // nb
+    lots = nh * seqs
+    chunk = min(512, width)
+
+    def kernel(grad_ref, qraw_ref, kraw_ref, inv_ref, gain_ref, group_ref, wq_ref, wk_ref, wv_ref, *refs):
+        out_ref, *refs = refs
+        tile_refs, refs = refs[:3], refs[3:]
+        qk_ref, product_ref, *refs = refs
+        d_ref, sum_ref, part_ref, got_ref, sum_send, sum_recv, part_send, part_recv, *refs = refs
+        give = refs[0]
+        back = TileReturn(give, tile_refs, refs[1:])
+        head, blk = lax.axis_index("head"), lax.axis_index("blk")
+        core, z = back.core, back.z
+        others = [lax.rem(head + k, nh) for k in range(1, nh)]
+        devices = [{"blk": blk, "head": other} for other in others]
+
+        def sum_copy(k, slot):
+            return pltpu.make_async_remote_copy(
+                src_ref=sum_ref.at[slot],
+                dst_ref=sum_ref.at[slot],
+                send_sem=sum_send.at[k],
+                recv_sem=sum_recv.at[slot],
+                device_id=devices[k],
+                device_id_type=pl.DeviceIdType.MESH,
+            )
+
+        def part_copy(k, slot):
+            return pltpu.make_async_remote_copy(
+                src_ref=part_ref.at[k],
+                dst_ref=got_ref.at[slot],
+                send_sem=part_send.at[k],
+                recv_sem=part_recv.at[slot],
+                device_id=devices[k],
+                device_id_type=pl.DeviceIdType.MESH,
+            )
+
+        def grad_tile(n, lot, hl):
+            at, s = lot // seqs, lot % seqs
+            return grad_ref[s * heads + hl, n, at * piece : (at + 1) * piece, :]
+
+        def upright(row):
+            return jnp.broadcast_to(row, (HEAD_DIM, piece)).T
+
+        for lot in range(lots):
+            here = slice(lot * piece, (lot + 1) * piece)
+            for n, raw_ref in enumerate((qraw_ref, kraw_ref)):
+                total = jnp.zeros((piece, HEAD_DIM), F32)
+                for hl in range(heads):
+                    cols = slice(hl * HEAD_DIM, (hl + 1) * HEAD_DIM)
+                    gained = grad_tile(n, lot, hl).astype(F32) * gain_ref[n : n + 1, cols]
+                    total = total + gained * raw_ref[here, cols]
+                sum_ref[head, n * lots + lot : n * lots + lot + 1, :] = jnp.sum(
+                    total.T, axis=0, keepdims=True
+                )
+        greet([(device, None) for device in devices] + back.peers())
+        for k in range(nh - 1):
+            sum_copy(k, head).start()
+        for lot in range(lots):
+            here = slice(lot * piece, (lot + 1) * piece)
+            for hl in range(heads):
+                cols = slice(2 * columns + hl * HEAD_DIM, 2 * columns + (hl + 1) * HEAD_DIM)
+                d_ref[here, cols] = grad_tile(2, lot, hl)
+        for k in range(nh - 1):
+            sum_copy(k, others[k]).wait_recv()
+        total_sums = sum_ref[0]
+        for slot in range(1, nh):
+            total_sums = total_sums + sum_ref[slot]
+        for n, raw_ref in enumerate((qraw_ref, kraw_ref)):
+            gain_total = [jnp.zeros((1, HEAD_DIM), F32) for _ in range(heads)]
+            for lot in range(lots):
+                here = slice(lot * piece, (lot + 1) * piece)
+                index = slice(n * lots + lot, n * lots + lot + 1)
+                inv = upright(inv_ref[index, :])
+                lean = inv * inv * inv * (upright(total_sums[index, :]) / width)
+                for hl in range(heads):
+                    cols = slice(hl * HEAD_DIM, (hl + 1) * HEAD_DIM)
+                    grad = grad_tile(n, lot, hl).astype(F32)
+                    raw = raw_ref[here, cols]
+                    gain_total[hl] = gain_total[hl] + jnp.sum(grad * raw * inv, axis=0, keepdims=True)
+                    d_ref[here, n * columns + hl * HEAD_DIM : n * columns + (hl + 1) * HEAD_DIM] = (
+                        inv * (grad * gain_ref[n : n + 1, cols]) - raw * lean
+                    ).astype(BF16)
+            for hl in range(heads):
+                qk_ref[n : n + 1, hl * HEAD_DIM : (hl + 1) * HEAD_DIM] = gain_total[hl]
+
+        edge = jnp.logical_or(z == 0, z == nz - 1)
+        inner = jnp.logical_not(edge)
+        for turn, target in enumerate(back.targets):
+            for at, dest in ((1 - core, give), (core, back.mine)):
+                cols = pl.ds(pl.multiple_of((target * 2 + at) * tile, tile), tile)
+                dest[target] = mm(group_ref[:, cols], d_ref[...], TN).astype(BF16)
+            for part in range(back.parts):
+                back.y_copy(target, part).start()
+            if turn < nz - 1:
+                pl.when(edge)(lambda turn=turn: back.send(turn))
+
+        product_ref[...] = jnp.zeros_like(product_ref)
+
+        def partial(at, store):
+            lines = pl.ds(pl.multiple_of(at * tok, tok), tok)
+            for col in range(0, width, chunk):
+                cols = slice(col, col + chunk)
+                total = mm(d_ref[lines, 0:columns], wq_ref[cols, :], NT)
+                total = total + mm(d_ref[lines, columns : 2 * columns], wk_ref[cols, :], NT)
+                total = total + mm(d_ref[lines, 2 * columns : 3 * columns], wv_ref[cols, :], NT)
+                product_ref[:, cols] += jnp.sum(
+                    total * group_ref[lines, cols].astype(F32), axis=0, keepdims=True
+                )
+                store(cols, total)
+
+        sent = 0
+        for k in range(nh - 1):
+
+            def keep(cols, total, k=k):
+                part_ref[k, :, cols] = total.astype(BF16)
+
+            partial(others[k], keep)
+            part_copy(k, head).start()
+            while sent < nz - 1 and (k + 1) * (nz - 1) >= (sent + 2) * (nh - 1):
+                pl.when(inner)(lambda turn=sent: back.send(turn))
+                sent += 1
+
+        def keep_own(cols, total):
+            out_ref[:, cols] = total
+
+        partial(head, keep_own)
+        for turn in range(sent, nz - 1):
+            pl.when(inner)(lambda turn=turn: back.send(turn))
+        for k in range(nh - 1):
+            part_copy(k, others[k]).wait_recv()
+            for r in range(0, tok, 64):
+                here = pl.ds(r, 64)
+                out_ref[here, :] += got_ref[others[k], here, :].astype(F32)
+        back.finish()
+        for k in range(nh - 1):
+            sum_copy(k, head).wait_send()
+            part_copy(k, head).wait_send()
+
+    inside = pl.BlockSpec(memory_space=pltpu.VMEM)
+    out = pl.pallas_call(
+        kernel,
+        in_specs=[inside] * 9,
+        out_specs=[inside] * 6,
+        out_shape=[jax.ShapeDtypeStruct((tok, width), F32)]
+        + [jax.ShapeDtypeStruct((tile, columns), F32)] * 3
+        + [jax.ShapeDtypeStruct((2, columns), F32), jax.ShapeDtypeStruct((1, width), F32)],
+        scratch_shapes=[
+            pltpu.VMEM((rows, 3 * columns), BF16),
+            pltpu.VMEM((nh, 2 * lots, piece), F32),
+            pltpu.VMEM((nh - 1, tok, width), BF16),
+            pltpu.VMEM((nh, tok, width), BF16),
+            pltpu.SemaphoreType.DMA((nh - 1,)),
+            pltpu.SemaphoreType.DMA((nh,)),
+            pltpu.SemaphoreType.DMA((nh - 1,)),
+            pltpu.SemaphoreType.DMA((nh,)),
+        ]
+        + TileReturn.scratch(nz, tile, 3 * columns),
+        compiler_params=pltpu.CompilerParams(
+            collective_id=collective_id, has_side_effects=True, vmem_limit_bytes=VMEM_BYTES
+        ),
+        name="project_backward",
+    )(grads, *raws, invs, gains, group, *weights)
+    return out[0], out[1:4], out[4], out[5]
+
+
 def local(
     hidden_in,
     attn_gain,
@@ -889,7 +1296,6 @@
     def flip_blk(values, bit):
         return lax.ppermute(values, "blk", [(b, b ^ bit) for b in range(blk_count)])
 
-    gate_other = flip_head(w_gate[0], 1)
 
     table = jnp.concatenate([own_rows(routes).astype(F32).T, own_rows(gate_weights).T], axis=0)
 
@@ -899,25 +1305,14 @@
 
     inv_one = inverse_rms(hidden_f)
     normed = (hidden_f * inv_one * attn_gain).astype(BF16)
-    group = lax.all_gather(normed, "head", axis=0, tiled=True)
-    query_cols = lax.all_gather(w_query, "blk", axis=0, tiled=True)
-    key_cols = lax.all_gather(w_key, "blk", axis=0, tiled=True)
-    value_cols = lax.all_gather(w_value, "blk", axis=0, tiled=True)
-    out_w = lax.all_gather(w_out, "blk", axis=1, tiled=True)
-
-    query_raw = mm(group, query_cols)
-    key_raw = mm(group, key_cols)
-    value_raw = mm(group, value_cols)
-    square_sums = lax.psum(
-        jnp.stack([jnp.sum(query_raw * query_raw, -1), jnp.sum(key_raw * key_raw, -1)]), "head"
-    )
-    inv_query = lax.rsqrt(square_sums[0][:, None] / width + EPSILON)
-    inv_key = lax.rsqrt(square_sums[1][:, None] / width + EPSILON)
     gain_query = lax.dynamic_slice_in_dim(query_gain, head_index * columns, columns)
     gain_key = lax.dynamic_slice_in_dim(key_gain, head_index * columns, columns)
-    query_n = (query_raw * inv_query * gain_query).astype(BF16)
-    key_n = (key_raw * inv_key * gain_key).astype(BF16)
-    value_n = value_raw.astype(BF16)
+    qk_gains = jnp.stack([gain_query, gain_key])
+    out_w = lax.all_gather(w_out, "blk", axis=1, tiled=True)
+    qkv, raws, invs, group, qkv_cols, (gate_other,) = project_forward(
+        normed, (w_query, w_key, w_value), qk_gains, (w_gate[0],), head_count, blk_count, seqs,
+        share, 5,
+    )
 
     def to_items(values):
         parts = values.reshape(head_count, seqs, piece, heads_here, HEAD_DIM)
@@ -935,9 +1330,6 @@
 
     item = blk_index // share
     starts = lax.dynamic_index_in_dim(block_starts, item // heads_here, 0, keepdims=False)
-    qkv = jnp.stack([to_items(query_n), to_items(key_n), to_items(value_n)], axis=1)
-    qkv, gate_other = lax.optimization_barrier((qkv, gate_other))
-    qkv = swap(qkv)
     qkv = qkv.reshape(blk_count, 3, per, BLOCK, HEAD_DIM)
     total_blocks = blk_count * per
     key_block = jnp.arange(total_blocks, dtype=jnp.int32)
@@ -1033,38 +1425,15 @@
     else:
         expert_sum = give_back(give_back(moe_share.swapaxes(0, 1), y_bits), z_bits)
     result = middle + expert_sum
-    grad_query_n = rounded(from_items(grad_qkv[:, 0]))
-    grad_key_n = rounded(from_items(grad_qkv[:, 1]))
-    grad_value_b = from_items(grad_qkv[:, 2]).astype(BF16)
-    gained_query = grad_query_n * gain_query
-    gained_key = grad_key_n * gain_key
-    row_sums = lax.psum(
-        jnp.stack([jnp.sum(gained_query * query_raw, -1), jnp.sum(gained_key * key_raw, -1)]),
-        "head",
+    if share > 1:
+        grad_qkv = grad_qkv.reshape(items, share, 3, span, HEAD_DIM).astype(F32).sum(1).astype(BF16)
+    grad_normed, (grad_query, grad_key, grad_value), qk_parts, product = project_backward(
+        grad_qkv, raws, invs, qk_gains, group, qkv_cols, head_count, blk_count, 4
     )
-    grad_query_b = (
-        inv_query * gained_query
-        - query_raw * inv_query * inv_query * inv_query * row_sums[0][:, None] / width
-    ).astype(BF16)
-    grad_key_b = (
-        inv_key * gained_key
-        - key_raw * inv_key * inv_key * inv_key * row_sums[1][:, None] / width
-    ).astype(BF16)
-    query_gain_part = jnp.sum(grad_query_n * query_raw * inv_query, 0)
-    key_gain_part = jnp.sum(grad_key_n * key_raw * inv_key, 0)
-    total = (
-        mm(grad_query_b, query_cols, NT)
-        + mm(grad_key_b, key_cols, NT)
-        + mm(grad_value_b, value_cols, NT)
-    )
-    grad_normed = rounded(
-        lax.psum_scatter(total.astype(BF16), "head", scatter_dimension=0, tiled=True).astype(F32)
-    )
-    query_part = mm(group, grad_query_b, TN)
-    key_part = mm(group, grad_key_b, TN)
-    value_part = mm(group, grad_value_b, TN)
+    grad_normed = rounded(grad_normed)
+    query_gain_part, key_gain_part = qk_parts[0], qk_parts[1]
     gained_one = grad_normed * attn_gain
-    attn_gain_part = jnp.sum(grad_normed * hidden_f * inv_one, 0)
+    attn_gain_part = product[0] / attn_gain
     grad_hidden_in = (
         grad_middle
         + inv_one * gained_one
@@ -1080,9 +1449,6 @@
             values.astype(BF16), "blk", scatter_dimension=dim, tiled=True
         ).astype(F32)
 
-    grad_query = over_blk(query_part, 0)
-    grad_key = over_blk(key_part, 0)
-    grad_value = over_blk(value_part, 0)
     grad_out = over_blk(out_part, 1)
     zero_width = jnp.zeros((width,), F32)
     query_gain_full = lax.dynamic_update_slice_in_dim(
@@ -1094,10 +1460,15 @@
     square_parts = jnp.stack(
         [jnp.sum(result * result), jnp.sum(branch * branch), jnp.sum(expert_sum * expert_sum)]
     )
-    totals = lax.psum(
-        (square_parts, attn_gain_part, ffn_gain_part, query_gain_full, key_gain_full),
-        everyone,
-    )
+    stacked = jnp.concatenate(
+        [attn_gain_part, ffn_gain_part, query_gain_full, key_gain_full, jnp.pad(square_parts, (0, 125))]
+    ).reshape(-1, 128)
+    for axis in ("head", "blk"):
+        stacked = jnp.sum(lax.all_gather(stacked, axis, axis=0, tiled=False), 0)
+    stacked = stacked.reshape(-1)
+    totals = [stacked[4 * width : 4 * width + 3]] + [
+        stacked[n * width : (n + 1) * width] for n in range(4)
+    ]
     entry_count = tok * width * devices
     stream_stats = jnp.sqrt(totals[0] / entry_count + EPSILON)
     return (

time: 1290 us -> 1070 us (0.83)
  waiting for transfers between devices: 434 us -> 122 us
  Pallas kernels: 462 us -> 693 us
  matrix products: 123 us -> 74.4 us
  blocking collectives: 121 us -> 83.9 us
  local copies, waits for them, and re-layouts: 50.9 us -> 22.3 us
  other arithmetic: 63.1 us -> 42.8 us
    pallas_call x0 -> x2, Pallas kernels: none -> 223 us  [the longest x1 145 us: project_forward(): pl.pallas_call(kernel, in_specs=[inside] * 5 + [anywhere] * count, out_sp...]
    all_gather x4 -> x0, waiting for transfers between devices: 111 us -> none  [the longest x1 65.2 us: local(): group = lax.all_gather(normed, 'head', axis=0, tiled=True)]
    all_to_all x2 -> x1, waiting for transfers between devices: 128 us -> 23.1 us  [swap(): lax.all_to_all(values, 'blk', split_axis=0, concat_axis=0, tiled=True)]
    psum x3 -> x0, blocking collectives: 60.2 us -> none  [the longest x1 40.7 us: local(): lax.psum((square_parts, attn_gain_part, ffn_gain_part, query_gain_full, k...]
    reduce_scatter x1 -> x0, waiting for transfers between devices: 52.7 us -> none  [local(): lax.psum_scatter(total.astype(BF16), 'head', scatter_dimension=0, tiled=T...]
    dot_general x18 -> x9, matrix products: 123 us -> 74.2 us  [mm(): return lax.dot_general(left, right, dims, preferred_element_type=F32)]
    ppermute x2 -> x1, waiting for transfers between devices: 40.6 us -> 0.01 us  [flip_head(): lax.ppermute(values, 'head', [(h, h ^ bit) for h in range(head_count)])]
    all_gather x0 -> x2, blocking collectives: none -> 22.5 us  [local(): stacked = jnp.sum(lax.all_gather(stacked, axis, axis=0, tiled=False), 0)]
  transfers between devices with their start and end apart: 16 -> 6, of which waited for: 10 -> 3; matrix products, arithmetic and copies ran while one was open for 15% -> 8% of each run, Pallas kernels for 8% -> 25%
where the time goes in v3:
time: 1070 us; the launch traced here: 1060 us
  Pallas kernels  693 us (65%)
  waiting for transfers between devices  122 us (11%)
  blocking collectives  83.9 us (8%)
  matrix products  74.4 us (7%)
  other arithmetic  42.8 us (4%)
  local copies, waits for them, and re-layouts  22.3 us (2%)
  between operations  14.4 us (1%)
    pallas_call x1, Pallas kernels, project_forward(): pl.pallas_call(kernel, in_specs=[inside] * 5 + [anywhere] * count, out_sp...  145 us
    pallas_call x1, Pallas kernels, expert_exchange(): pl.pallas_call(kernel, in_specs=[anywhere, inside, inside] + [anywhere] *...  134 us
    pallas_call x1, Pallas kernels, attend_backward(): pl.pallas_call(kernel, in_specs=[pl.BlockSpec(memory_space=pltpu.SMEM)] +...  125 us
    pallas_call x1, Pallas kernels, attend_forward(): pl.pallas_call(kernel, in_specs=[pl.BlockSpec(memory_space=pltpu.SMEM), i...  115 us
    pallas_call x1, Pallas kernels, return_sum(): pl.pallas_call(kernel, in_specs=[pl.BlockSpec(memory_space=pl.ANY)], out_...  95.3 us
    pallas_call x1, Pallas kernels, project_backward(): pl.pallas_call(kernel, in_specs=[inside] * 9, out_specs=[inside] * 6, out...  77.7 us
    dot_general x9, matrix products, mm(): return lax.dot_general(left, right, dims, preferred_element_type=F32)  74.2 us
    all_to_all x2, blocking collectives, swap(): lax.all_to_all(values, 'blk', split_axis=0, concat_axis=0, tiled=True)  61.4 us
  transfers between devices with their start and end apart: 6, of which 3 were waited for; matrix products, arithmetic and copies ran while one was open for 8% of the time, Pallas kernels for 25%

profile of v3, /device:TPU:0, one launch (start us, length us, event | category | flops | bytes accessed | tf_op | source)
XLA Modules:
  0.0 1057.9 jit_solution(2994073298697926138)
XLA Ops:
  7.2 0.7 all-gather.5.cloned.1.call-update
  8.1 0.6 select_n.49.bias_ref
  8.7 0.8 dynamic_slice.11
  9.5 0.8 dynamic_slice.12
  10.3 2.4 convert_bitcast_fusion
  12.7 1.2 copy.59
  14.0 1.2 fusion.21
  15.2 1.3 copy.61
  16.6 0.6 pad_maximum_fusion.1.gain_ref
  17.2 1.2 multiply_convert_fusion.1.normed_ref
  18.4 145.4 %project_forward.1 = (bf16[8,3,512,128]{3,2,1,0:T(8,128)(2,1)}, f32[1024,512]{1,0:T(8,128)}, f32[1024,512]{1,0:T(8,128)}, f32[16,128]{1,0:T(8,128)}, bf16[1024,2...) custom-call(bf16[256,2048]{1,0:T(8,128)(2,1)} %multiply_convert_fusi, ...), custom_call_target="tpu_custom_call" | custom-call | tf_op jit(solution)/shard_map/project_forward/pallas_call | solution.py:1036
  163.9 0.6 pad_maximum_fusion.table_ref
  164.5 114.7 %attend_forward.1 = (bf16[16,256,128]{2,1,0:T(8,128)(2,1)}, f32[16,128,256]{2,1,0:T(8,128)}, f32[16,1,256]{2,1,0:T(1,128)}, bf16[4,2,2,256,2048]{4,3,2,1,0:T(8,1...) custom-call(f32[256]{0:T(256)} %select_n.49.bias_ref, ...), custom_call_target="tpu_custom_call" | custom-call | tf_op jit(solution)/shard_map/attend_forward/pallas_call | solution.py:461
  279.2 30.8 %all_to_all.15 = bf16[8,512,128]{2,1,0:T(8,128)(2,1)S(1)} all-to-all(bf16[8,512,128]{2,1,0:T(8,128)(2,1)} %bitcast.127), channel_id=1, replica_groups=mesh['head'=4,'blk'=8] {'blk'}, dimensions={0} | all-to-all | bytes 2097152 | tf_op jit(solution)/shard_map/all_to_all | solution.py:1329
  310.0 0.8 copy.62
  310.9 6.3 convolution_convert_fusion
  317.3 0.9 copy-done.14
  318.3 0.1 convolution_convert_fusion.3
  318.5 0.6 broadcast_in_dim.55.gate_ref
  319.1 0.6 copy_select_fusion.slot_ref
  319.7 48.4 %reduce-scatter.3.cloned.1.call-done = bf16[256,2048]{1,0:T(8,128)(2,1)} async-done(((bf16[1024,2048]{1,0:T(8,128)(2,1)}), bf16[256,2048]{1,0:T(8,128)(2,1)}) %reduce-scatter.3.cloned.1.call-update) | async-done | bytes 1048592 | tf_op jit(solution)/shard_map/reduce_scatter | solution.py:1353
  368.1 2.7 multiply_reduce_fusion.1
  370.8 1.4 multiply_convert_fusion.own_ref
  372.2 134.2 %expert_exchange.1 = (bf16[4,2,256,2048]{3,2,1,0:T(8,128)(2,1)}, bf16[4,2,256,2048]{3,2,1,0:T(8,128)(2,1)}, bf16[8,320,2048]{2,1,0:T(8,128)(2,1)}, bf16[8,320,20...) custom-call(bf16[256,2048]{1,0:T(8,128)(2,1)} %multiply_convert_fusi, ...), custom_call_target="tpu_custom_call" | custom-call | tf_op jit(solution)/shard_map/expert_exchange/pallas_call | solution.py:814
  506.4 95.3 %return_sum.1 = bf16[256,2048]{1,0:T(8,128)(2,1)} custom-call(bf16[4,2,256,2048]{3,2,1,0:T(8,128)(2,1)} %get-tuple-element.64.share_ref), custom_call_target="tpu_custom_call" | custom-call | tf_op jit(solution)/shard_map/return_sum/pallas_call | solution.py:870
  601.7 2.0 fusion.19
  603.8 1.9 fusion.37
  605.7 11.7 %fusion.refs_1_ = bf16[2048,512]{1,0:T(8,128)(2,1)} fusion(bf16[2560,2048]{1,0:T(8,128)(2,1)} %bitcast.140, bf16[2560,2048]{1,0:T(8,128)(2,1)} %bitcast.146), kind=kOutput, calls=%fused_computation.13 | convolution fusion | flops 5368709120 | bytes 15204352 | tf_op jit(solution)/shard_map/dot_general | solution.py:24
  617.4 10.3 fusion.4
  627.7 10.6 fusion.10
  638.3 7.3 fusion.2.refs_0_
  645.6 8.0 fusion.6
  653.6 7.6 fusion.8
  661.2 6.3 convolution_convert_fusion.2
  667.5 2.1 reshape.173
  669.6 1.5 copy.65
  671.1 30.6 %all_to_all.16 = bf16[8,512,128]{2,1,0:T(8,128)(2,1)} all-to-all(bf16[8,512,128]{2,1,0:T(8,128)(2,1)S(1)} %bitcast.119), channel_id=1, replica_groups=mesh['head'=4,'blk'=8] {'blk'}, dimensions={0} | all-to-all | bytes 2097152 | tf_op jit(solution)/shard_map/all_to_all | solution.py:1329
  701.6 125.4 %attend_backward.1 = (bf16[8,3,2,256,128]{4,3,2,1,0:T(8,128)(2,1)}, bf16[2048,512]{1,0:T(8,128)(2,1)}, bf16[2048,512]{1,0:T(8,128)(2,1)}, bf16[256,2048]{1,0:T(8,128)(2,1)}) custom-call(f32[256]{0:T(256)} %select_n.49.bias_ref, bf16[8,3,2,256,128]{4,3,2,1,0:T(8,128)(2,1)} %bitcast.107, bf16[16,256,128]{2,1,0:T(8,128)(2,1)} %bitcast.114, ...), custom_call_target="tpu_custom_call" | custom-call | tf_op jit(solution)/shard_map/attend_backward/pallas_call | solution.py:568
  827.0 4.5 all-to-all-start.2
  831.5 6.3 convolution_convert_fusion.1
  837.8 1.2 collective-permute-start
  839.0 9.5 add_bitcast_fusion.1
  848.5 49.3 %reduce-scatter.5.cloned.1.call-done = bf16[512,256]{1,0:T(8,128)(2,1)} async-done(((bf16[512,2048]{1,0:T(8,128)(2,1)}), bf16[512,256]{1,0:T(8,128)(2,1)}) %reduce-scatter.5.cloned.1.call-update) | async-done | bytes 262160 | tf_op jit(solution)/shard_map/reduce_scatter | solution.py:1448
  897.8 1.8 convert_element_type.120
  899.6 23.1 %all-to-all-done.2.grad_ref = bf16[8,3,512,128]{3,2,1,0:T(8,128)(2,1)} async-done(((bf16[8,3,512,128]{3,2,1,0:T(8,128)(2,1)}), bf16[8,3,512,128]{3,2,1,0:T(8,128)(2,1)}, u32[]{:S(2)}, u32[]{:S(2)}) %all-to-all-start.2) | async-done | bytes 3145760 | tf_op jit(solution)/shard_map/all_to_all | solution.py:1329
  922.7 77.7 %project_backward.1 = (f32[256,2048]{1,0:T(8,128)}, f32[256,512]{1,0:T(8,128)}, f32[256,512]{1,0:T(8,128)}, f32[256,512]{1,0:T(8,128)}, f32[2,512]{1,0:T(2,128)}, /*index=5*/f32[1,2048]{1,0:T(1,128)}) custom-call(bf16[8,3,512,128]{3,2,1,0:T(8,128)(2,1)} %all-to-all-done.2.grad_ref, f32[1024,512]{1,0:T(8,128)} %get-tuple-element.81.qraw_ref, ...), custom_call_target="tpu_custom_call" | custom-call | tf_op jit(solution)/shard_map/project_backward/pallas_call | solution.py:1221
  1000.4 0.7 divide_dynamic-update-slice_fusion
  1001.1 0.8 fusion.38
  1001.9 1.7 convert_element_type.116
  1003.6 1.0 copy-done.5
  1004.6 0.4 fusion.22
  1005.0 0.3 dynamic_update_slice.6
  1005.3 0.3 dynamic_update_slice.7
  1005.6 5.4 multiply_reduce_fusion
  1011.0 2.0 constant_dynamic-update-slice_fusion
  1013.0 8.1 all_gather.17
  1021.1 14.4 %all-gather.1 = f32[8,65,128]{2,1,0:T(8,128)S(1)} all-gather(f32[1,65,128]{2,1,0:T(8,128)S(1)} %bitcast.128), channel_id=2, replica_groups=mesh['head'=4,'blk'=8] {'blk'}, dimensions={0}, use_global_device_ids=true | all-gather | bytes 299520 | tf_op jit(solution)/shard_map/all_gather | solution.py:1467
  1035.6 0.6 slice_bitcast_fusion
  1036.2 0.5 fusion.34
  1036.7 5.9 add_bitcast_fusion
  1042.6 6.1 copy_bitcast_fusion
  1048.8 0.8 copy.94
  1049.6 0.8 copy.95
  1050.4 0.8 copy.96
  (79 shorter events, 0.8 us)
Async XLA Ops:
  7.2 0.8 copy-start
  7.2 303.7 %all-gather.5.cloned.1.call-start = ((), (), s32[]{:S(2)}) async-start(), calls=%async_computation.5 | async-start | bytes 2359296 | tf_op jit(solution)/shard_map/all_gather | solution.py:1311
  7.9 360.2 %reduce-scatter.3.cloned.1.call-start = ((), (), s32[]{:S(2)}) async-start(), calls=%async_computation.6 | async-start | bytes 5242880 | tf_op jit(solution)/shard_map/reduce_scatter | solution.py:1353
  12.7 1.2 copy-start.6
  12.7 2.5 copy-start.9
  14.0 3.2 copy-start.16
  18.4 145.5 %copy-start.17 = (s32[128,2,8]{0,2,1:T(8,128)S(1)}, s32[128,2,8]{0,2,1:T(8,128)}, u32[]{:S(2)}) copy-start(s32[128,2,8]{0,2,1:T(8,128)} %param.28) | copy-start | bytes 24580
  18.4 145.5 %copy-start.18 = (f32[128,2,8]{0,2,1:T(8,128)S(1)}, f32[128,2,8]{0,2,1:T(8,128)}, u32[]{:S(2)}) copy-start(f32[128,2,8]{0,2,1:T(8,128)} %param.29) | copy-start | bytes 24580
  310.8 6.3 copy-start.10
  317.2 1.0 copy-start.14
  317.2 343.9 %all-gather.7.cloned.1.call-start = ((), (), s32[]{:S(2)}) async-start(), calls=%async_computation.7 | async-start | bytes 5242880 | tf_op jit(solution)/shard_map/all_gather | solution.py:1406
  319.7 51.1 %copy-start.15 = (f32[2048]{0:T(1024)S(1)}, f32[2048]{0:T(1024)}, u32[]{:S(2)}) copy-start(f32[2048]{0:T(1024)} %param.24) | copy-start | bytes 24580
  370.8 233.0 %copy-start.2 = (f32[256,2048]{1,0:T(8,128)}, f32[256,2048]{1,0:T(8,128)S(1)}, u32[]{:S(2)}) copy-start(f32[256,2048]{1,0:T(8,128)S(1)} %get-tuple-element.107) | copy-start | bytes 6291460
  601.7 2.1 copy-start.3
  601.7 2.1 copy-start.4
  617.4 20.9 %slice-start = ((s8[10485760]{0:T(1024)(128)(4,1)}), s8[4194304]{0:T(1024)(128)(4,1)S(1)}, s32[]{:S(2)}) async-start(s8[10485760]{0:T(1024)(128)(4,1)} %bitcast.141), calls=%async_computation.9 | async-start | bytes 8388608
  617.4 20.9 %slice-start.1 = ((s8[10485760]{0:T(1024)(128)(4,1)}), s8[4194304]{0:T(1024)(128)(4,1)S(1)}, s32[]{:S(2)}) async-start(s8[10485760]{0:T(1024)(128)(4,1)} %bitcast.141), calls=%async_computation.10 | async-start | bytes 8388608
  617.4 20.9 %slice-start.3 = ((s8[10485760]{0:T(1024)(128)(4,1)}), s8[4194304]{0:T(1024)(128)(4,1)S(1)}, s32[]{:S(2)}) async-start(s8[10485760]{0:T(1024)(128)(4,1)} %bitcast.147), calls=%async_computation.12 | async-start | bytes 8388608
  617.4 20.9 %slice-start.4 = ((s8[10485760]{0:T(1024)(128)(4,1)}), s8[4194304]{0:T(1024)(128)(4,1)S(1)}, s32[]{:S(2)}) async-start(s8[10485760]{0:T(1024)(128)(4,1)} %bitcast.147), calls=%async_computation.13 | async-start | bytes 8388608
  627.7 10.6 %slice-start.2 = ((s8[10485760]{0:T(1024)(128)(4,1)}), s8[2097152]{0:T(1024)(128)(4,1)S(1)}, s32[]{:S(2)}) async-start(s8[10485760]{0:T(1024)(128)(4,1)} %bitcast.141), calls=%async_computation.11 | async-start | bytes 4194304
  627.7 10.6 %slice-start.5 = ((s8[10485760]{0:T(1024)(128)(4,1)}), s8[2097152]{0:T(1024)(128)(4,1)S(1)}, s32[]{:S(2)}) async-start(s8[10485760]{0:T(1024)(128)(4,1)} %bitcast.147), calls=%async_computation.14 | async-start | bytes 4194304
  827.0 95.7 %all-to-all-start.2 = ((bf16[8,3,512,128]{3,2,1,0:T(8,128)(2,1)}), bf16[8,3,512,128]{3,2,1,0:T(8,128)(2,1)}, u32[]{:S(2)}, u32[]{:S(2)}) async-start(bf16[8,3,512,128]{3,2,1,0:T(8,128)(2,1)} %bitcast.120), calls=%async_computation.3 | async-start | bytes 6291456 | tf_op jit(solution)/shard_map/all_to_all | solution.py:1329
  831.5 66.3 %reduce-scatter.5.cloned.1.call-start = ((), (), s32[]{:S(2)}) async-start(), calls=%async_computation.8 | async-start | bytes 2359296 | tf_op jit(solution)/shard_map/reduce_scatter | solution.py:1448
  837.8 61.8 %collective-permute-start = (bf16[512,2048]{1,0:T(8,128)(2,1)}, bf16[512,2048]{1,0:T(8,128)(2,1)}, u32[]{:S(2)}, u32[]{:S(2)}) collective-permute-start(bf16[512,2048]{1,0:T(8,128)(2,1)} %fusion.4), channel_id=1, source_target_pairs={{0,8},{8,0},{16,24},{24,16},{1,9},{9,1},{17,25},{25,17},{2,10},{10... | collective-permute-start | bytes 6291464 | tf_op jit(solution)/shard_map/ppermute | solution.py:1294
  1003.6 1.0 copy-start.5
  1036.7 5.9 copy-start.7
  1036.7 5.9 copy-start.8
  1042.6 6.2 copy-start.13
  1042.6 7.0 copy-start.12
  1042.6 8.5 copy-start.1
  1048.8 1.6 copy-start.11
Sparse Core Ops, SparseCore 0:
  9.6 44.7 all-gather.4
  317.3 50.7 reduce-scatter.2
  605.8 52.1 all-gather.6
  837.9 59.8 reduce-scatter.4

commit v4 on v3

--- a/solution.py
+++ b/solution.py
@@ -195,6 +195,52 @@
             copy.wait()
 
 
+class Deliver:
+    def __init__(self, stage, out_ref, send_sem, recv_sem):
+        self.stage, self.out_ref = stage, out_ref
+        self.send_sem, self.recv_sem = send_sem, recv_sem
+        self.count, self.per = out_ref.shape[:2]
+        self.blk, self.head = lax.axis_index("blk"), lax.axis_index("head")
+        self.others = [lax.rem(self.blk + k, self.count) for k in range(1, self.count)]
+
+    def device(self, blk):
+        return {"blk": blk, "head": self.head}
+
+    def peers(self):
+        return [(self.device(other), None) for other in self.others]
+
+    def copy(self, block, source, owner):
+        at = lax.rem(block, self.per)
+        return pltpu.make_async_remote_copy(
+            src_ref=self.stage.at[block],
+            dst_ref=self.out_ref.at[source, at],
+            send_sem=self.send_sem.at[block],
+            recv_sem=self.recv_sem.at[source, at],
+            device_id=self.device(owner),
+            device_id_type=pl.DeviceIdType.MESH,
+        )
+
+    def send(self, block):
+        owner = block // self.per
+        pl.when(owner != self.blk)(lambda: self.copy(block, self.blk, owner).start())
+
+        @pl.when(owner == self.blk)
+        def _():
+            self.out_ref[self.blk, lax.rem(block, self.per)] = self.stage[block]
+
+    def wait(self):
+        for other in self.others:
+            for at in range(self.per):
+                self.copy(self.blk * self.per + at, other, other).wait_recv()
+
+        def sent(block, carry):
+            owner = block // self.per
+            pl.when(owner != self.blk)(lambda: self.copy(block, self.blk, owner).wait_send())
+            return carry
+
+        lax.fori_loop(0, self.count * self.per, sent, 0)
+
+
 class Return:
     parts = 2
 
@@ -203,12 +249,12 @@
         return [
             pltpu.VMEM((nz, tok, width), BF16),
             pltpu.VMEM((nz, tok, width), BF16),
-            pltpu.VMEM((2, nz, tok, width), BF16),
+            pltpu.VMEM((nz + 1, tok, width), BF16),
             pltpu.SemaphoreType.DMA((nz, cls.parts)),
             pltpu.SemaphoreType.DMA((nz, cls.parts)),
             pltpu.SemaphoreType.DMA((nz, cls.parts)),
             pltpu.SemaphoreType.DMA((nz, cls.parts)),
-            pltpu.SemaphoreType.DMA((2, nz, cls.parts)),
+            pltpu.SemaphoreType.DMA((nz + 1, cls.parts)),
         ]
 
     def __init__(self, share_ref, out_ref, scratch):
@@ -243,6 +289,14 @@
     def own_wait(self, target, part):
         self.own_copy(target, part).wait()
 
+    def y_wait(self, target, part):
+        self.y_copy(target, part).wait_recv()
+
+    def y_drain(self):
+        for target in self.targets:
+            for part in range(self.parts):
+                self.y_copy(target, part).wait_send()
+
     def y_copy(self, target, part):
         return pltpu.make_async_remote_copy(
             src_ref=self.share_ref.at[target, 1 - self.y, self.cut(part)],
@@ -253,12 +307,17 @@
             device_id_type=pl.DeviceIdType.MESH,
         )
 
-    def z_copy(self, way, target, part):
+    def slot(self, way, target, at):
+        return target if way == 0 else jnp.where(target == at, self.nz, target)
+
+    def z_copy(self, way, target, part, at=None):
+        at = (self.z + 1, self.z - 1)[way] if at is None else at
+        slot = self.slot(way, target, at)
         return pltpu.make_async_remote_copy(
             src_ref=self.mine.at[target, self.cut(part)],
-            dst_ref=self.from_z.at[way, target, self.cut(part)],
+            dst_ref=self.from_z.at[slot, self.cut(part)],
             send_sem=self.z_send.at[target, part],
-            recv_sem=self.z_recv.at[way, target, part],
+            recv_sem=self.z_recv.at[slot, part],
             device_id=self.onward[way],
             device_id_type=pl.DeviceIdType.MESH,
         )
@@ -269,12 +328,14 @@
                 self.y_copy(target, part).start()
                 self.own_copy(target, part).start()
 
-    def add(self, target, part, ways, out=None):
+    def add(self, target, part, ways, out=None, beside=True):
         for r in range(part * self.piece, (part + 1) * self.piece, self.step_rows):
             here = pl.ds(r, self.step_rows)
-            total = self.mine[target, here, :].astype(F32) + self.from_y[target, here, :].astype(F32)
+            total = self.mine[target, here, :].astype(F32)
+            if beside and self.from_y is not None:
+                total = total + self.from_y[target, here, :].astype(F32)
             for way in ways:
-                total = total + self.from_z[way, target, here, :].astype(F32)
+                total = total + self.from_z[self.slot(way, target, self.z), here, :].astype(F32)
             if out is None:
                 self.mine[target, here, :] = total.astype(BF16)
             else:
@@ -283,48 +344,106 @@
     def store(self, out, here, total):
         out[here, :] = total.astype(out.dtype)
 
-    def send(self, turn):
+    def send(self, turn, part=None):
+        target = self.targets[turn]
+        for part in range(self.parts) if part is None else (part,):
+            self.own_wait(target, part)
+            self.y_wait(target, part)
+            for way in range(2):
+                going = target > self.z if way == 0 else target < self.z
+
+                @pl.when(going & self.has[way])
+                def _(way=way, part=part):
+                    self.z_copy(way, target, part, self.z).wait_recv()
+                    self.add(target, part, (way,))
+
+                @pl.when(going & jnp.logical_not(self.has[way]))
+                def _(part=part):
+                    self.add(target, part, ())
+
+                @pl.when(going)
+                def _(way=way, part=part):
+                    self.z_copy(way, target, part).start()
+
+    def pair(self, turn):
         target = self.targets[turn]
         for part in range(self.parts):
             self.own_wait(target, part)
-            self.y_copy(target, part).wait_recv()
+            self.y_wait(target, part)
+            self.add(target, part, ())
             for way in range(2):
-                going = target > self.z if way == 0 else target < self.z
-
-                @pl.when(going & self.has[way])
+                first = (target > self.z if way == 0 else target < self.z) & jnp.logical_not(
+                    self.has[way]
+                )
+                pl.when(first)(lambda way=way, part=part: self.z_copy(way, target, part).start())
+
+    def link(self, turn):
+        target = self.targets[turn]
+        for part in range(self.parts):
+            for way in range(2):
+                later = (target > self.z if way == 0 else target < self.z) & self.has[way]
+
+                @pl.when(later)
                 def _(way=way, part=part):
-                    self.z_copy(way, target, part).wait_recv()
-                    self.add(target, part, (way,))
-
-                @pl.when(going & jnp.logical_not(self.has[way]))
-                def _(part=part):
-                    self.add(target, part, ())
-
-                @pl.when(going)
-                def _(way=way, part=part):
+                    self.z_copy(way, target, part, self.z).wait_recv()
+                    self.add(target, part, (way,), beside=False)
                     self.z_copy(way, target, part).start()
 
-    def finish(self):
+    def finish(self, paired=False):
         z, has = self.z, self.has
         for part in range(self.parts):
-            self.own_wait(z, part)
-            self.y_copy(z, part).wait_recv()
+            if not paired:
+                self.own_wait(z, part)
+                self.y_wait(z, part)
             for way in range(2):
-                pl.when(has[way])(lambda way=way, part=part: self.z_copy(way, z, part).wait_recv())
+                pl.when(has[way])(lambda way=way, part=part: self.z_copy(way, z, part, z).wait_recv())
             for condition, ways in (
                 (has[0] & has[1], (0, 1)),
                 (has[0] & jnp.logical_not(has[1]), (0,)),
                 (jnp.logical_not(has[0]) & has[1], (1,)),
             ):
                 pl.when(condition)(
-                    lambda ways=ways, part=part: self.add(z, part, ways, self.out_ref)
+                    lambda ways=ways, part=part: self.add(z, part, ways, self.out_ref, not paired)
                 )
-        for target in self.targets:
-            for part in range(self.parts):
-                self.y_copy(target, part).wait_send()
+        self.y_drain()
         for target in self.targets[:-1]:
             for part in range(self.parts):
                 self.z_copy(0, target, part).wait_send()
+
+
+class ZReturn(Return):
+    @classmethod
+    def scratch(cls, nz, tok, width):
+        return [
+            pltpu.VMEM((nz + 1, tok, width), BF16),
+            pltpu.SemaphoreType.DMA((nz, cls.parts)),
+            pltpu.SemaphoreType.DMA((nz, cls.parts)),
+            pltpu.SemaphoreType.DMA((nz + 1, cls.parts)),
+        ]
+
+    def __init__(self, mine, share_ref, out_ref, scratch):
+        from_z, mine_sem, z_send, z_recv = scratch
+        super().__init__(
+            share_ref, out_ref, (mine, None, from_z, mine_sem, None, None, z_send, z_recv)
+        )
+
+    def own_copy(self, target, part):
+        return pltpu.make_async_copy(
+            self.share_ref.at[target, self.cut(part)],
+            self.mine.at[target, self.cut(part)],
+            self.mine_sem.at[target, part],
+        )
+
+    def y_wait(self, target, part):
+        pass
+
+    def y_drain(self):
+        pass
+
+    def start(self):
+        for target in self.targets:
+            for part in range(self.parts):
+                self.own_copy(target, part).start()
 
 
 class TileReturn(Return):
@@ -374,12 +493,14 @@
         swap_out, refs = refs[:count], refs[count:]
         (
             vt_ref, cot_stage, table_stage, send_sem, recv_sem, own_sem, swap_send, swap_recv,
+            out_stage, out_send, out_recv,
         ) = refs
         swap = Swap(list(zip(swap_in, swap_out)), swap_send, swap_recv)
+        deliver = Deliver(out_stage, out_ref, out_send, out_recv)
         relay = Relay(
             [(cot_ref, cots_ref, parts), (table_ref, tables_ref, 1)], nz, ny, send_sem, recv_sem
         )
-        greet(relay.peers() + swap.peers())
+        greet(deliver.peers() + relay.peers()[1:3] + swap.peers())
         relay.start()
         swap.start()
         kept = relay.keep((cot_stage, table_stage), own_sem)
@@ -422,7 +543,7 @@
                 )
                 result = acc / total
                 out_t_ref[step] = result
-                out_ref[step] = result.T.astype(BF16)
+                out_stage[step] = result.T.astype(BF16)
                 lse_ref[step] = top + jnp.log(total)
 
             if share == 1:
@@ -434,9 +555,10 @@
                 @pl.when(jnp.logical_not(mine))
                 def _():
                     out_t_ref[step] = jnp.zeros((dim, block), F32)
-                    out_ref[step] = jnp.zeros((block, dim), BF16)
+                    out_stage[step] = jnp.zeros((block, dim), BF16)
                     lse_ref[step] = jnp.zeros((1, block), F32)
 
+            deliver.send(step)
             return carry
 
         lax.fori_loop(0, blocks, query_block, 0)
@@ -452,6 +574,7 @@
 
         lax.fori_loop(0, nz * ny, from_sibling, 0)
         relay.drain()
+        deliver.wait()
         swap.wait()
         for copy in kept:
             copy.wait()
@@ -464,7 +587,7 @@
         + [anywhere] * count,
         out_specs=[inside] * 3 + [anywhere] * (2 + count),
         out_shape=[
-            jax.ShapeDtypeStruct((blocks, block, dim), BF16),
+            jax.ShapeDtypeStruct((src, per, block, dim), BF16),
             jax.ShapeDtypeStruct((blocks, dim, block), F32),
             jax.ShapeDtypeStruct((blocks, 1, block), F32),
             jax.ShapeDtypeStruct((nz, 2, ny) + cots.shape, cots.dtype),
@@ -480,6 +603,9 @@
             pltpu.SemaphoreType.DMA((2,)),
             pltpu.SemaphoreType.DMA((count,)),
             pltpu.SemaphoreType.DMA((count,)),
+            pltpu.VMEM((blocks, block, dim), BF16),
+            pltpu.SemaphoreType.DMA((blocks,)),
+            pltpu.SemaphoreType.DMA((src, per)),
         ],
         compiler_params=pltpu.CompilerParams(
             collective_id=collective_id, has_side_effects=True, vmem_limit_bytes=VMEM_BYTES
@@ -492,7 +618,7 @@
     src, _, per, block, dim = qkv.shape
     blocks = src * per
     count = len(swaps)
-    events = [blocks * 9 // 16, blocks * 13 // 16]
+    events = [blocks * n // 16 for n in (3, 7, 13)]
 
     def kernel(bias_ref, qkv_ref, go_ref, out_t_ref, lse_ref, *refs):
         swap_in, refs = refs[:count], refs[count:]
@@ -500,66 +626,100 @@
         grad_ref, *refs = refs
         swap_out, refs = refs[:count], refs[count:]
         sum_ref, refs = refs[: len(shares)], refs[len(shares) :]
-        dk_ref, dv_ref, swap_send, swap_recv, *refs = refs
+        dk_ref, dv_ref, delta_ref, swap_send, swap_recv, stage, out_send, out_recv, *refs = refs
+        deliver = Deliver(stage, grad_ref, out_send, out_recv)
         swap = Swap(list(zip(swap_in, swap_out)), swap_send, swap_recv)
         back = Return(share_ref[0], sum_ref[0], refs) if shares else None
-        greet(swap.peers() + (back.peers() if back else []))
+        greet(deliver.peers() + swap.peers() + (back.peers()[:1] if back else []))
         if back:
             back.start()
         swap.start()
         dk_ref[...] = jnp.zeros_like(dk_ref)
         dv_ref[...] = jnp.zeros_like(dv_ref)
         own = lax.axis_index("blk") % share
-
-        def query_block(step, carry):
-            for n, event in enumerate(events):
-                if back and n < back.nz - 1:
-                    pl.when(step == event)(lambda n=n: back.send(n))
+        core = lax.axis_index("blk") % 2
+
+        def block_delta(i, carry):
+            delta_ref[i] = jnp.sum(go_ref[i].astype(F32).T * out_t_ref[i], axis=0, keepdims=True)
+            return carry
+
+        lax.fori_loop(0, blocks, block_delta, 0)
+
+        def pair(i, j):
+            scores = mm(qkv_ref[j // per, 1, j % per], qkv_ref[i // per, 0, i % per], NT) * scale
+            probs = jnp.exp(scores + bias_ref[i * blocks + j] - lse_ref[i])
+            grad_probs = mm(qkv_ref[j // per, 2, j % per], go_ref[i], NT)
+            return probs.astype(BF16), (probs * (grad_probs - delta_ref[i])).astype(BF16)
+
+        def down(turn):
+            i = blocks - 1 - turn
 
             def work():
-                query = qkv_ref[step // per, 0, step % per]
-                go = go_ref[step]
-                delta = jnp.sum(go.astype(F32).T * out_t_ref[step], axis=0, keepdims=True)
-                log_total = lse_ref[step]
+                query, go = qkv_ref[i // per, 0, i % per], go_ref[i]
 
                 def body(j, dq):
-                    key = qkv_ref[j // per, 1, j % per]
-                    value = qkv_ref[j // per, 2, j % per]
-                    scores = mm(key, query, NT) * scale + bias_ref[step * blocks + j]
-                    probs = jnp.exp(scores - log_total)
-                    grad_scores = (probs * (mm(value, go, NT) - delta)).astype(BF16)
-                    dv_ref[j] += mm(probs.astype(BF16), go)
+                    probs, grad_scores = pair(i, j)
+                    dv_ref[j] += mm(probs, go)
                     dk_ref[j] += mm(grad_scores, query)
-                    return dq + mm(grad_scores, key, TN)
-
-                dq = lax.fori_loop(0, step + 1, body, jnp.zeros((block, dim), F32))
-                grad_ref[step // per, 0, step % per] = (dq * scale).astype(BF16)
+                    return dq + mm(grad_scores, qkv_ref[j // per, 1, j % per], TN)
+
+                dq = lax.fori_loop(0, i + 1, body, jnp.zeros((block, dim), F32))
+                stage[i, 0] = (dq * scale).astype(BF16)
 
             if share == 1:
                 work()
             else:
-                mine = step % share == own
+                mine = i % share == own
                 pl.when(mine)(work)
 
                 @pl.when(jnp.logical_not(mine))
                 def _():
-                    grad_ref[step // per, 0, step % per] = jnp.zeros((block, dim), BF16)
-
-            return carry
-
-        lax.fori_loop(0, blocks, query_block, 0)
+                    stage[i, 0] = jnp.zeros((block, dim), BF16)
+
+            stage[i, 1] = (dk_ref[i] * scale).astype(BF16)
+            stage[i, 2] = dv_ref[i].astype(BF16)
+            deliver.send(i)
+
+        def up(j):
+            key = qkv_ref[j // per, 1, j % per]
+
+            def body(turn, carry):
+                dk, dv = carry
+                i = own + share * turn
+                probs, grad_scores = pair(i, j)
+                dk_ref[i] += mm(grad_scores, key, TN)
+                query = qkv_ref[i // per, 0, i % per]
+                return dk + mm(grad_scores, query), dv + mm(probs, go_ref[i])
+
+            zero = jnp.zeros((block, dim), F32)
+            first = jnp.maximum(j - own + share - 1, 0) // share
+            dk, dv = lax.fori_loop(first, blocks // share, body, (zero, zero))
+            stage[j, 0] = (dk_ref[j] * scale).astype(BF16)
+            stage[j, 1] = (dk * scale).astype(BF16)
+            stage[j, 2] = dv.astype(BF16)
+            deliver.send(j)
+
+        def rounds(work):
+            def one(turn, carry):
+                for n, event in enumerate(events):
+                    if back and n < back.nz:
+                        pl.when(turn == event)(lambda n=n: back.pair(n))
+                if back:
+                    pl.when(turn == events[-1])(lambda: back.link(0))
+                work(turn)
+                return carry
+
+            lax.fori_loop(0, blocks, one, 0)
+
+        pl.when(core == 0)(lambda: rounds(down))
+        pl.when(core == 1)(lambda: rounds(up))
         if back:
-            for turn in range(len(events), back.nz - 1):
-                back.send(turn)
-
-        def store(j, carry):
-            grad_ref[j // per, 1, j % per] = (dk_ref[j] * scale).astype(BF16)
-            grad_ref[j // per, 2, j % per] = dv_ref[j].astype(BF16)
-            return carry
-
-        lax.fori_loop(0, blocks, store, 0)
-        if back:
-            back.finish()
+            for n in range(min(len(events), back.nz), back.nz):
+                back.pair(n)
+            for n in range(1, back.nz - 1):
+                back.link(n)
+            back.finish(True)
+        deliver.wait()
         swap.wait()
 
     anywhere = pl.BlockSpec(memory_space=pl.ANY)
@@ -570,14 +730,18 @@
         in_specs=[pl.BlockSpec(memory_space=pltpu.SMEM)] + [inside] * 4
         + [anywhere] * (count + len(shares)),
         out_specs=[inside] + [anywhere] * count + [inside] * len(shares),
-        out_shape=[jax.ShapeDtypeStruct(qkv.shape, BF16)]
+        out_shape=[jax.ShapeDtypeStruct((src, per, 3, block, dim), BF16)]
         + [jax.ShapeDtypeStruct(v.shape, v.dtype) for v in swaps]
         + [jax.ShapeDtypeStruct((tok, width), BF16)] * len(shares),
         scratch_shapes=[
             pltpu.VMEM((blocks, block, dim), F32),
             pltpu.VMEM((blocks, block, dim), F32),
+            pltpu.VMEM((blocks, 1, block), F32),
             pltpu.SemaphoreType.DMA((count,)),
             pltpu.SemaphoreType.DMA((count,)),
+            pltpu.VMEM((blocks, 3, block, dim), BF16),
+            pltpu.SemaphoreType.DMA((blocks,)),
+            pltpu.SemaphoreType.DMA((src, per)),
         ]
         + (Return.scratch(nz, tok, width) if shares else []),
         compiler_params=pltpu.CompilerParams(
@@ -1070,7 +1234,9 @@
     return out[0], out[1:3], out[3], out[4], gathered, out[8:]
 
 
-def project_backward(grads, raws, invs, gains, group, weights, nh, nb, collective_id):
+def project_backward(
+    grads, raws, invs, gains, group, weights, swaps, sums, nh, nb, collective_id
+):
     rows, width = group.shape
     columns = raws[0].shape[1]
     items = grads.shape[0]
@@ -1082,11 +1248,21 @@
     tile = width // nb
     lots = nh * seqs
     chunk = min(512, width)
+    count = len(swaps)
 
     def kernel(grad_ref, qraw_ref, kraw_ref, inv_ref, gain_ref, group_ref, wq_ref, wk_ref, wv_ref, *refs):
+        swap_in, refs = refs[:count], refs[count:]
+        share_ref, refs = refs[: len(sums)], refs[len(sums) :]
         out_ref, *refs = refs
         tile_refs, refs = refs[:3], refs[3:]
         qk_ref, product_ref, *refs = refs
+        swap_out, refs = refs[:count], refs[count:]
+        total_ref, refs = refs[: len(sums)], refs[len(sums) :]
+        swap_send, swap_recv, *refs = refs
+        chain = None
+        if sums:
+            chain, refs = ZReturn(refs[0], share_ref[0], total_ref[0], refs[1:5]), refs[5:]
+        swap = Swap(list(zip(swap_in, swap_out)), swap_send, swap_recv)
         d_ref, sum_ref, part_ref, got_ref, sum_send, sum_recv, part_send, part_recv, *refs = refs
         give = refs[0]
         back = TileReturn(give, tile_refs, refs[1:])
@@ -1105,19 +1281,20 @@
                 device_id_type=pl.DeviceIdType.MESH,
             )
 
-        def part_copy(k, slot):
+        def part_copy(k):
             return pltpu.make_async_remote_copy(
                 src_ref=part_ref.at[k],
-                dst_ref=got_ref.at[slot],
+                dst_ref=got_ref.at[nh - 2 - k],
                 send_sem=part_send.at[k],
-                recv_sem=part_recv.at[slot],
+                recv_sem=part_recv.at[nh - 2 - k],
                 device_id=devices[k],
                 device_id_type=pl.DeviceIdType.MESH,
             )
 
         def grad_tile(n, lot, hl):
             at, s = lot // seqs, lot % seqs
-            return grad_ref[s * heads + hl, n, at * piece : (at + 1) * piece, :]
+            block, offset = divmod(at * piece, BLOCK)
+            return grad_ref[s * heads + hl, block, n, offset : offset + piece, :]
 
         def upright(row):
             return jnp.broadcast_to(row, (HEAD_DIM, piece)).T
@@ -1136,6 +1313,13 @@
         greet([(device, None) for device in devices] + back.peers())
         for k in range(nh - 1):
             sum_copy(k, head).start()
+        swap.start()
+        edge = jnp.logical_or(z == 0, z == nz - 1)
+        inner = jnp.logical_not(edge)
+        if chain:
+            chain.start()
+            for turn in range(nz - 1):
+                pl.when(edge)(lambda turn=turn: chain.send(turn))
         for lot in range(lots):
             here = slice(lot * piece, (lot + 1) * piece)
             for hl in range(heads):
@@ -1164,8 +1348,6 @@
             for hl in range(heads):
                 qk_ref[n : n + 1, hl * HEAD_DIM : (hl + 1) * HEAD_DIM] = gain_total[hl]
 
-        edge = jnp.logical_or(z == 0, z == nz - 1)
-        inner = jnp.logical_not(edge)
         for turn, target in enumerate(back.targets):
             for at, dest in ((1 - core, give), (core, back.mine)):
                 cols = pl.ds(pl.multiple_of((target * 2 + at) * tile, tile), tile)
@@ -1196,8 +1378,10 @@
                 part_ref[k, :, cols] = total.astype(BF16)
 
             partial(others[k], keep)
-            part_copy(k, head).start()
+            part_copy(k).start()
             while sent < nz - 1 and (k + 1) * (nz - 1) >= (sent + 2) * (nh - 1):
+                if chain:
+                    pl.when(inner)(lambda turn=sent: chain.send(turn))
                 pl.when(inner)(lambda turn=sent: back.send(turn))
                 sent += 1
 
@@ -1206,42 +1390,55 @@
 
         partial(head, keep_own)
         for turn in range(sent, nz - 1):
+            if chain:
+                pl.when(inner)(lambda turn=turn: chain.send(turn))
             pl.when(inner)(lambda turn=turn: back.send(turn))
         for k in range(nh - 1):
-            part_copy(k, others[k]).wait_recv()
+            part_copy(nh - 2 - k).wait_recv()
             for r in range(0, tok, 64):
                 here = pl.ds(r, 64)
-                out_ref[here, :] += got_ref[others[k], here, :].astype(F32)
+                out_ref[here, :] += got_ref[k, here, :].astype(F32)
         back.finish()
+        if chain:
+            chain.finish()
         for k in range(nh - 1):
             sum_copy(k, head).wait_send()
-            part_copy(k, head).wait_send()
-
+            part_copy(k).wait_send()
+        swap.wait()
+
+    anywhere = pl.BlockSpec(memory_space=pl.ANY)
     inside = pl.BlockSpec(memory_space=pltpu.VMEM)
     out = pl.pallas_call(
         kernel,
-        in_specs=[inside] * 9,
-        out_specs=[inside] * 6,
+        in_specs=[inside] * 9 + [anywhere] * (count + len(sums)),
+        out_specs=[inside] * 6 + [anywhere] * count + [inside] * len(sums),
         out_shape=[jax.ShapeDtypeStruct((tok, width), F32)]
         + [jax.ShapeDtypeStruct((tile, columns), F32)] * 3
-        + [jax.ShapeDtypeStruct((2, columns), F32), jax.ShapeDtypeStruct((1, width), F32)],
+        + [jax.ShapeDtypeStruct((2, columns), F32), jax.ShapeDtypeStruct((1, width), F32)]
+        + [jax.ShapeDtypeStruct(v.shape, v.dtype) for v in swaps]
+        + [jax.ShapeDtypeStruct((tok, width), BF16)] * len(sums),
         scratch_shapes=[
+            pltpu.SemaphoreType.DMA((count,)),
+            pltpu.SemaphoreType.DMA((count,)),
+        ]
+        + ([pltpu.VMEM((nz, tok, width), BF16)] + ZReturn.scratch(nz, tok, width)) * len(sums)
+        + [
             pltpu.VMEM((rows, 3 * columns), BF16),
             pltpu.VMEM((nh, 2 * lots, piece), F32),
             pltpu.VMEM((nh - 1, tok, width), BF16),
-            pltpu.VMEM((nh, tok, width), BF16),
+            pltpu.VMEM((nh - 1, tok, width), BF16),
             pltpu.SemaphoreType.DMA((nh - 1,)),
             pltpu.SemaphoreType.DMA((nh,)),
             pltpu.SemaphoreType.DMA((nh - 1,)),
-            pltpu.SemaphoreType.DMA((nh,)),
+            pltpu.SemaphoreType.DMA((nh - 1,)),
         ]
         + TileReturn.scratch(nz, tile, 3 * columns),
         compiler_params=pltpu.CompilerParams(
             collective_id=collective_id, has_side_effects=True, vmem_limit_bytes=VMEM_BYTES
         ),
         name="project_backward",
-    )(grads, *raws, invs, gains, group, *weights)
-    return out[0], out[1:4], out[4], out[5]
+    )(grads, *raws, invs, gains, group, *weights, *swaps, *sums)
+    return out[0], out[1:4], out[4], out[5], out[6 : 6 + count], out[6 + count :]
 
 
 def local(
@@ -1349,7 +1546,7 @@
     ).astype(jnp.int32)
     slots = jnp.where(hit, ranks.reshape(hit.shape), -1)[..., None, :]
 
-    attended = from_items(swap(heads_out.reshape(blk_count, span, HEAD_DIM))).astype(BF16)
+    attended = from_items(heads_out.reshape(blk_count, span, HEAD_DIM)).astype(BF16)
     branch = lax.psum_scatter(
         mm(attended, out_w).astype(BF16), "head", scatter_dimension=0, tiled=True
     ).astype(F32)
@@ -1410,26 +1607,31 @@
     out_part = mm(attended, grad_group, TN)
     grad_heads = swap(to_items(grad_attended)).reshape(blk_count * per, BLOCK, HEAD_DIM)
     own_sum = ny == 2
-    grad_qkv, others[1:], sums = attend_backward(
-        bias, qkv, grad_heads, heads_out_t, log_total, others[1:], [moe_share] * own_sum,
-        scale, share, 3,
+    middle_row = half // 2
+    grad_qkv, (down_first, gate_part, up_part), sums = attend_backward(
+        bias, qkv, grad_heads, heads_out_t, log_total,
+        (others[0][:middle_row], others[1], others[2]), [moe_share] * own_sum, scale, share, 3,
     )
-    others[0] = flip_head(others[0], 1)
-    grad_qkv = swap(grad_qkv.reshape(blk_count, 3, span, HEAD_DIM))
-    grad_qkv, others[0] = lax.optimization_barrier((grad_qkv, others[0]))
-    grad_down, grad_gate, grad_up = [
-        (mine + other.astype(F32))[None] for mine, other in zip(halves[:3], others)
-    ]
+    if share > 1:
+        grad_qkv = grad_qkv.reshape((items, share) + grad_qkv.shape[1:])
+        grad_qkv = grad_qkv.astype(F32).sum(1).astype(BF16)
+    grad_normed, (grad_query, grad_key, grad_value), qk_parts, product, (down_last,), _ = (
+        project_backward(
+            grad_qkv, raws, invs, qk_gains, group, qkv_cols, (others[0][middle_row:],), (),
+            head_count, blk_count, 4,
+        )
+    )
     if own_sum:
         expert_sum = sums[0].astype(F32)
     else:
         expert_sum = give_back(give_back(moe_share.swapaxes(0, 1), y_bits), z_bits)
     result = middle + expert_sum
-    if share > 1:
-        grad_qkv = grad_qkv.reshape(items, share, 3, span, HEAD_DIM).astype(F32).sum(1).astype(BF16)
-    grad_normed, (grad_query, grad_key, grad_value), qk_parts, product = project_backward(
-        grad_qkv, raws, invs, qk_gains, group, qkv_cols, head_count, blk_count, 4
-    )
+    grad_down, grad_gate, grad_up = [
+        (mine + other.astype(F32))[None]
+        for mine, other in zip(
+            halves[:3], (jnp.concatenate([down_first, down_last]), gate_part, up_part)
+        )
+    ]
     grad_normed = rounded(grad_normed)
     query_gain_part, key_gain_part = qk_parts[0], qk_parts[1]
     gained_one = grad_normed * attn_gain

time: 1070 us -> 1000 us (0.935)
  blocking collectives: 83.9 us -> 23 us
  waiting for transfers between devices: 122 us -> 75 us
  Pallas kernels: 693 us -> 732 us
    all_to_all x2 -> x0, blocking collectives: 61.4 us -> none  [swap(): lax.all_to_all(values, 'blk', split_axis=0, concat_axis=0, tiled=True)]
    reduce_scatter x1, waiting for transfers between devices: 49.3 us -> 0.01 us  [over_blk(): lax.psum_scatter(values.astype(BF16), 'blk', scatter_dimension=dim, tiled...]
    pallas_call x1, Pallas kernels: 125 us -> 150 us  [attend_backward(): pl.pallas_call(kernel, in_specs=[pl.BlockSpec(memory_space=pltpu.SMEM)] +...]
  transfers between devices with their start and end apart: 6 -> 5, of which waited for: 3 -> 2; matrix products, arithmetic and copies ran while one was open for 8% -> 11% of each run, Pallas kernels for 25% -> 51%
where the time goes in v4:
time: 1000 us; the launch traced here: 992 us
  Pallas kernels  732 us (73%)
  waiting for transfers between devices  75 us (8%)
  matrix products  74.3 us (7%)
  other arithmetic  40.5 us (4%)
  local copies, waits for them, and re-layouts  28.2 us (3%)
  blocking collectives  23 us (2%)
  between operations  14.6 us (1%)
    pallas_call x1, Pallas kernels, attend_backward(): pl.pallas_call(kernel, in_specs=[pl.BlockSpec(memory_space=pltpu.SMEM)] +...  150 us
    pallas_call x1, Pallas kernels, project_forward(): pl.pallas_call(kernel, in_specs=[inside] * 5 + [anywhere] * count, out_sp...  145 us
    pallas_call x1, Pallas kernels, expert_exchange(): pl.pallas_call(kernel, in_specs=[anywhere, inside, inside] + [anywhere] *...  134 us
    pallas_call x1, Pallas kernels, attend_forward(): pl.pallas_call(kernel, in_specs=[pl.BlockSpec(memory_space=pltpu.SMEM), i...  121 us
    pallas_call x1, Pallas kernels, return_sum(): pl.pallas_call(kernel, in_specs=[pl.BlockSpec(memory_space=pl.ANY)], out_...  95.2 us
    pallas_call x1, Pallas kernels, project_backward(): pl.pallas_call(kernel, in_specs=[inside] * 9 + [anywhere] * (count + len(...  86.2 us
    dot_general x9, matrix products, mm(): return lax.dot_general(left, right, dims, preferred_element_type=F32)  74.2 us
    reduce_scatter x1, waiting for transfers between devices, local(): lax.psum_scatter(mm(attended, out_w).astype(BF16), 'head', scatter_dimens...  49.4 us
  transfers between devices with their start and end apart: 5, of which 2 were waited for; matrix products, arithmetic and copies ran while one was open for 11% of the time, Pallas kernels for 51%

profile of v4, /device:TPU:0, one launch (start us, length us, event | category | flops | bytes accessed | tf_op | source)
XLA Modules:
  0.0 992.1 jit_solution(7779762207979459030)
XLA Ops:
  7.2 0.7 all-gather.5.cloned.1.call-update
  8.1 0.6 select_n.49.bias_ref
  8.7 0.8 dynamic_slice.11
  9.5 0.8 dynamic_slice.12
  10.3 2.4 convert_bitcast_fusion
  12.7 1.2 copy.52
  14.0 1.2 fusion.21
  15.2 0.1 copy.64
  15.2 1.3 copy.54
  16.6 0.6 pad_maximum_fusion.1.gain_ref
  17.2 1.2 multiply_convert_fusion.1.normed_ref
  18.4 145.5 %project_forward.1 = (bf16[8,3,512,128]{3,2,1,0:T(8,128)(2,1)}, f32[1024,512]{1,0:T(8,128)}, f32[1024,512]{1,0:T(8,128)}, f32[16,128]{1,0:T(8,128)}, bf16[1024,2...) custom-call(bf16[256,2048]{1,0:T(8,128)(2,1)} %multiply_convert_fusi, ...), custom_call_target="tpu_custom_call" | custom-call | tf_op jit(solution)/shard_map/project_forward/pallas_call | solution.py:1200
  163.9 0.6 pad_maximum_fusion.table_ref
  164.5 120.7 %attend_forward.1 = (bf16[8,2,256,128]{3,2,1,0:T(8,128)(2,1)}, f32[16,128,256]{2,1,0:T(8,128)}, f32[16,1,256]{2,1,0:T(1,128)}, bf16[4,2,2,256,2048]{4,3,2,1,0:T(...) custom-call(f32[256]{0:T(256)} %select_n.49.bias_ref, ...), custom_call_target="tpu_custom_call" | custom-call | tf_op jit(solution)/shard_map/attend_forward/pallas_call | solution.py:584
  285.2 2.0 copy.55
  287.3 6.3 convolution_convert_fusion
  293.7 0.9 copy-done.18
  294.7 0.1 convolution_convert_fusion.3
  294.9 0.6 broadcast_in_dim.55.gate_ref
  295.5 0.6 copy_select_fusion.slot_ref
  296.2 49.4 %reduce-scatter.3.cloned.1.call-done = bf16[256,2048]{1,0:T(8,128)(2,1)} async-done(((bf16[1024,2048]{1,0:T(8,128)(2,1)}), bf16[256,2048]{1,0:T(8,128)(2,1)}) %reduce-scatter.3.cloned.1.call-update) | async-done | bytes 1048592 | tf_op jit(solution)/shard_map/reduce_scatter | solution.py:1550
  345.5 2.7 multiply_reduce_fusion.1
  348.2 1.4 multiply_convert_fusion.own_ref
  349.6 134.2 %expert_exchange.1 = (bf16[4,2,256,2048]{3,2,1,0:T(8,128)(2,1)}, bf16[4,2,256,2048]{3,2,1,0:T(8,128)(2,1)}, bf16[8,320,2048]{2,1,0:T(8,128)(2,1)}, bf16[8,320,20...) custom-call(bf16[256,2048]{1,0:T(8,128)(2,1)} %multiply_convert_fusi, ...), custom_call_target="tpu_custom_call" | custom-call | tf_op jit(solution)/shard_map/expert_exchange/pallas_call | solution.py:978
  483.8 95.2 %return_sum.1 = bf16[256,2048]{1,0:T(8,128)(2,1)} custom-call(bf16[4,2,256,2048]{3,2,1,0:T(8,128)(2,1)} %get-tuple-element.64.share_ref), custom_call_target="tpu_custom_call" | custom-call | tf_op jit(solution)/shard_map/return_sum/pallas_call | solution.py:1034
  579.0 2.0 fusion.19
  581.1 1.9 fusion.37
  583.0 11.7 %fusion.refs_2_ = bf16[2048,512]{1,0:T(8,128)(2,1)} fusion(bf16[2560,2048]{1,0:T(8,128)(2,1)} %bitcast.134, bf16[2560,2048]{1,0:T(8,128)(2,1)} %bitcast.140), kind=kOutput, calls=%fused_computation.13 | convolution fusion | flops 5368709120 | bytes 15204352 | tf_op jit(solution)/shard_map/dot_general | solution.py:24
  594.7 10.3 %fusion.4 = bf16[512,2048]{1,0:T(8,128)(2,1)} fusion(bf16[2560,2048]{1,0:T(8,128)(2,1)} %bitcast.146, bf16[2560,1024]{1,0:T(8,128)(2,1)} %bitcast.148), kind=kOutput, calls=%fused_computation.17 | convolution fusion | flops 5368709120 | bytes 15204352 | tf_op jit(solution)/shard_map/dot_general | solution.py:24
  605.0 10.6 %fusion.10 = f32[512,2048]{1,0:T(8,128)} fusion(bf16[2560,2048]{1,0:T(8,128)(2,1)} %bitcast.147, bf16[2560,1024]{1,0:T(8,128)(2,1)} %bitcast.149), kind=kOutput, calls=%fused_computation.23 | convolution fusion | flops 5368709120 | bytes 17301504 | tf_op jit(solution)/shard_map/dot_general | solution.py:24
  615.6 7.3 fusion.2.refs_1_
  623.0 8.0 fusion.6
  630.9 7.6 fusion.8
  638.5 6.2 convolution_convert_fusion.2
  644.7 2.1 reshape.162
  646.8 2.4 copy.58
  649.3 4.2 all-to-all-start
  653.6 6.2 convolution_convert_fusion.1
  659.8 3.1 fusion.38
  662.9 24.9 %all-to-all-done = bf16[8,512,128]{2,1,0:T(8,128)(2,1)} async-done(((bf16[8,512,128]{2,1,0:T(8,128)(2,1)}), bf16[8,512,128]{2,1,0:T(8,128)(2,1)}, u32[]{:S(2)}, u32[]{:S(2)}) %all-to-all-start) | async-done | bytes 1048608 | tf_op jit(solution)/shard_map/all_to_all | solution.py:1526
  687.8 150.3 %attend_backward.1 = (bf16[8,2,3,256,128]{4,3,2,1,0:T(8,128)(2,1)}, bf16[256,2048]{1,0:T(8,128)(2,1)}, bf16[2048,512]{1,0:T(8,128)(2,1)}, bf16[2048,512]{1,0:T(8,128)(2,1)}, bf16[256,2048]{1,0:T(8,128)(2,1)}) custom-call(f32[256]{0:T(256)} %select_n.49.bias_ref, bf16[8,3,2,256,128]{4,3,2,1,0:T(8,128)(2,1)} %bitcast.104, ...), custom_call_target="tpu_custom_call" | custom-call | tf_op jit(solution)/shard_map/attend_backward/pallas_call | solution.py:728
  838.1 86.2 %project_backward.1 = (f32[256,2048]{1,0:T(8,128)}, f32[256,512]{1,0:T(8,128)}, f32[256,512]{1,0:T(8,128)}, f32[256,512]{1,0:T(8,128)}, f32[2,512]{1,0:T(2,128)}...) custom-call(bf16[8,2,3,256,128]{4,3,2,1,0:T(8,128)(2,1)} %get-tuple-element.79.grad_ref, ...), custom_call_target="tpu_custom_call" | custom-call | tf_op jit(solution)/shard_map/project_backward/pallas_call | solution.py:1411
  924.4 0.7 divide_dynamic-update-slice_fusion
  925.1 0.8 fusion.39
  925.8 0.3 dynamic_update_slice.6
  926.1 2.7 convert_element_type.116
  928.8 0.2 dynamic_update_slice.7
  929.0 1.9 fusion.22
  930.9 0.3 copy-done.6
  931.2 5.0 multiply_reduce_fusion
  936.2 2.0 constant_dynamic-update-slice_fusion
  938.2 8.7 all_gather.17
  947.0 14.3 %all-gather.1 = f32[8,65,128]{2,1,0:T(8,128)S(1)} all-gather(f32[1,65,128]{2,1,0:T(8,128)S(1)} %bitcast.122), channel_id=2, replica_groups=mesh['head'=4,'blk'=8] {'blk'}, dimensions={0}, use_global_device_ids=true | all-gather | bytes 299520 | tf_op jit(solution)/shard_map/all_gather | solution.py:1669
  961.2 0.5 fusion.34
  961.8 0.6 slice_bitcast_fusion
  962.4 5.9 copy_bitcast_fusion
  968.3 4.2 add_bitcast_fusion
  972.5 1.1 copy-done.8
  973.5 0.6 copy-done.11
  974.2 6.7 add_bitcast_fusion.1
  980.9 1.9 convert_element_type.120
  982.7 0.8 copy.87
  983.5 0.8 copy.88
  984.3 0.8 copy.89
  (84 shorter events, 0.7 us)
Async XLA Ops:
  7.2 0.8 copy-start
  7.2 280.1 %all-gather.5.cloned.1.call-start = ((), (), s32[]{:S(2)}) async-start(), calls=%async_computation.3 | async-start | bytes 2359296 | tf_op jit(solution)/shard_map/all_gather | solution.py:1508
  7.9 337.6 %reduce-scatter.3.cloned.1.call-start = ((), (), s32[]{:S(2)}) async-start(), calls=%async_computation.4 | async-start | bytes 5242880 | tf_op jit(solution)/shard_map/reduce_scatter | solution.py:1550
  12.7 1.2 copy-start.9
  12.7 2.5 copy-start.13
  14.0 3.2 copy-start.20
  18.4 145.5 %copy-start.21 = (s32[128,2,8]{0,2,1:T(8,128)S(1)}, s32[128,2,8]{0,2,1:T(8,128)}, u32[]{:S(2)}) copy-start(s32[128,2,8]{0,2,1:T(8,128)} %param.28) | copy-start | bytes 24580
  18.4 145.5 %copy-start.22 = (f32[128,2,8]{0,2,1:T(8,128)S(1)}, f32[128,2,8]{0,2,1:T(8,128)}, u32[]{:S(2)}) copy-start(f32[128,2,8]{0,2,1:T(8,128)} %param.29) | copy-start | bytes 24580
  287.3 6.4 copy-start.14
  293.6 1.0 copy-start.18
  293.7 344.8 %all-gather.7.cloned.1.call-start = ((), (), s32[]{:S(2)}) async-start(), calls=%async_computation.5 | async-start | bytes 5242880 | tf_op jit(solution)/shard_map/all_gather | solution.py:1603
  296.2 52.0 %copy-start.19 = (f32[2048]{0:T(1024)S(1)}, f32[2048]{0:T(1024)}, u32[]{:S(2)}) copy-start(f32[2048]{0:T(1024)} %param.24) | copy-start | bytes 24580
  348.2 232.9 %copy-start.2 = (f32[256,2048]{1,0:T(8,128)}, f32[256,2048]{1,0:T(8,128)S(1)}, u32[]{:S(2)}) copy-start(f32[256,2048]{1,0:T(8,128)S(1)} %get-tuple-element.107) | copy-start | bytes 6291460
  579.0 2.1 copy-start.4
  579.0 2.1 copy-start.5
  594.7 20.9 %slice-start = ((s8[10485760]{0:T(1024)(128)(4,1)}), s8[4194304]{0:T(1024)(128)(4,1)S(1)}, s32[]{:S(2)}) async-start(s8[10485760]{0:T(1024)(128)(4,1)} %bitcast.135), calls=%async_computation.7 | async-start | bytes 8388608
  594.7 20.9 %slice-start.1 = ((s8[10485760]{0:T(1024)(128)(4,1)}), s8[4194304]{0:T(1024)(128)(4,1)S(1)}, s32[]{:S(2)}) async-start(s8[10485760]{0:T(1024)(128)(4,1)} %bitcast.135), calls=%async_computation.8 | async-start | bytes 8388608
  594.7 20.9 %slice-start.3 = ((s8[10485760]{0:T(1024)(128)(4,1)}), s8[4194304]{0:T(1024)(128)(4,1)S(1)}, s32[]{:S(2)}) async-start(s8[10485760]{0:T(1024)(128)(4,1)} %bitcast.141), calls=%async_computation.10 | async-start | bytes 8388608
  594.7 20.9 %slice-start.4 = ((s8[10485760]{0:T(1024)(128)(4,1)}), s8[4194304]{0:T(1024)(128)(4,1)S(1)}, s32[]{:S(2)}) async-start(s8[10485760]{0:T(1024)(128)(4,1)} %bitcast.141), calls=%async_computation.11 | async-start | bytes 8388608
  605.0 10.6 %slice-start.2 = ((s8[10485760]{0:T(1024)(128)(4,1)}), s8[2097152]{0:T(1024)(128)(4,1)S(1)}, s32[]{:S(2)}) async-start(s8[10485760]{0:T(1024)(128)(4,1)} %bitcast.135), calls=%async_computation.9 | async-start | bytes 4194304
  605.0 10.6 %slice-start.5 = ((s8[10485760]{0:T(1024)(128)(4,1)}), s8[2097152]{0:T(1024)(128)(4,1)S(1)}, s32[]{:S(2)}) async-start(s8[10485760]{0:T(1024)(128)(4,1)} %bitcast.141), calls=%async_computation.12 | async-start | bytes 4194304
  649.3 38.6 %all-to-all-start = ((bf16[8,512,128]{2,1,0:T(8,128)(2,1)}), bf16[8,512,128]{2,1,0:T(8,128)(2,1)}, u32[]{:S(2)}, u32[]{:S(2)}) async-start(bf16[8,512,128]{2,1,0:T(8,128)(2,1)} %bitcast.113), calls=%async_computation.1 | async-start | bytes 2097152 | tf_op jit(solution)/shard_map/all_to_all | solution.py:1526
  653.5 327.3 %reduce-scatter.5.cloned.1.call-start = ((), (), s32[]{:S(2)}) async-start(), calls=%async_computation.6 | async-start | bytes 2359296 | tf_op jit(solution)/shard_map/reduce_scatter | solution.py:1650
  929.0 1.9 copy-start.3
  929.0 2.2 copy-start.6
  938.2 30.0 %copy-start.12 = (bf16[256,2048]{1,0:T(8,128)(2,1)S(1)}, bf16[256,2048]{1,0:T(8,128)(2,1)}, u32[]{:S(2)}) copy-start(bf16[256,2048]{1,0:T(8,128)(2,1)} %get-tuple-element.98) | copy-start | bytes 3145732
  962.4 5.9 copy-start.10
  968.2 4.2 copy-start.7
  968.3 5.3 copy-start.8
  968.3 5.9 copy-start.11
  974.1 8.6 copy-start.17
  974.1 11.0 %copy-start.1 = (s32[2,16]{1,0:T(2,128)S(1)}, s32[2,16]{1,0:T(2,128)}, u32[]{:S(2)}) copy-start(s32[2,16]{1,0:T(2,128)} %param.30) | copy-start | bytes 388
  980.8 2.7 copy-start.16
  980.8 3.5 copy-start.15
Sparse Core Ops, SparseCore 0:
  9.6 44.7 all-gather.4
  293.8 51.6 reduce-scatter.2
  583.1 52.1 all-gather.6
  659.9 41.3 reduce-scatter.4

commit v5 on v4

--- a/solution.py
+++ b/solution.py
@@ -483,7 +483,7 @@
     src, _, per, block, dim = qkv.shape
     blocks = src * per
     parts = 2
-    events = [blocks * 5 // 8, blocks * 7 // 8]
+    events = [(blocks * 10 // 16, blocks * 3 // 16), (blocks * 14 // 16, blocks * 7 // 16)]
 
     count = len(swaps)
 
@@ -512,10 +512,13 @@
         lax.fori_loop(0, blocks, flip, 0)
         own = lax.axis_index("blk") % share
 
-        def query_block(step, carry):
+        def query_block(turn, carry):
+            step = jnp.where(relay.core == 0, turn, blocks - 1 - turn)
             for n, event in enumerate(events):
                 if n + 1 < nz:
-                    pl.when(step == event)(lambda n=n: relay.pass_on_z(n + 1))
+                    pl.when(turn == jnp.where(relay.core == 0, *event))(
+                        lambda n=n: relay.pass_on_z(n + 1)
+                    )
 
             def work():
                 query = qkv_ref[step // per, 0, step % per]
@@ -1235,7 +1238,7 @@
 
 
 def project_backward(
-    grads, raws, invs, gains, group, weights, swaps, sums, nh, nb, collective_id
+    grads, raws, invs, gains, group, weights, swaps, sums, stats, nh, nb, collective_id
 ):
     rows, width = group.shape
     columns = raws[0].shape[1]
@@ -1250,15 +1253,17 @@
     chunk = min(512, width)
     count = len(swaps)
 
-    def kernel(grad_ref, qraw_ref, kraw_ref, inv_ref, gain_ref, group_ref, wq_ref, wk_ref, wv_ref, *refs):
+    def kernel(grad_ref, qraw_ref, kraw_ref, inv_ref, gain_ref, group_ref, wq_ref, wk_ref, wv_ref, stat_ref, *refs):
         swap_in, refs = refs[:count], refs[count:]
         share_ref, refs = refs[: len(sums)], refs[len(sums) :]
         out_ref, *refs = refs
         tile_refs, refs = refs[:3], refs[3:]
-        qk_ref, product_ref, *refs = refs
+        qk_ref, product_ref, stat_out, *refs = refs
         swap_out, refs = refs[:count], refs[count:]
         total_ref, refs = refs[: len(sums)], refs[len(sums) :]
         swap_send, swap_recv, *refs = refs
+        stat_own, stat_row, stat_head, stat_blk, *refs = refs
+        head_send, head_recv, blk_send, blk_recv, *refs = refs
         chain = None
         if sums:
             chain, refs = ZReturn(refs[0], share_ref[0], total_ref[0], refs[1:5]), refs[5:]
@@ -1270,6 +1275,27 @@
         core, z = back.core, back.z
         others = [lax.rem(head + k, nh) for k in range(1, nh)]
         devices = [{"blk": blk, "head": other} for other in others]
+        column = [{"blk": lax.rem(blk + k, nb), "head": head} for k in range(1, nb)]
+
+        def head_copy(k):
+            return pltpu.make_async_remote_copy(
+                src_ref=stat_own,
+                dst_ref=stat_head.at[nh - 2 - k],
+                send_sem=head_send.at[k],
+                recv_sem=head_recv.at[nh - 2 - k],
+                device_id=devices[k],
+                device_id_type=pl.DeviceIdType.MESH,
+            )
+
+        def blk_copy(k):
+            return pltpu.make_async_remote_copy(
+                src_ref=stat_row,
+                dst_ref=stat_blk.at[nb - 2 - k],
+                send_sem=blk_send.at[k],
+                recv_sem=blk_recv.at[nb - 2 - k],
+                device_id=column[k],
+                device_id_type=pl.DeviceIdType.MESH,
+            )
 
         def sum_copy(k, slot):
             return pltpu.make_async_remote_copy(
@@ -1310,7 +1336,7 @@
                 sum_ref[head, n * lots + lot : n * lots + lot + 1, :] = jnp.sum(
                     total.T, axis=0, keepdims=True
                 )
-        greet([(device, None) for device in devices] + back.peers())
+        greet([(device, None) for device in devices + column])
         for k in range(nh - 1):
             sum_copy(k, head).start()
         swap.start()
@@ -1389,10 +1415,27 @@
             out_ref[:, cols] = total
 
         partial(head, keep_own)
+        stat_own[...] = stat_ref[...]
+        lots_wide = width // 128
+        for c in range(lots_wide):
+            stat_own[c : c + 1, :] = product_ref[:, c * 128 : (c + 1) * 128]
+        for n in range(2):
+            for c in range(columns // 128):
+                line = (2 + n) * lots_wide + head * (columns // 128) + c
+                stat_own[pl.ds(line, 1), :] = qk_ref[n : n + 1, c * 128 : (c + 1) * 128]
+        for k in range(nh - 1):
+            head_copy(k).start()
         for turn in range(sent, nz - 1):
             if chain:
                 pl.when(inner)(lambda turn=turn: chain.send(turn))
             pl.when(inner)(lambda turn=turn: back.send(turn))
+        total = stat_own[...]
+        for k in range(nh - 1):
+            head_copy(nh - 2 - k).wait_recv()
+            total = total + stat_head[k]
+        stat_row[...] = total
+        for k in range(nb - 1):
+            blk_copy(k).start()
         for k in range(nh - 1):
             part_copy(nh - 2 - k).wait_recv()
             for r in range(0, tok, 64):
@@ -1404,23 +1447,35 @@
         for k in range(nh - 1):
             sum_copy(k, head).wait_send()
             part_copy(k).wait_send()
+            head_copy(k).wait_send()
+        total = stat_row[...]
+        for k in range(nb - 1):
+            blk_copy(nb - 2 - k).wait_recv()
+            total = total + stat_blk[k]
+        stat_out[...] = total
+        for k in range(nb - 1):
+            blk_copy(k).wait_send()
         swap.wait()
 
     anywhere = pl.BlockSpec(memory_space=pl.ANY)
     inside = pl.BlockSpec(memory_space=pltpu.VMEM)
     out = pl.pallas_call(
         kernel,
-        in_specs=[inside] * 9 + [anywhere] * (count + len(sums)),
-        out_specs=[inside] * 6 + [anywhere] * count + [inside] * len(sums),
+        in_specs=[inside] * 10 + [anywhere] * (count + len(sums)),
+        out_specs=[inside] * 7 + [anywhere] * count + [inside] * len(sums),
         out_shape=[jax.ShapeDtypeStruct((tok, width), F32)]
         + [jax.ShapeDtypeStruct((tile, columns), F32)] * 3
         + [jax.ShapeDtypeStruct((2, columns), F32), jax.ShapeDtypeStruct((1, width), F32)]
+        + [jax.ShapeDtypeStruct(stats.shape, F32)]
         + [jax.ShapeDtypeStruct(v.shape, v.dtype) for v in swaps]
         + [jax.ShapeDtypeStruct((tok, width), BF16)] * len(sums),
         scratch_shapes=[
             pltpu.SemaphoreType.DMA((count,)),
             pltpu.SemaphoreType.DMA((count,)),
         ]
+        + [pltpu.VMEM(stats.shape, F32)] * 2
+        + [pltpu.VMEM((n - 1,) + stats.shape, F32) for n in (nh, nb)]
+        + [pltpu.SemaphoreType.DMA((n - 1,)) for n in (nh, nh, nb, nb)]
         + ([pltpu.VMEM((nz, tok, width), BF16)] + ZReturn.scratch(nz, tok, width)) * len(sums)
         + [
             pltpu.VMEM((rows, 3 * columns), BF16),
@@ -1437,8 +1492,8 @@
             collective_id=collective_id, has_side_effects=True, vmem_limit_bytes=VMEM_BYTES
         ),
         name="project_backward",
-    )(grads, *raws, invs, gains, group, *weights, *swaps, *sums)
-    return out[0], out[1:4], out[4], out[5], out[6 : 6 + count], out[6 + count :]
+    )(grads, *raws, invs, gains, group, *weights, stats, *swaps, *sums)
+    return out[0], out[1:4], out[6], out[7 : 7 + count], out[7 + count :]
 
 
 def local(
@@ -1615,17 +1670,22 @@
     if share > 1:
         grad_qkv = grad_qkv.reshape((items, share) + grad_qkv.shape[1:])
         grad_qkv = grad_qkv.astype(F32).sum(1).astype(BF16)
-    grad_normed, (grad_query, grad_key, grad_value), qk_parts, product, (down_last,), _ = (
-        project_backward(
-            grad_qkv, raws, invs, qk_gains, group, qkv_cols, (others[0][middle_row:],), (),
-            head_count, blk_count, 4,
-        )
-    )
     if own_sum:
         expert_sum = sums[0].astype(F32)
     else:
         expert_sum = give_back(give_back(moe_share.swapaxes(0, 1), y_bits), z_bits)
     result = middle + expert_sum
+    square_parts = jnp.stack(
+        [jnp.sum(result * result), jnp.sum(branch * branch), jnp.sum(expert_sum * expert_sum)]
+    )
+    zero_width = jnp.zeros((width,), F32)
+    stats = jnp.concatenate(
+        [zero_width, ffn_gain_part, zero_width, zero_width, jnp.pad(square_parts, (0, 8 * 128 - 3))]
+    ).reshape(-1, 128)
+    grad_normed, (grad_query, grad_key, grad_value), totals, (down_last,), _ = project_backward(
+        grad_qkv, raws, invs, qk_gains, group, qkv_cols, (others[0][middle_row:],), (), stats,
+        head_count, blk_count, 4,
+    )
     grad_down, grad_gate, grad_up = [
         (mine + other.astype(F32))[None]
         for mine, other in zip(
@@ -1633,9 +1693,7 @@
         )
     ]
     grad_normed = rounded(grad_normed)
-    query_gain_part, key_gain_part = qk_parts[0], qk_parts[1]
     gained_one = grad_normed * attn_gain
-    attn_gain_part = product[0] / attn_gain
     grad_hidden_in = (
         grad_middle
         + inv_one * gained_one
@@ -1652,38 +1710,20 @@
         ).astype(F32)
 
     grad_out = over_blk(out_part, 1)
-    zero_width = jnp.zeros((width,), F32)
-    query_gain_full = lax.dynamic_update_slice_in_dim(
-        zero_width, query_gain_part, head_index * columns, 0
-    )
-    key_gain_full = lax.dynamic_update_slice_in_dim(
-        zero_width, key_gain_part, head_index * columns, 0
-    )
-    square_parts = jnp.stack(
-        [jnp.sum(result * result), jnp.sum(branch * branch), jnp.sum(expert_sum * expert_sum)]
-    )
-    stacked = jnp.concatenate(
-        [attn_gain_part, ffn_gain_part, query_gain_full, key_gain_full, jnp.pad(square_parts, (0, 125))]
-    ).reshape(-1, 128)
-    for axis in ("head", "blk"):
-        stacked = jnp.sum(lax.all_gather(stacked, axis, axis=0, tiled=False), 0)
-    stacked = stacked.reshape(-1)
-    totals = [stacked[4 * width : 4 * width + 3]] + [
-        stacked[n * width : (n + 1) * width] for n in range(4)
-    ]
+    *totals, squares = jnp.split(totals.reshape(-1), [width, 2 * width, 3 * width, 4 * width])
     entry_count = tok * width * devices
-    stream_stats = jnp.sqrt(totals[0] / entry_count + EPSILON)
+    stream_stats = jnp.sqrt(squares[:3] / entry_count + EPSILON)
     return (
         out_rows(result.astype(BF16)),
         out_rows(grad_hidden_in.astype(BF16)),
-        totals[1],
+        totals[0] / attn_gain,
         grad_query,
         grad_key,
         grad_value,
+        totals[2],
         totals[3],
-        totals[4],
         grad_out,
-        totals[2],
+        totals[1],
         grad_gate,
         grad_up,
         grad_down,

time: 1000 us -> 987 us (0.987)
  blocking collectives: 23 us -> 0 us
  Pallas kernels: 732 us -> 743 us
    all_gather x2 -> x0, blocking collectives: 23 us -> none  [local(): stacked = jnp.sum(lax.all_gather(stacked, axis, axis=0, tiled=False), 0)]
    pallas_call x1, Pallas kernels: 86.2 us -> 96.5 us  [project_backward(): pl.pallas_call(kernel, in_specs=[inside] * 10 + [anywhere] * (count + len...]
  transfers between devices with their start and end apart: 5 -> 5, of which waited for: 2 -> 2; matrix products, arithmetic and copies ran while one was open for 11% -> 11% of each run, Pallas kernels for 51% -> 52%
where the time goes in v5:
time: 987 us; the launch traced here: 978 us
  Pallas kernels  743 us (75%)
  waiting for transfers between devices  76 us (8%)
  matrix products  74.2 us (8%)
  other arithmetic  36.7 us (4%)
  local copies, waits for them, and re-layouts  28.6 us (3%)
  between operations  14.6 us (1%)
    pallas_call x1, Pallas kernels, attend_backward(): pl.pallas_call(kernel, in_specs=[pl.BlockSpec(memory_space=pltpu.SMEM)] +...  150 us
    pallas_call x1, Pallas kernels, project_forward(): pl.pallas_call(kernel, in_specs=[inside] * 5 + [anywhere] * count, out_sp...  146 us
    pallas_call x1, Pallas kernels, expert_exchange(): pl.pallas_call(kernel, in_specs=[anywhere, inside, inside] + [anywhere] *...  134 us
    pallas_call x1, Pallas kernels, attend_forward(): pl.pallas_call(kernel, in_specs=[pl.BlockSpec(memory_space=pltpu.SMEM), i...  116 us
    pallas_call x1, Pallas kernels, return_sum(): pl.pallas_call(kernel, in_specs=[pl.BlockSpec(memory_space=pl.ANY)], out_...  100 us
    pallas_call x1, Pallas kernels, project_backward(): pl.pallas_call(kernel, in_specs=[inside] * 10 + [anywhere] * (count + len...  96.5 us
    dot_general x9, matrix products, mm(): return lax.dot_general(left, right, dims, preferred_element_type=F32)  74.1 us
    reduce_scatter x1, waiting for transfers between devices, local(): lax.psum_scatter(mm(attended, out_w).astype(BF16), 'head', scatter_dimens...  50.3 us
  transfers between devices with their start and end apart: 5, of which 2 were waited for; matrix products, arithmetic and copies ran while one was open for 11% of the time, Pallas kernels for 52%

profile of v5, /device:TPU:0, one launch (start us, length us, event | category | flops | bytes accessed | tf_op | source)
XLA Modules:
  0.0 977.9 jit_solution(5230111113184784493)
XLA Ops:
  7.2 0.7 all-gather.3.cloned.1.call-update
  8.0 0.1 fusion.32
  8.1 0.6 select_n.47.bias_ref
  8.7 0.8 dynamic_slice.11
  9.5 0.8 dynamic_slice.12
  10.3 2.4 convert_bitcast_fusion
  12.7 1.2 copy.52
  14.0 1.2 fusion.21
  15.2 0.1 copy.64
  15.2 1.3 copy.54
  16.6 0.6 pad_maximum_fusion.1.gain_ref
  17.2 1.2 multiply_convert_fusion.1.normed_ref
  18.4 145.7 %project_forward.1 = (bf16[8,3,512,128]{3,2,1,0:T(8,128)(2,1)}, f32[1024,512]{1,0:T(8,128)}, f32[1024,512]{1,0:T(8,128)}, f32[16,128]{1,0:T(8,128)}, bf16[1024,2...) custom-call(bf16[256,2048]{1,0:T(8,128)(2,1)} %multiply_convert_fusi, ...), custom_call_target="tpu_custom_call" | custom-call | tf_op jit(solution)/shard_map/project_forward/pallas_call | solution.py:1203
  164.1 0.6 pad_maximum_fusion.table_ref
  164.7 116.0 %attend_forward.1 = (bf16[8,2,256,128]{3,2,1,0:T(8,128)(2,1)}, f32[16,128,256]{2,1,0:T(8,128)}, f32[16,1,256]{2,1,0:T(1,128)}, bf16[4,2,2,256,2048]{4,3,2,1,0:T(...) custom-call(f32[256]{0:T(256)} %select_n.47.bias_ref, ...), custom_call_target="tpu_custom_call" | custom-call | tf_op jit(solution)/shard_map/attend_forward/pallas_call | solution.py:587
  280.7 2.0 copy.55
  282.8 6.3 convolution_convert_fusion
  289.2 0.9 copy-done.19
  290.2 0.1 convolution_convert_fusion.3
  290.4 0.6 broadcast_in_dim.55.gate_ref
  291.0 0.6 copy_select_fusion.slot_ref
  291.6 50.3 %reduce-scatter.3.cloned.1.call-done = bf16[256,2048]{1,0:T(8,128)(2,1)} async-done(((bf16[1024,2048]{1,0:T(8,128)(2,1)}), bf16[256,2048]{1,0:T(8,128)(2,1)}) %reduce-scatter.3.cloned.1.call-update) | async-done | bytes 1048592 | tf_op jit(solution)/shard_map/reduce_scatter | solution.py:1605
  341.9 3.3 multiply_reduce_fusion.1
  345.2 1.2 multiply_convert_fusion.own_ref
  346.5 134.2 %expert_exchange.1 = (bf16[4,2,256,2048]{3,2,1,0:T(8,128)(2,1)}, bf16[4,2,256,2048]{3,2,1,0:T(8,128)(2,1)}, bf16[8,320,2048]{2,1,0:T(8,128)(2,1)}, bf16[8,320,20...) custom-call(bf16[256,2048]{1,0:T(8,128)(2,1)} %multiply_convert_fusi, ...), custom_call_target="tpu_custom_call" | custom-call | tf_op jit(solution)/shard_map/expert_exchange/pallas_call | solution.py:981
  480.7 100.5 %return_sum.1 = bf16[256,2048]{1,0:T(8,128)(2,1)} custom-call(bf16[4,2,256,2048]{3,2,1,0:T(8,128)(2,1)} %get-tuple-element.63.share_ref), custom_call_target="tpu_custom_call" | custom-call | tf_op jit(solution)/shard_map/return_sum/pallas_call | solution.py:1037
  581.2 2.0 fusion.19
  583.3 1.9 fusion.35
  585.2 11.7 %fusion.refs_2_ = bf16[2048,512]{1,0:T(8,128)(2,1)} fusion(bf16[2560,2048]{1,0:T(8,128)(2,1)} %bitcast.126, bf16[2560,2048]{1,0:T(8,128)(2,1)} %bitcast.132), kind=kOutput, calls=%fused_computation.13 | convolution fusion | flops 5368709120 | bytes 15204352 | tf_op jit(solution)/shard_map/dot_general | solution.py:24
  596.9 10.2 %fusion.4 = bf16[512,2048]{1,0:T(8,128)(2,1)} fusion(bf16[2560,2048]{1,0:T(8,128)(2,1)} %bitcast.138, bf16[2560,1024]{1,0:T(8,128)(2,1)} %bitcast.140), kind=kOutput, calls=%fused_computation.17 | convolution fusion | flops 5368709120 | bytes 15204352 | tf_op jit(solution)/shard_map/dot_general | solution.py:24
  607.1 10.6 %fusion.10 = f32[512,2048]{1,0:T(8,128)} fusion(bf16[2560,2048]{1,0:T(8,128)(2,1)} %bitcast.139, bf16[2560,1024]{1,0:T(8,128)(2,1)} %bitcast.141), kind=kOutput, calls=%fused_computation.23 | convolution fusion | flops 5368709120 | bytes 17301504 | tf_op jit(solution)/shard_map/dot_general | solution.py:24
  617.7 7.3 fusion.2.refs_1_
  625.1 8.0 fusion.6
  633.0 7.6 fusion.8
  640.6 6.2 convolution_convert_fusion.2
  646.8 2.1 reshape.164
  648.9 2.4 copy.58
  651.4 4.5 all-to-all-start
  655.9 6.2 convolution_convert_fusion.1
  662.2 3.1 fusion.36
  665.3 25.0 %all-to-all-done = bf16[8,512,128]{2,1,0:T(8,128)(2,1)} async-done(((bf16[8,512,128]{2,1,0:T(8,128)(2,1)}), bf16[8,512,128]{2,1,0:T(8,128)(2,1)}, u32[]{:S(2)}, u32[]{:S(2)}) %all-to-all-start) | async-done | bytes 1048608 | tf_op jit(solution)/shard_map/all_to_all | solution.py:1581
  690.3 150.3 %attend_backward.1 = (bf16[8,2,3,256,128]{4,3,2,1,0:T(8,128)(2,1)}, bf16[256,2048]{1,0:T(8,128)(2,1)}, bf16[2048,512]{1,0:T(8,128)(2,1)}, bf16[2048,512]{1,0:T(8,128)(2,1)}, bf16[256,2048]{1,0:T(8,128)(2,1)}) custom-call(f32[256]{0:T(256)} %select_n.47.bias_ref, bf16[8,3,2,256,128]{4,3,2,1,0:T(8,128)(2,1)} %bitcast.102, ...), custom_call_target="tpu_custom_call" | custom-call | tf_op jit(solution)/shard_map/attend_backward/pallas_call | solution.py:731
  840.6 2.4 multiply_reduce_fusion
  843.0 2.0 select_maximum_fusion
  845.0 0.6 maximum_bitcast_fusion.stat_ref
  845.7 96.5 %project_backward.1 = (f32[256,2048]{1,0:T(8,128)}, f32[256,512]{1,0:T(8,128)}, f32[256,512]{1,0:T(8,128)}, f32[256,512]{1,0:T(8,128)}, f32[2,512]{1,0:T(2,128)}...) custom-call(bf16[8,2,3,256,128]{4,3,2,1,0:T(8,128)(2,1)} %get-tuple-element.78.grad_ref, ...), custom_call_target="tpu_custom_call" | custom-call | tf_op jit(solution)/shard_map/project_backward/pallas_call | solution.py:1462
  942.2 1.9 convert_element_type.116
  944.1 0.3 copy-done.3
  944.4 0.4 fusion.22
  944.8 0.1 copy-done.22
  944.9 0.5 add_sqrt_fusion
  945.4 0.6 bitcast_divide_fusion
  946.0 0.6 slice_bitcast_fusion
  946.6 1.6 subtract_convert_fusion
  948.3 6.1 copy_bitcast_fusion
  954.5 2.7 add_bitcast_fusion
  957.2 0.9 copy-done.7
  958.1 1.3 copy-done.8
  959.4 0.6 copy-done.11
  960.0 6.7 add_bitcast_fusion.1
  966.7 1.9 convert_element_type.120
  968.6 0.8 copy.79
  969.4 0.8 copy.80
  970.2 0.8 copy.81
  (81 shorter events, 0.6 us)
Async XLA Ops:
  7.2 0.8 copy-start
  7.2 275.6 %all-gather.3.cloned.1.call-start = ((), (), s32[]{:S(2)}) async-start(), calls=%async_computation.3 | async-start | bytes 2359296 | tf_op jit(solution)/shard_map/all_gather | solution.py:1563
  7.9 334.0 %reduce-scatter.3.cloned.1.call-start = ((), (), s32[]{:S(2)}) async-start(), calls=%async_computation.4 | async-start | bytes 5242880 | tf_op jit(solution)/shard_map/reduce_scatter | solution.py:1605
  12.7 1.2 copy-start.9
  12.7 2.5 copy-start.14
  14.0 4.4 copy-start.2
  14.0 3.2 copy-start.21
  18.4 145.7 %copy-start.23 = (s32[128,2,8]{0,2,1:T(8,128)S(1)}, s32[128,2,8]{0,2,1:T(8,128)}, u32[]{:S(2)}) copy-start(s32[128,2,8]{0,2,1:T(8,128)} %param.28) | copy-start | bytes 24580
  18.4 145.7 %copy-start.24 = (f32[128,2,8]{0,2,1:T(8,128)S(1)}, f32[128,2,8]{0,2,1:T(8,128)}, u32[]{:S(2)}) copy-start(f32[128,2,8]{0,2,1:T(8,128)} %param.29) | copy-start | bytes 24580
  282.7 6.3 copy-start.15
  289.1 1.0 copy-start.19
  289.1 351.5 %all-gather.5.cloned.1.call-start = ((), (), s32[]{:S(2)}) async-start(), calls=%async_computation.5 | async-start | bytes 5242880 | tf_op jit(solution)/shard_map/all_gather | solution.py:1658
  291.6 53.6 %copy-start.20 = (f32[2048]{0:T(1024)S(1)}, f32[2048]{0:T(1024)}, u32[]{:S(2)}) copy-start(f32[2048]{0:T(1024)} %param.24) | copy-start | bytes 24580
  581.2 2.1 copy-start.4
  581.2 2.1 copy-start.5
  596.9 20.8 %slice-start = ((s8[10485760]{0:T(1024)(128)(4,1)}), s8[4194304]{0:T(1024)(128)(4,1)S(1)}, s32[]{:S(2)}) async-start(s8[10485760]{0:T(1024)(128)(4,1)} %bitcast.127), calls=%async_computation.7 | async-start | bytes 8388608
  596.9 20.8 %slice-start.1 = ((s8[10485760]{0:T(1024)(128)(4,1)}), s8[4194304]{0:T(1024)(128)(4,1)S(1)}, s32[]{:S(2)}) async-start(s8[10485760]{0:T(1024)(128)(4,1)} %bitcast.127), calls=%async_computation.8 | async-start | bytes 8388608
  596.9 20.8 %slice-start.3 = ((s8[10485760]{0:T(1024)(128)(4,1)}), s8[4194304]{0:T(1024)(128)(4,1)S(1)}, s32[]{:S(2)}) async-start(s8[10485760]{0:T(1024)(128)(4,1)} %bitcast.133), calls=%async_computation.10 | async-start | bytes 8388608
  596.9 20.8 %slice-start.4 = ((s8[10485760]{0:T(1024)(128)(4,1)}), s8[4194304]{0:T(1024)(128)(4,1)S(1)}, s32[]{:S(2)}) async-start(s8[10485760]{0:T(1024)(128)(4,1)} %bitcast.133), calls=%async_computation.11 | async-start | bytes 8388608
  607.1 10.6 %slice-start.2 = ((s8[10485760]{0:T(1024)(128)(4,1)}), s8[2097152]{0:T(1024)(128)(4,1)S(1)}, s32[]{:S(2)}) async-start(s8[10485760]{0:T(1024)(128)(4,1)} %bitcast.127), calls=%async_computation.9 | async-start | bytes 4194304
  607.1 10.6 %slice-start.5 = ((s8[10485760]{0:T(1024)(128)(4,1)}), s8[2097152]{0:T(1024)(128)(4,1)S(1)}, s32[]{:S(2)}) async-start(s8[10485760]{0:T(1024)(128)(4,1)} %bitcast.133), calls=%async_computation.12 | async-start | bytes 4194304
  651.4 38.9 %all-to-all-start = ((bf16[8,512,128]{2,1,0:T(8,128)(2,1)}), bf16[8,512,128]{2,1,0:T(8,128)(2,1)}, u32[]{:S(2)}, u32[]{:S(2)}) async-start(bf16[8,512,128]{2,1,0:T(8,128)(2,1)} %bitcast.110), calls=%async_computation.1 | async-start | bytes 2097152 | tf_op jit(solution)/shard_map/all_to_all | solution.py:1581
  655.9 310.8 %reduce-scatter.5.cloned.1.call-start = ((), (), s32[]{:S(2)}) async-start(), calls=%async_computation.6 | async-start | bytes 2359296 | tf_op jit(solution)/shard_map/reduce_scatter | solution.py:1708
  942.1 2.2 copy-start.3
  944.0 0.9 copy-start.22
  944.0 2.6 copy-start.6
  946.6 7.8 copy-start.12
  946.6 7.8 copy-start.13
  948.3 6.2 copy-start.10
  954.4 3.7 copy-start.7
  954.4 5.0 copy-start.8
  954.4 5.6 copy-start.11
  960.0 8.6 copy-start.18
  960.0 11.0 %copy-start.1 = (s32[2,16]{1,0:T(2,128)S(1)}, s32[2,16]{1,0:T(2,128)}, u32[]{:S(2)}) copy-start(s32[2,16]{1,0:T(2,128)} %param.30) | copy-start | bytes 388
  966.7 2.7 copy-start.17
  966.7 3.5 copy-start.16
Sparse Core Ops, SparseCore 0:
  9.6 44.7 all-gather.2
  289.2 52.6 reduce-scatter.2
  585.3 52.5 all-gather.4
  662.3 41.5 reduce-scatter.4

commit v6 on v5

--- a/solution.py
+++ b/solution.py
@@ -311,6 +311,7 @@
         return target if way == 0 else jnp.where(target == at, self.nz, target)
 
     def z_copy(self, way, target, part, at=None):
+        device = self.onward[way] if at is None else self.beside
         at = (self.z + 1, self.z - 1)[way] if at is None else at
         slot = self.slot(way, target, at)
         return pltpu.make_async_remote_copy(
@@ -318,7 +319,7 @@
             dst_ref=self.from_z.at[slot, self.cut(part)],
             send_sem=self.z_send.at[target, part],
             recv_sem=self.z_recv.at[slot, part],
-            device_id=self.onward[way],
+            device_id=device,
             device_id_type=pl.DeviceIdType.MESH,
         )
 
@@ -408,7 +409,7 @@
         self.y_drain()
         for target in self.targets[:-1]:
             for part in range(self.parts):
-                self.z_copy(0, target, part).wait_send()
+                self.z_copy(0, target, part, self.z).wait_send()
 
 
 class ZReturn(Return):

time: 987 us -> 987 us (level)
  no operation moved by 1% of the time
where the time goes in v6:
time: 987 us; the launch traced here: 978 us
  Pallas kernels  743 us (75%)
  waiting for transfers between devices  76 us (8%)
  matrix products  74.2 us (8%)
  other arithmetic  36.7 us (4%)
  local copies, waits for them, and re-layouts  28.6 us (3%)
  between operations  14.6 us (1%)
    pallas_call x1, Pallas kernels, attend_backward(): pl.pallas_call(kernel, in_specs=[pl.BlockSpec(memory_space=pltpu.SMEM)] +...  150 us
    pallas_call x1, Pallas kernels, project_forward(): pl.pallas_call(kernel, in_specs=[inside] * 5 + [anywhere] * count, out_sp...  146 us
    pallas_call x1, Pallas kernels, expert_exchange(): pl.pallas_call(kernel, in_specs=[anywhere, inside, inside] + [anywhere] *...  134 us
    pallas_call x1, Pallas kernels, attend_forward(): pl.pallas_call(kernel, in_specs=[pl.BlockSpec(memory_space=pltpu.SMEM), i...  116 us
    pallas_call x1, Pallas kernels, return_sum(): pl.pallas_call(kernel, in_specs=[pl.BlockSpec(memory_space=pl.ANY)], out_...  100 us
    pallas_call x1, Pallas kernels, project_backward(): pl.pallas_call(kernel, in_specs=[inside] * 10 + [anywhere] * (count + len...  96.5 us
    dot_general x9, matrix products, mm(): return lax.dot_general(left, right, dims, preferred_element_type=F32)  74.1 us
    reduce_scatter x1, waiting for transfers between devices, local(): lax.psum_scatter(mm(attended, out_w).astype(BF16), 'head', scatter_dimens...  50.3 us
  transfers between devices with their start and end apart: 5, of which 2 were waited for; matrix products, arithmetic and copies ran while one was open for 11% of the time, Pallas kernels for 52%

profile of v6, /device:TPU:0, one launch (start us, length us, event | category | flops | bytes accessed | tf_op | source)
XLA Modules:
  0.0 977.9 jit_solution(5230111113184784493)
XLA Ops:
  7.2 0.7 all-gather.3.cloned.1.call-update
  8.0 0.1 fusion.32
  8.1 0.6 select_n.47.bias_ref
  8.7 0.8 dynamic_slice.11
  9.5 0.8 dynamic_slice.12
  10.3 2.4 convert_bitcast_fusion
  12.7 1.2 copy.52
  14.0 1.2 fusion.21
  15.2 0.1 copy.64
  15.2 1.3 copy.54
  16.6 0.6 pad_maximum_fusion.1.gain_ref
  17.2 1.2 multiply_convert_fusion.1.normed_ref
  18.4 145.7 %project_forward.1 = (bf16[8,3,512,128]{3,2,1,0:T(8,128)(2,1)}, f32[1024,512]{1,0:T(8,128)}, f32[1024,512]{1,0:T(8,128)}, f32[16,128]{1,0:T(8,128)}, bf16[1024,2...) custom-call(bf16[256,2048]{1,0:T(8,128)(2,1)} %multiply_convert_fusi, ...), custom_call_target="tpu_custom_call" | custom-call | tf_op jit(solution)/shard_map/project_forward/pallas_call | solution.py:1204
  164.1 0.6 pad_maximum_fusion.table_ref
  164.7 116.0 %attend_forward.1 = (bf16[8,2,256,128]{3,2,1,0:T(8,128)(2,1)}, f32[16,128,256]{2,1,0:T(8,128)}, f32[16,1,256]{2,1,0:T(1,128)}, bf16[4,2,2,256,2048]{4,3,2,1,0:T(...) custom-call(f32[256]{0:T(256)} %select_n.47.bias_ref, ...), custom_call_target="tpu_custom_call" | custom-call | tf_op jit(solution)/shard_map/attend_forward/pallas_call | solution.py:588
  280.7 2.0 copy.55
  282.8 6.3 convolution_convert_fusion
  289.2 0.9 copy-done.19
  290.2 0.1 convolution_convert_fusion.3
  290.4 0.6 broadcast_in_dim.55.gate_ref
  291.0 0.6 copy_select_fusion.slot_ref
  291.6 50.3 %reduce-scatter.3.cloned.1.call-done = bf16[256,2048]{1,0:T(8,128)(2,1)} async-done(((bf16[1024,2048]{1,0:T(8,128)(2,1)}), bf16[256,2048]{1,0:T(8,128)(2,1)}) %reduce-scatter.3.cloned.1.call-update) | async-done | bytes 1048592 | tf_op jit(solution)/shard_map/reduce_scatter | solution.py:1606
  341.9 3.3 multiply_reduce_fusion.1
  345.2 1.2 multiply_convert_fusion.own_ref
  346.5 134.2 %expert_exchange.1 = (bf16[4,2,256,2048]{3,2,1,0:T(8,128)(2,1)}, bf16[4,2,256,2048]{3,2,1,0:T(8,128)(2,1)}, bf16[8,320,2048]{2,1,0:T(8,128)(2,1)}, bf16[8,320,20...) custom-call(bf16[256,2048]{1,0:T(8,128)(2,1)} %multiply_convert_fusi, ...), custom_call_target="tpu_custom_call" | custom-call | tf_op jit(solution)/shard_map/expert_exchange/pallas_call | solution.py:982
  480.7 100.5 %return_sum.1 = bf16[256,2048]{1,0:T(8,128)(2,1)} custom-call(bf16[4,2,256,2048]{3,2,1,0:T(8,128)(2,1)} %get-tuple-element.63.share_ref), custom_call_target="tpu_custom_call" | custom-call | tf_op jit(solution)/shard_map/return_sum/pallas_call | solution.py:1038
  581.2 2.0 fusion.19
  583.3 1.9 fusion.35
  585.2 11.7 %fusion.refs_2_ = bf16[2048,512]{1,0:T(8,128)(2,1)} fusion(bf16[2560,2048]{1,0:T(8,128)(2,1)} %bitcast.126, bf16[2560,2048]{1,0:T(8,128)(2,1)} %bitcast.132), kind=kOutput, calls=%fused_computation.13 | convolution fusion | flops 5368709120 | bytes 15204352 | tf_op jit(solution)/shard_map/dot_general | solution.py:24
  596.9 10.2 %fusion.4 = bf16[512,2048]{1,0:T(8,128)(2,1)} fusion(bf16[2560,2048]{1,0:T(8,128)(2,1)} %bitcast.138, bf16[2560,1024]{1,0:T(8,128)(2,1)} %bitcast.140), kind=kOutput, calls=%fused_computation.17 | convolution fusion | flops 5368709120 | bytes 15204352 | tf_op jit(solution)/shard_map/dot_general | solution.py:24
  607.1 10.6 %fusion.10 = f32[512,2048]{1,0:T(8,128)} fusion(bf16[2560,2048]{1,0:T(8,128)(2,1)} %bitcast.139, bf16[2560,1024]{1,0:T(8,128)(2,1)} %bitcast.141), kind=kOutput, calls=%fused_computation.23 | convolution fusion | flops 5368709120 | bytes 17301504 | tf_op jit(solution)/shard_map/dot_general | solution.py:24
  617.7 7.3 fusion.2.refs_1_
  625.1 8.0 fusion.6
  633.0 7.6 fusion.8
  640.6 6.2 convolution_convert_fusion.2
  646.8 2.1 reshape.164
  648.9 2.4 copy.58
  651.4 4.5 all-to-all-start
  655.9 6.2 convolution_convert_fusion.1
  662.2 3.1 fusion.36
  665.3 25.0 %all-to-all-done = bf16[8,512,128]{2,1,0:T(8,128)(2,1)} async-done(((bf16[8,512,128]{2,1,0:T(8,128)(2,1)}), bf16[8,512,128]{2,1,0:T(8,128)(2,1)}, u32[]{:S(2)}, u32[]{:S(2)}) %all-to-all-start) | async-done | bytes 1048608 | tf_op jit(solution)/shard_map/all_to_all | solution.py:1582
  690.3 150.3 %attend_backward.1 = (bf16[8,2,3,256,128]{4,3,2,1,0:T(8,128)(2,1)}, bf16[256,2048]{1,0:T(8,128)(2,1)}, bf16[2048,512]{1,0:T(8,128)(2,1)}, bf16[2048,512]{1,0:T(8,128)(2,1)}, bf16[256,2048]{1,0:T(8,128)(2,1)}) custom-call(f32[256]{0:T(256)} %select_n.47.bias_ref, bf16[8,3,2,256,128]{4,3,2,1,0:T(8,128)(2,1)} %bitcast.102, ...), custom_call_target="tpu_custom_call" | custom-call | tf_op jit(solution)/shard_map/attend_backward/pallas_call | solution.py:732
  840.6 2.4 multiply_reduce_fusion
  843.0 2.0 select_maximum_fusion
  845.0 0.6 maximum_bitcast_fusion.stat_ref
  845.7 96.5 %project_backward.1 = (f32[256,2048]{1,0:T(8,128)}, f32[256,512]{1,0:T(8,128)}, f32[256,512]{1,0:T(8,128)}, f32[256,512]{1,0:T(8,128)}, f32[2,512]{1,0:T(2,128)}...) custom-call(bf16[8,2,3,256,128]{4,3,2,1,0:T(8,128)(2,1)} %get-tuple-element.78.grad_ref, ...), custom_call_target="tpu_custom_call" | custom-call | tf_op jit(solution)/shard_map/project_backward/pallas_call | solution.py:1463
  942.2 1.9 convert_element_type.116
  944.1 0.3 copy-done.3
  944.4 0.4 fusion.22
  944.8 0.1 copy-done.22
  944.9 0.5 add_sqrt_fusion
  945.4 0.6 bitcast_divide_fusion
  946.0 0.6 slice_bitcast_fusion
  946.6 1.6 subtract_convert_fusion
  948.3 6.1 copy_bitcast_fusion
  954.5 2.7 add_bitcast_fusion
  957.2 0.9 copy-done.7
  958.1 1.3 copy-done.8
  959.4 0.6 copy-done.11
  960.0 6.7 add_bitcast_fusion.1
  966.7 1.9 convert_element_type.120
  968.6 0.8 copy.79
  969.4 0.8 copy.80
  970.2 0.8 copy.81
  (81 shorter events, 0.6 us)
Async XLA Ops:
  7.2 0.8 copy-start
  7.2 275.6 %all-gather.3.cloned.1.call-start = ((), (), s32[]{:S(2)}) async-start(), calls=%async_computation.3 | async-start | bytes 2359296 | tf_op jit(solution)/shard_map/all_gather | solution.py:1564
  7.9 334.0 %reduce-scatter.3.cloned.1.call-start = ((), (), s32[]{:S(2)}) async-start(), calls=%async_computation.4 | async-start | bytes 5242880 | tf_op jit(solution)/shard_map/reduce_scatter | solution.py:1606
  12.7 1.2 copy-start.9
  12.7 2.5 copy-start.14
  14.0 4.4 copy-start.2
  14.0 3.2 copy-start.21
  18.4 145.7 %copy-start.23 = (s32[128,2,8]{0,2,1:T(8,128)S(1)}, s32[128,2,8]{0,2,1:T(8,128)}, u32[]{:S(2)}) copy-start(s32[128,2,8]{0,2,1:T(8,128)} %param.28) | copy-start | bytes 24580
  18.4 145.7 %copy-start.24 = (f32[128,2,8]{0,2,1:T(8,128)S(1)}, f32[128,2,8]{0,2,1:T(8,128)}, u32[]{:S(2)}) copy-start(f32[128,2,8]{0,2,1:T(8,128)} %param.29) | copy-start | bytes 24580
  282.7 6.3 copy-start.15
  289.1 1.0 copy-start.19
  289.1 351.5 %all-gather.5.cloned.1.call-start = ((), (), s32[]{:S(2)}) async-start(), calls=%async_computation.5 | async-start | bytes 5242880 | tf_op jit(solution)/shard_map/all_gather | solution.py:1659
  291.6 53.6 %copy-start.20 = (f32[2048]{0:T(1024)S(1)}, f32[2048]{0:T(1024)}, u32[]{:S(2)}) copy-start(f32[2048]{0:T(1024)} %param.24) | copy-start | bytes 24580
  581.2 2.1 copy-start.4
  581.2 2.1 copy-start.5
  596.9 20.8 %slice-start = ((s8[10485760]{0:T(1024)(128)(4,1)}), s8[4194304]{0:T(1024)(128)(4,1)S(1)}, s32[]{:S(2)}) async-start(s8[10485760]{0:T(1024)(128)(4,1)} %bitcast.127), calls=%async_computation.7 | async-start | bytes 8388608
  596.9 20.8 %slice-start.1 = ((s8[10485760]{0:T(1024)(128)(4,1)}), s8[4194304]{0:T(1024)(128)(4,1)S(1)}, s32[]{:S(2)}) async-start(s8[10485760]{0:T(1024)(128)(4,1)} %bitcast.127), calls=%async_computation.8 | async-start | bytes 8388608
  596.9 20.8 %slice-start.3 = ((s8[10485760]{0:T(1024)(128)(4,1)}), s8[4194304]{0:T(1024)(128)(4,1)S(1)}, s32[]{:S(2)}) async-start(s8[10485760]{0:T(1024)(128)(4,1)} %bitcast.133), calls=%async_computation.10 | async-start | bytes 8388608
  596.9 20.8 %slice-start.4 = ((s8[10485760]{0:T(1024)(128)(4,1)}), s8[4194304]{0:T(1024)(128)(4,1)S(1)}, s32[]{:S(2)}) async-start(s8[10485760]{0:T(1024)(128)(4,1)} %bitcast.133), calls=%async_computation.11 | async-start | bytes 8388608
  607.1 10.6 %slice-start.2 = ((s8[10485760]{0:T(1024)(128)(4,1)}), s8[2097152]{0:T(1024)(128)(4,1)S(1)}, s32[]{:S(2)}) async-start(s8[10485760]{0:T(1024)(128)(4,1)} %bitcast.127), calls=%async_computation.9 | async-start | bytes 4194304
  607.1 10.6 %slice-start.5 = ((s8[10485760]{0:T(1024)(128)(4,1)}), s8[2097152]{0:T(1024)(128)(4,1)S(1)}, s32[]{:S(2)}) async-start(s8[10485760]{0:T(1024)(128)(4,1)} %bitcast.133), calls=%async_computation.12 | async-start | bytes 4194304
  651.4 38.9 %all-to-all-start = ((bf16[8,512,128]{2,1,0:T(8,128)(2,1)}), bf16[8,512,128]{2,1,0:T(8,128)(2,1)}, u32[]{:S(2)}, u32[]{:S(2)}) async-start(bf16[8,512,128]{2,1,0:T(8,128)(2,1)} %bitcast.110), calls=%async_computation.1 | async-start | bytes 2097152 | tf_op jit(solution)/shard_map/all_to_all | solution.py:1582
  655.9 310.8 %reduce-scatter.5.cloned.1.call-start = ((), (), s32[]{:S(2)}) async-start(), calls=%async_computation.6 | async-start | bytes 2359296 | tf_op jit(solution)/shard_map/reduce_scatter | solution.py:1709
  942.1 2.2 copy-start.3
  944.0 0.9 copy-start.22
  944.0 2.6 copy-start.6
  946.6 7.8 copy-start.12
  946.6 7.8 copy-start.13
  948.3 6.2 copy-start.10
  954.4 3.7 copy-start.7
  954.4 5.0 copy-start.8
  954.4 5.6 copy-start.11
  960.0 8.6 copy-start.18
  960.0 11.0 %copy-start.1 = (s32[2,16]{1,0:T(2,128)S(1)}, s32[2,16]{1,0:T(2,128)}, u32[]{:S(2)}) copy-start(s32[2,16]{1,0:T(2,128)} %param.30) | copy-start | bytes 388
  966.7 2.7 copy-start.17
  966.7 3.5 copy-start.16
Sparse Core Ops, SparseCore 0:
  9.6 44.7 all-gather.2
  289.2 52.6 reduce-scatter.2
  585.3 52.5 all-gather.4
  662.3 41.5 reduce-scatter.4
